TPU v7x, 32 devices: a whole 2x2x4 slice. The times are simulated.
32 devices in a mesh: gx: 4 (over y, core), gy: 8 (over z, x).
Axes of the slice: x: 2, y: 2, z: 4, core: 2. Of those that a mesh axis runs over, the one named last changes fastest.
Arguments:
- log_perm: float32 [1, 32, 128, 2048], P(None, None, 'gx', 'gy'), may hold values from -4 to 4
- source: float32 [1, 32, 128, 2048], P(None, None, 'gx', 'gy'), may hold values from -24 to 24
Outputs:
- pressure: float32 [1, 32, 128, 2048], P(None, None, 'gx', 'gy')
- residual: float32 [1, 32, 128, 2048], P(None, None, 'gx', 'gy')
- flux_east: float32 [1, 32, 128, 2048], P(None, None, 'gx', 'gy')
- flux_north: float32 [1, 32, 128, 2048], P(None, None, 'gx', 'gy')
All inputs are finite; a program needn't handle non-finite values.
Results may differ from a plain program's by a relative error of at most 0.0003.
Values sent between devices are 32-bit elements; how exact they have to be, the bound alone decides.
No kernel may reach another device: no remote copies, remote signals or barrier semaphores. Data moves between devices by JAX's collectives and lax.ppermute only.
A program may use at most 128 MiB of HBM per device.

v0:
```python
import functools

import jax
import jax.numpy as jnp
from jax import lax
from jax.experimental import pallas as pl
from jax.experimental.pallas import tpu as pltpu
from jax.sharding import PartitionSpec as P

DEPTH = 4
LANES = 128
SUB = 8
LO = 8
GROUP = 4 * DEPTH
F32 = jnp.float32
VMEM_SPEC = pl.BlockSpec(memory_space=pltpu.VMEM)
ANY_SPEC = pl.BlockSpec(memory_space=pl.ANY)


def in_vmem(*shape):
    return pltpu.VMEM(shape, F32)


def params(limit):
    return pltpu.CompilerParams(vmem_limit_bytes=limit * 1024 * 1024)


def lane_ids():
    return lax.broadcasted_iota(jnp.int32, (SUB, LANES), 1)


def row_ids():
    return lax.broadcasted_iota(jnp.int32, (SUB, LANES), 0)


def turn(value, shift):
    return pltpu.roll(value, shift % LANES, 1)


def reciprocal(value):
    return 1.0 / value


def load_kernel(log_hbm, src_hbm, log_ref, src_ref, head_ref, tail_ref, sems):
    _, layers, rows, cols = log_hbm.shape
    tiles = cols // LANES
    copies = []
    for index, (hbm, ref) in enumerate(((log_hbm, log_ref), (src_hbm, src_ref))):
        for tile in range(tiles):
            copies.append(
                pltpu.make_async_copy(
                    hbm.at[0, :, :, pl.ds(tile * LANES, LANES)],
                    ref.at[:, tile, pl.ds(LO, rows), :],
                    sems.at[index, tile],
                )
            )
            copies[-1].start()
    for copy in copies:
        copy.wait()
    for index, ref in enumerate((log_ref, src_ref)):
        for tile in range(tiles):
            place = pl.ds(tile * DEPTH, DEPTH)
            head_ref[index, :, place, :] = ref[:, tile, LO : LO + DEPTH, :]
            tail_ref[index, :, place, :] = ref[:, tile, LO + rows - DEPTH : LO + rows, :]


def halo_block(past_ref, before_ref, index, layer, tile):
    place = pl.ds(tile * DEPTH, DEPTH)
    return jnp.concatenate([past_ref[index, layer, place, :], before_ref[index, layer, place, :]], axis=0)


def edge_kernel(log_ref, src_ref, past_ref, before_ref, last_ref, first_ref):
    layers, tiles, height, _ = log_ref.shape
    rows = height - 3 * SUB
    lanes = lane_ids()
    for index, ref in enumerate((log_ref, src_ref)):
        for block in range(rows // SUB + 1):
            for out_ref, tile, lane in ((last_ref, tiles - 1, LANES - DEPTH), (first_ref, 0, 0)):
                total = jnp.zeros((SUB, LANES), F32)
                for layer in range(layers):
                    if block < rows // SUB:
                        value = ref[layer, tile, LO + block * SUB : LO + (block + 1) * SUB, :]
                    else:
                        value = halo_block(past_ref, before_ref, index, layer, tile)
                    moved = turn(value, layer * DEPTH - lane)
                    total = jnp.where(lanes // DEPTH == layer, moved, total)
                out_ref[index, block * SUB : (block + 1) * SUB, :] = total


def basis_kernel(
    log_ref,
    src_ref,
    past_ref,
    before_ref,
    last_ref,
    first_ref,
    right_ref,
    left_ref,
    base_ref,
    one_ref,
    two_ref,
    three_ref,
    four_ref,
    face_x_ref,
    face_y_ref,
    rims_ref,
    sums_ref,
    inverse_ref,
    face_w_ref,
    face_z_ref,
    diag_ref,
    strip_ref,
    strip_inv_ref,
    strip_x_ref,
    strip_y_ref,
    strip_w_ref,
    strip_z_ref,
    strip_d_ref,
    rim_ref,
):
    layers, tiles, height, _ = log_ref.shape
    rows = height - 3 * SUB
    slots = layers // (LANES // GROUP)
    blocks = rows // SUB
    ring = LO + rows + SUB
    lanes = lane_ids()
    place = lanes % GROUP
    subs = row_ids()
    here_x, here_y = lax.axis_index("gx"), lax.axis_index("gy")
    past_x, before_x = here_x < lax.axis_size("gx") - 1, here_x > 0
    past_y, before_y = here_y < lax.axis_size("gy") - 1, here_y > 0
    inside_rows = jnp.where(subs < DEPTH, past_x.astype(jnp.int32), before_x.astype(jnp.int32)) > 0
    inside_cols = (
        jnp.where(
            (place >= DEPTH) & (place < 2 * DEPTH),
            past_y.astype(jnp.int32),
            jnp.where((place >= 2 * DEPTH) & (place < 3 * DEPTH), before_y.astype(jnp.int32), 1),
        )
        > 0
    )
    inside_both = inside_rows & inside_cols
    first_lane, last_lane = lanes == 0, lanes == LANES - 1

    def at(block):
        return pl.ds(LO + block * SUB, SUB)

    def shifted(block, step):
        return pl.ds(LO + block * SUB + step, SUB)

    def close_ring(ref, index, block, value):
        if block == 0:
            ref[(*index, pl.ds(ring, 1), slice(None))] = value[0:1]
        if block == blocks:
            ref[(*index, pl.ds(LO - 1, 1), slice(None))] = value[SUB - 1 : SUB]

    def spread(index, block):
        part = pl.ds(block * SUB, SUB)
        packed = [ref[index, part, :] for ref in (last_ref, right_ref, left_ref, first_ref)]
        found = []
        for slot in range(slots):
            moved = [turn(value, (kind - slot) * DEPTH) for kind, value in enumerate(packed)]
            found.append(
                jnp.where(
                    place < 2 * DEPTH,
                    jnp.where(place < DEPTH, moved[0], moved[1]),
                    jnp.where(place < 3 * DEPTH, moved[2], moved[3]),
                )
            )
        return found

    def put_strip(ref, block, values):
        ref[0, at(block), :] = turn(values[-1], GROUP)
        ref[slots + 1, at(block), :] = turn(values[0], -GROUP)
        for slot, value in enumerate(values):
            ref[slot + 1, at(block), :] = value
            close_ring(ref, (slot + 1,), block, value)

    def put_rim(number, block, values):
        for slot, value in enumerate(values):
            other = turn(value, 2 - 2 * DEPTH)
            rim = jnp.where(place == DEPTH, value, other)
            if number is None:
                rim_ref[slot, at(block), :] = rim
            else:
                rims_ref[number, slot, at(block), :] = rim

    def rim_of(ref, index, group, slot, block):
        found = ref[(*index, slot, at(block), slice(None))]
        return pltpu.roll(found, LANES - 1 - DEPTH - group * GROUP, 1)

    def east(values, rim):
        moved = [turn(value, -1) for value in values] + [rim]
        return [jnp.where(last_lane, moved[tile + 1], moved[tile]) for tile in range(tiles)]

    def west(values, rim):
        moved = [rim] + [turn(value, 1) for value in values]
        return [jnp.where(first_lane, moved[tile], moved[tile + 1]) for tile in range(tiles)]

    for block in range(blocks + 1):
        values = spread(1, block)
        put_strip(strip_ref.at[0], block, values)
        put_rim(0, block, values)
        values = [0.5 * jnp.exp(-value) for value in spread(0, block)]
        put_strip(strip_inv_ref, block, values)
        put_rim(None, block, values)
    top, bottom = lanes >= LANES - GROUP, lanes < GROUP
    for block in range(blocks + 1):
        for slot in range(1, slots + 1):
            value = strip_inv_ref[slot, at(block), :]
            face = reciprocal(value + strip_inv_ref[slot, shifted(block, 1), :])
            strip_x_ref[slot - 1, at(block), :] = face
            close_ring(strip_x_ref, (slot - 1,), block, face)
            face = reciprocal(value + turn(value, -1))
            strip_y_ref[slot - 1, at(block), :] = face
            strip_w_ref[slot - 1, at(block), :] = turn(face, 1)
        for slot in range(slots + 1):
            face = reciprocal(strip_inv_ref[slot, at(block), :] + strip_inv_ref[slot + 1, at(block), :])
            if slot == 0:
                face = jnp.where(bottom, 0.0, face)
            if slot == slots:
                face = jnp.where(top, 0.0, face)
            strip_z_ref[slot, at(block), :] = face
    for block in range(blocks + 1):
        for slot in range(slots):
            strip_d_ref[slot, at(block), :] = (
                (strip_x_ref[slot, at(block), :] + strip_x_ref[slot, shifted(block, -1), :])
                + (strip_y_ref[slot, at(block), :] + strip_w_ref[slot, at(block), :])
                + (strip_z_ref[slot, at(block), :] + strip_z_ref[slot + 1, at(block), :])
            )

    for power in range(1, DEPTH):
        old, new = strip_ref.at[power - 1], strip_ref.at[power]
        for block in range(blocks + 1):
            values = []
            for slot in range(slots):
                value = old[slot + 1, at(block), :]
                result = (
                    strip_d_ref[slot, at(block), :] * value
                    - (
                        strip_x_ref[slot, at(block), :] * old[slot + 1, shifted(block, 1), :]
                        + strip_x_ref[slot, shifted(block, -1), :] * old[slot + 1, shifted(block, -1), :]
                    )
                    - (
                        strip_y_ref[slot, at(block), :] * turn(value, -1)
                        + strip_w_ref[slot, at(block), :] * turn(value, 1)
                    )
                    - (
                        strip_z_ref[slot + 1, at(block), :] * old[slot + 2, at(block), :]
                        + strip_z_ref[slot, at(block), :] * old[slot, at(block), :]
                    )
                )
                values.append(jnp.where(inside_both if block == blocks else inside_cols, result, 0.0))
            put_strip(new, block, values)
            put_rim(power, block, values)

    def fill(layer, _):
        for tile in range(tiles):
            for block in range(blocks + 1):
                if block == blocks:
                    value = halo_block(past_ref, before_ref, 0, layer, tile)
                    source = halo_block(past_ref, before_ref, 1, layer, tile)
                    base_ref[layer, tile, at(block), :] = source
                    close_ring(base_ref, (layer, tile), block, source)
                else:
                    value = log_ref[layer, tile, at(block), :]
                if block == 0:
                    close_ring(base_ref, (layer, tile), 0, base_ref[layer, tile, at(0), :])
                value = 0.5 * jnp.exp(-value)
                inverse_ref[layer, tile, at(block), :] = value
                close_ring(inverse_ref, (layer, tile), block, value)
        return 0

    lax.fori_loop(0, layers, fill, 0)

    zero = jnp.zeros((SUB, LANES), F32)
    for tile in range(tiles):
        for block in range(blocks + 1):
            face_z_ref[0, tile, at(block), :] = zero
            face_z_ref[layers, tile, at(block), :] = zero

    def faces(group, _):
        for slot in range(slots):
            layer = group * slots + slot
            for block in range(blocks + 1):
                values = [inverse_ref[layer, tile, at(block), :] for tile in range(tiles)]
                rim = rim_of(rim_ref, (), group, slot, block)
                nexts = east(values, rim)
                ys = [reciprocal(value + other) for value, other in zip(values, nexts, strict=True)]
                before = reciprocal(values[0] + rim)
                ws = west(ys, before)
                for tile in range(tiles):
                    face = reciprocal(values[tile] + inverse_ref[layer, tile, shifted(block, 1), :])
                    face_x_ref[layer, tile, at(block), :] = face
                    close_ring(face_x_ref, (layer, tile), block, face)
                    face_y_ref[layer, tile, at(block), :] = ys[tile]
                    face_w_ref[layer, tile, at(block), :] = ws[tile]

        return 0

    lax.fori_loop(0, layers // slots, faces, 0)

    def faces_z(layer, _):
        for tile in range(tiles):
            for block in range(blocks + 1):
                face_z_ref[layer, tile, at(block), :] = reciprocal(
                    inverse_ref[layer - 1, tile, at(block), :] + inverse_ref[layer, tile, at(block), :]
                )
        return 0

    lax.fori_loop(1, layers, faces_z, 0)

    def diagonal(layer, _):
        for tile in range(tiles):
            for block in range(blocks + 1):
                diag_ref[layer, tile, at(block), :] = (
                    (face_x_ref[layer, tile, at(block), :] + face_x_ref[layer, tile, shifted(block, -1), :])
                    + (face_y_ref[layer, tile, at(block), :] + face_w_ref[layer, tile, at(block), :])
                    + (face_z_ref[layer, tile, at(block), :] + face_z_ref[layer + 1, tile, at(block), :])
                )
        return 0

    lax.fori_loop(0, layers, diagonal, 0)

    def power_step(number, old, new):
        last_power = number == DEPTH

        def chunk(group, sums):
            own_sums, next_sums = list(sums[0]), list(sums[1])
            for block in range(blocks if last_power else blocks + 1):
                levels = []
                for slot in range(-1, slots + 1):
                    layer = group * slots + slot
                    if slot < 0:
                        layer = jnp.maximum(layer, 0)
                    if slot == slots:
                        layer = jnp.minimum(layer, layers - 1)
                    levels.append([old[layer, tile, at(block), :] for tile in range(tiles)])
                for slot in range(slots):
                    layer = group * slots + slot
                    values = levels[slot + 1]
                    rim = rim_of(rims_ref, (number - 1,), group, slot, block)
                    easts, wests = east(values, rim), west(values, rim)
                    for tile in range(tiles):
                        value = values[tile]
                        result = (
                            diag_ref[layer, tile, at(block), :] * value
                            - (
                                face_x_ref[layer, tile, at(block), :] * old[layer, tile, shifted(block, 1), :]
                                + face_x_ref[layer, tile, shifted(block, -1), :]
                                * old[layer, tile, shifted(block, -1), :]
                            )
                            - (
                                face_y_ref[layer, tile, at(block), :] * easts[tile]
                                + face_w_ref[layer, tile, at(block), :] * wests[tile]
                            )
                            - (
                                face_z_ref[layer + 1, tile, at(block), :] * levels[slot + 2][tile]
                                + face_z_ref[layer, tile, at(block), :] * levels[slot][tile]
                            )
                        )
                        if block == blocks:
                            result = jnp.where(inside_rows, result, 0.0)
                        else:
                            own_sums[tile] = own_sums[tile] + value * value
                            next_sums[tile] = next_sums[tile] + value * result
                        new[layer, tile, at(block), :] = result
                        if not last_power:
                            close_ring(new, (layer, tile), block, result)
            return tuple(own_sums), tuple(next_sums)

        start = (zero,) * tiles
        own_sums, next_sums = lax.fori_loop(0, layers // slots, chunk, (start, start))
        for which, parts in enumerate((own_sums, next_sums)):
            total = functools.reduce(jnp.add, parts)
            row = 2 * (number - 1) + which
            sums_ref[row : row + 1, :] = jnp.sum(total, axis=0, keepdims=True)

    fields = (base_ref, one_ref, two_ref, three_ref, four_ref)
    for number in range(1, DEPTH + 1):
        power_step(number, fields[number - 1], fields[number])


def two_sum(first, second):
    total = first + second
    part = total - first
    return total, (first - (total - part)) + (second - part)


def quick_sum(first, second):
    total = first + second
    return total, second - (total - first)


def halves(value):
    scaled = 4097.0 * value
    high = scaled - (scaled - value)
    return high, value - high


def two_product(first, second):
    total = first * second
    first_high, first_low = halves(first)
    second_high, second_low = halves(second)
    rest = ((first_high * second_high - total) + first_high * second_low + first_low * second_high) + (
        first_low * second_low
    )
    return total, rest


def pair_add(first, second):
    total, rest = two_sum(first[0], second[0])
    return quick_sum(total, rest + (first[1] + second[1]))


def pair_sub(first, second):
    return pair_add(first, (-second[0], -second[1]))


def pair_mul(first, second):
    total, rest = two_product(first[0], second[0])
    return quick_sum(total, rest + (first[0] * second[1] + first[1] * second[0]))


def pair_div(first, second):
    guess = first[0] / second[0]
    total, rest = two_product(guess, second[0])
    left = ((first[0] - total) - rest) + (first[1] - guess * second[1])
    return quick_sum(guess, left / second[0])


def galerkin(moments):
    count = DEPTH
    matrix = {(i, j): moments[i + j + 1] for i in range(count) for j in range(i + 1)}
    right = [moments[i] for i in range(count)]
    for pivot in range(count):
        for i in range(pivot + 1, count):
            ratio = pair_div(matrix[i, pivot], matrix[pivot, pivot])
            for j in range(pivot + 1, i + 1):
                matrix[i, j] = pair_sub(matrix[i, j], pair_mul(ratio, matrix[j, pivot]))
            right[i] = pair_sub(right[i], pair_mul(ratio, right[pivot]))
    found = [None] * count
    for i in reversed(range(count)):
        value = right[i]
        for j in range(i + 1, count):
            value = pair_sub(value, pair_mul(matrix[j, i], found[j]))
        found[i] = pair_div(value, matrix[i, i])
    return [value[0] for value in found]


def finish_kernel(
    sums_ref,
    base_ref,
    one_ref,
    two_ref,
    three_ref,
    four_ref,
    face_x_ref,
    face_y_ref,
    rims_ref,
    pressure_hbm,
    residual_hbm,
    east_hbm,
    north_hbm,
    pressure_ref,
    residual_ref,
    east_ref,
    north_ref,
    field_ref,
    sems,
):
    layers, tiles, height, _ = base_ref.shape
    rows = height - 3 * SUB
    slots = layers // (LANES // GROUP)
    blocks = rows // SUB
    last_lane = lane_ids() == LANES - 1
    fields = (base_ref, one_ref, two_ref, three_ref, four_ref)

    total, rest = sums_ref[...], jnp.zeros((SUB, LANES), F32)
    step = 1
    while step < LANES:
        total, lost = two_sum(total, turn(total, step))
        rest = rest + turn(rest, step) + lost
        step *= 2
    total, rest = quick_sum(total, rest)
    coefs = galerkin([(total[k : k + 1], rest[k : k + 1]) for k in range(2 * DEPTH)])
    coefs = [jnp.broadcast_to(value, (SUB, LANES)) for value in coefs]

    def at(block, step=0):
        return pl.ds(LO + block * SUB + step, SUB)

    def mix(values):
        return functools.reduce(jnp.add, [coef * value for coef, value in zip(coefs, values, strict=True)])

    outs = (
        (pressure_ref, pressure_hbm),
        (residual_ref, residual_hbm),
        (east_ref, east_hbm),
        (north_ref, north_hbm),
    )

    def copies(group):
        part = pl.ds(group * slots, slots)
        return [
            pltpu.make_async_copy(ref.at[part], hbm.at[0, part], sems.at[index, group])
            for index, (ref, hbm) in enumerate(outs)
        ]

    def chunk(group, _):
        for slot in range(slots):
            layer = group * slots + slot
            for block in range(blocks + 1):
                values = []
                for tile in range(tiles):
                    found = [ref[layer, tile, at(block), :] for ref in fields[: DEPTH + (block < blocks)]]
                    value = mix(found[:DEPTH])
                    values.append(value)
                    field_ref[tile, at(block), :] = value
                    if block < blocks:
                        spot = (layer, pl.ds(block * SUB, SUB), pl.ds(tile * LANES, LANES))
                        pressure_ref[spot] = value
                        residual_ref[spot] = found[0] - mix(found[1:])
                if block < blocks:
                    rim = mix([rims_ref[power, slot, at(block), :] for power in range(DEPTH)])
                    rim = pltpu.roll(rim, LANES - 1 - DEPTH - group * GROUP, 1)
                    moved = [turn(value, -1) for value in values] + [rim]
                    for tile in range(tiles):
                        other = jnp.where(last_lane, moved[tile + 1], moved[tile])
                        spot = (layer, pl.ds(block * SUB, SUB), pl.ds(tile * LANES, LANES))
                        north_ref[spot] = face_y_ref[layer, tile, at(block), :] * (values[tile] - other)
            for block in range(blocks):
                for tile in range(tiles):
                    spot = (layer, pl.ds(block * SUB, SUB), pl.ds(tile * LANES, LANES))
                    east_ref[spot] = face_x_ref[layer, tile, at(block), :] * (
                        field_ref[tile, at(block), :] - field_ref[tile, at(block, 1), :]
                    )
        for copy in copies(group):
            copy.start()
        return 0

    lax.fori_loop(0, layers // slots, chunk, 0)

    def drain(group, _):
        for copy in copies(group):
            copy.wait()
        return 0

    lax.fori_loop(0, layers // slots, drain, 0)


def send(value, axis, step):
    count = lax.axis_size(axis)
    return lax.ppermute(value, axis, [(i, i + step) for i in range(count) if 0 <= i + step < count])


def total_over(value, axis):
    step = 1
    while step < lax.axis_size(axis):
        value = value + lax.ppermute(value, axis, [(i, i ^ step) for i in range(lax.axis_size(axis))])
        step *= 2
    return value


def on_device(log_perm, source):
    _, layers, rows, cols = log_perm.shape
    tiles, slots, blocks = cols // LANES, layers // (LANES // GROUP), rows // SUB
    height = rows + 3 * SUB
    full = (layers, tiles, height, LANES)
    ends = (2, layers, tiles * DEPTH, LANES)
    edges = (2, rows + SUB, LANES)
    log_own, src_own, head, tail = pl.pallas_call(
        load_kernel,
        out_shape=(in_vmem(*full), in_vmem(*full), in_vmem(*ends), in_vmem(*ends)),
        in_specs=[ANY_SPEC] * 2,
        out_specs=[VMEM_SPEC] * 4,
        scratch_shapes=[pltpu.SemaphoreType.DMA((2, tiles))],
        compiler_params=params(16),
        name="load",
    )(log_perm, source)
    past = send(head, "gx", -1)
    before = send(tail, "gx", 1)
    last, first = pl.pallas_call(
        edge_kernel,
        out_shape=(in_vmem(*edges), in_vmem(*edges)),
        in_specs=[VMEM_SPEC] * 4,
        out_specs=[VMEM_SPEC] * 2,
        compiler_params=params(16),
        name="edges",
    )(log_own, src_own, past, before)
    right = send(first, "gy", -1)
    left = send(last, "gy", 1)
    strip = (slots + 2, height, LANES)
    inner = (slots, height, LANES)
    results = pl.pallas_call(
        basis_kernel,
        out_shape=(in_vmem(*full),) * 7 + (in_vmem(DEPTH, *inner), in_vmem(SUB, LANES)),
        in_specs=[VMEM_SPEC] * 8,
        out_specs=[VMEM_SPEC] * 9,
        input_output_aliases={1: 0},
        scratch_shapes=[
            in_vmem(*full),
            in_vmem(*full),
            in_vmem(layers + 1, *full[1:]),
            in_vmem(*full),
            in_vmem(DEPTH, *strip),
            in_vmem(*strip),
            in_vmem(*inner),
            in_vmem(*inner),
            in_vmem(*inner),
            in_vmem(slots + 1, height, LANES),
            in_vmem(*inner),
            in_vmem(*inner),
        ],
        compiler_params=params(24),
        name="basis",
    )(log_own, src_own, past, before, last, first, right, left)
    *fields, sums = results
    sums = total_over(total_over(sums, "gx"), "gy")
    block = (layers, rows, cols)
    return pl.pallas_call(
        finish_kernel,
        out_shape=(jax.ShapeDtypeStruct((1, *block), F32),) * 4,
        in_specs=[VMEM_SPEC] * 9,
        out_specs=[ANY_SPEC] * 4,
        scratch_shapes=[in_vmem(*block)] * 4
        + [in_vmem(tiles, height, LANES), pltpu.SemaphoreType.DMA((4, layers // slots))],
        compiler_params=params(16),
        name="finish",
    )(sums, *fields)


def solution(mesh):
    spec = P(None, None, "gx", "gy")
    return jax.shard_map(on_device, mesh=mesh, in_specs=(spec,) * 2, out_specs=(spec,) * 4, check_vma=False)
```

profile of v0, /device:TPU:0, one launch (start us, length us, event | category | flops | bytes accessed | tf_op | source)
XLA Modules:
  0.0 55.6 jit_solution(15176454838520180983)
XLA Ops:
  0.6 0.0 copy-start
  0.6 1.2 %copy-done = f32[1,32,32,256]{3,2,1,0:T(8,128)S(1)} copy-done((f32[1,32,32,256]{3,2,1,0:T(8,128)S(1)}, f32[1,32,32,256]{3,2,1,0:T(8,128)}, u32[]{:S(2)}) %copy-start) | copy-done | bytes 1048600
  1.9 0.0 copy-start.1
  1.9 1.2 %copy-done.1 = f32[1,32,32,256]{3,2,1,0:T(8,128)S(1)} copy-done((f32[1,32,32,256]{3,2,1,0:T(8,128)S(1)}, f32[1,32,32,256]{3,2,1,0:T(8,128)}, u32[]{:S(2)}) %copy-start.1) | copy-done | bytes 1048600
  3.1 0.3 load.1
  3.4 1.3 %collective-permute-start = (f32[2,32,8,128]{3,2,1,0:T(8,128)S(1)}, f32[2,32,8,128]{3,2,1,0:T(8,128)S(1)}, u32[]{:S(2)}, u32[]{:S(2)}) collective-permute-start(f32[2,32,8,128]{3,2,1,0:T(8,128)S(1)} %get-tuple-element.21), channel_id=1, source_target_pairs={{8,0},{16,8},{24,16},{9,1},{17,9},{25,17},{10,2},{18,10},{26,18},{... | collective-permute-start | bytes 786440 | tf_op jit(solution)/shard_map/ppermute | solution.py:552
  4.7 3.0 %collective-permute-start.1 = (f32[2,32,8,128]{3,2,1,0:T(8,128)S(1)}, f32[2,32,8,128]{3,2,1,0:T(8,128)S(1)}, u32[]{:S(2)}, u32[]{:S(2)}) collective-permute-start(f32[2,32,8,128]{3,2,1,0:T(8,128)S(1)} %get-tuple-element.22), channel_id=1, source_target_pairs={{0,8},{8,16},{16,24},{1,9},{9,17},{17,25},{2,10},{10,18},{18,26},{... | collective-permute-start | bytes 786440 | tf_op jit(solution)/shard_map/ppermute | solution.py:552
  7.7 0.0 collective-permute-done.past_ref
  7.7 1.1 %collective-permute-done.1.before_ref = f32[2,32,8,128]{3,2,1,0:T(8,128)S(1)} collective-permute-done((f32[2,32,8,128]{3,2,1,0:T(8,128)S(1)}, f32[2,32,8,128]{3,2,1,0:T(8,128)S(1)}, u32[]{:S(2)}, u32[]{:S(2)}) %collective-permute-start.1) | collective-permute-done | bytes 262176 | tf_op jit(solution)/shard_map/ppermute | solution.py:552
  8.8 0.7 %edges.1 = (f32[2,40,128]{2,1,0:T(8,128)S(1)}, f32[2,40,128]{2,1,0:T(8,128)S(1)}) custom-call(f32[32,2,56,128]{3,2,1,0:T(8,128)S(1)} %get-tuple-element.19.log_ref, f32[32,2,56,128]{3,2,1,0:T(8,128)S(1)} %get-tuple-element.20.src_ref, f32[2,32,8,128]{3,2,1,0:T(8,128)S(1)} %collective-permute-done.past_ref, ...), custom_call_target="tpu_custom_call" | custom-call | tf_op jit(solution)/shard_map/edges/pallas_call | solution.py:581
  9.6 4.8 %collective-permute-start.3 = (f32[2,40,128]{2,1,0:T(8,128)S(1)}, f32[2,40,128]{2,1,0:T(8,128)S(1)}, u32[]{:S(2)}, u32[]{:S(2)}) collective-permute-start(f32[2,40,128]{2,1,0:T(8,128)S(1)} %get-tuple-element.23.last_ref), channel_id=1, source_target_pairs={{0,1},{1,2},{2,3},{3,4},{4,5},{5,6},{6,7},{8,9},{9,10},{10,11},{11... | collective-permute-start | bytes 122888 | tf_op jit(solution)/shard_map/ppermute | solution.py:552
  14.4 1.3 %collective-permute-start.2 = (f32[2,40,128]{2,1,0:T(8,128)S(1)}, f32[2,40,128]{2,1,0:T(8,128)S(1)}, u32[]{:S(2)}, u32[]{:S(2)}) collective-permute-start(f32[2,40,128]{2,1,0:T(8,128)S(1)} %get-tuple-element.24.first_ref), channel_id=1, source_target_pairs={{1,0},{2,1},{3,2},{4,3},{5,4},{6,5},{7,6},{9,8},{10,9},{11,10},{12... | collective-permute-start | bytes 122888 | tf_op jit(solution)/shard_map/ppermute | solution.py:552
  15.7 0.4 collective-permute-done.3.left_ref
  16.1 4.2 %collective-permute-done.2.right_ref = f32[2,40,128]{2,1,0:T(8,128)S(1)} collective-permute-done((f32[2,40,128]{2,1,0:T(8,128)S(1)}, f32[2,40,128]{2,1,0:T(8,128)S(1)}, u32[]{:S(2)}, u32[]{:S(2)}) %collective-permute-start.2) | collective-permute-done | bytes 40992 | tf_op jit(solution)/shard_map/ppermute | solution.py:552
  20.3 11.3 %basis.1 = (f32[32,2,56,128]{3,2,1,0:T(8,128)S(1)}, f32[32,2,56,128]{3,2,1,0:T(8,128)S(1)}, f32[32,2,56,128]{3,2,1,0:T(8,128)S(1)}, f32[32,2,56,128]{3,2,1,0:T(8...) custom-call(f32[32,2,56,128]{3,2,1,0:T(8,128)S(1)} %get-tuple-elemen, ...), custom_call_target="tpu_custom_call", output_to_operand_aliasing={{0}: (1, {})} | custom-call | tf_op jit(solution)/shard_map/basis/pallas_call | solution.py:593
  31.7 1.9 %collective-permute-start.4 = (f32[8,128]{1,0:T(8,128)S(1)}, f32[8,128]{1,0:T(8,128)S(1)}, u32[]{:S(2)}, u32[]{:S(2)}) collective-permute-start(f32[8,128]{1,0:T(8,128)S(1)} %get-tuple-element.25), channel_id=1, source_target_pairs={{0,8},{8,0},{16,24},{24,16},{1,9},{9,1},{17,25},{25,17},{2,10},{10... | collective-permute-start | bytes 12296 | tf_op jit(solution)/shard_map/ppermute | solution.py:558
  33.6 0.8 %collective-permute-done.4 = f32[8,128]{1,0:T(8,128)S(1)} collective-permute-done((f32[8,128]{1,0:T(8,128)S(1)}, f32[8,128]{1,0:T(8,128)S(1)}, u32[]{:S(2)}, u32[]{:S(2)}) %collective-permute-start.4) | collective-permute-done | bytes 4128 | tf_op jit(solution)/shard_map/ppermute | solution.py:558
  34.4 4.1 %collective-permute-start.5 = (f32[8,128]{1,0:T(8,128)S(1)}, f32[8,128]{1,0:T(8,128)S(1)}, u32[]{:S(2)}, u32[]{:S(2)}) collective-permute-start(f32[8,128]{1,0:T(8,128)S(1)} %add.15), channel_id=1, source_target_pairs={{0,16},{8,24},{16,0},{24,8},{1,17},{9,25},{17,1},{25,9},{2,18},{10... | collective-permute-start | bytes 12296 | tf_op jit(solution)/shard_map/ppermute | solution.py:558
  38.5 1.6 %collective-permute-done.5 = f32[8,128]{1,0:T(8,128)S(1)} collective-permute-done((f32[8,128]{1,0:T(8,128)S(1)}, f32[8,128]{1,0:T(8,128)S(1)}, u32[]{:S(2)}, u32[]{:S(2)}) %collective-permute-start.5) | collective-permute-done | bytes 4128 | tf_op jit(solution)/shard_map/ppermute | solution.py:558
  40.1 2.4 %collective-permute-start.6 = (f32[8,128]{1,0:T(8,128)S(1)}, f32[8,128]{1,0:T(8,128)S(1)}, u32[]{:S(2)}, u32[]{:S(2)}) collective-permute-start(f32[8,128]{1,0:T(8,128)S(1)} %add.16), channel_id=1, source_target_pairs={{0,1},{1,0},{2,3},{3,2},{4,5},{5,4},{6,7},{7,6},{8,9},{9,8},{10,11... | collective-permute-start | bytes 12296 | tf_op jit(solution)/shard_map/ppermute | solution.py:558
  42.6 1.6 %collective-permute-done.6 = f32[8,128]{1,0:T(8,128)S(1)} collective-permute-done((f32[8,128]{1,0:T(8,128)S(1)}, f32[8,128]{1,0:T(8,128)S(1)}, u32[]{:S(2)}, u32[]{:S(2)}) %collective-permute-start.6) | collective-permute-done | bytes 4128 | tf_op jit(solution)/shard_map/ppermute | solution.py:558
  44.2 1.6 %collective-permute-start.7 = (f32[8,128]{1,0:T(8,128)S(1)}, f32[8,128]{1,0:T(8,128)S(1)}, u32[]{:S(2)}, u32[]{:S(2)}) collective-permute-start(f32[8,128]{1,0:T(8,128)S(1)} %add.17), channel_id=1, source_target_pairs={{0,2},{1,3},{2,0},{3,1},{4,6},{5,7},{6,4},{7,5},{8,10},{9,11},{10,... | collective-permute-start | bytes 12296 | tf_op jit(solution)/shard_map/ppermute | solution.py:558
  45.8 2.0 %collective-permute-done.7 = f32[8,128]{1,0:T(8,128)S(1)} collective-permute-done((f32[8,128]{1,0:T(8,128)S(1)}, f32[8,128]{1,0:T(8,128)S(1)}, u32[]{:S(2)}, u32[]{:S(2)}) %collective-permute-start.7) | collective-permute-done | bytes 4128 | tf_op jit(solution)/shard_map/ppermute | solution.py:558
  47.8 2.6 %collective-permute-start.8 = (f32[8,128]{1,0:T(8,128)S(1)}, f32[8,128]{1,0:T(8,128)S(1)}, u32[]{:S(2)}, u32[]{:S(2)}) collective-permute-start(f32[8,128]{1,0:T(8,128)S(1)} %add.18), channel_id=1, source_target_pairs={{0,4},{1,5},{2,6},{3,7},{4,0},{5,1},{6,2},{7,3},{8,12},{9,13},{10,... | collective-permute-start | bytes 12296 | tf_op jit(solution)/shard_map/ppermute | solution.py:558
  50.4 1.9 %collective-permute-done.8 = f32[8,128]{1,0:T(8,128)S(1)} collective-permute-done((f32[8,128]{1,0:T(8,128)S(1)}, f32[8,128]{1,0:T(8,128)S(1)}, u32[]{:S(2)}, u32[]{:S(2)}) %collective-permute-start.8) | collective-permute-done | bytes 4128 | tf_op jit(solution)/shard_map/ppermute | solution.py:558
  52.3 3.3 %finish.1 = (f32[1,32,32,256]{3,2,1,0:T(8,128)}, f32[1,32,32,256]{3,2,1,0:T(8,128)}, f32[1,32,32,256]{3,2,1,0:T(8,128)}, f32[1,32,32,256]{3,2,1,0:T(8,128)}) custom-call(f32[8,128]{1,0:T(8,128)S(1)} %add.19.sums_ref, f32[32,2,56,128]{3,2,1,0:T(8,128)S(1)} %get-tuple-element.26.base_ref, f32[32,2,56,128]{3,2,1,0:T(8,128)S(1)} %get-tuple-element.27.one_ref, ...), custom_call_target="tpu_custom_call" | custom-call | tf_op jit(solution)/shard_map/finish/pallas_call | solution.py:619
  (5 shorter events, 0.0 us)
Async XLA Ops:
  0.6 1.2 %copy-start = (f32[1,32,32,256]{3,2,1,0:T(8,128)S(1)}, f32[1,32,32,256]{3,2,1,0:T(8,128)}, u32[]{:S(2)}) copy-start(f32[1,32,32,256]{3,2,1,0:T(8,128)} %log_hbm.1) | copy-start | bytes 3145732
  1.9 1.2 %copy-start.1 = (f32[1,32,32,256]{3,2,1,0:T(8,128)S(1)}, f32[1,32,32,256]{3,2,1,0:T(8,128)}, u32[]{:S(2)}) copy-start(f32[1,32,32,256]{3,2,1,0:T(8,128)} %src_hbm.1) | copy-start | bytes 3145732
  3.4 4.4 %collective-permute-start = (f32[2,32,8,128]{3,2,1,0:T(8,128)S(1)}, f32[2,32,8,128]{3,2,1,0:T(8,128)S(1)}, u32[]{:S(2)}, u32[]{:S(2)}) collective-permute-start(f32[2,32,8,128]{3,2,1,0:T(8,128)S(1)} %get-tuple-element.21), channel_id=1, source_target_pairs={{8,0},{16,8},{24,16},{9,1},{17,9},{25,17},{10,2},{18,10},{26,18},{... | collective-permute-start | bytes 786440 | tf_op jit(solution)/shard_map/ppermute | solution.py:552
  4.7 4.2 %collective-permute-start.1 = (f32[2,32,8,128]{3,2,1,0:T(8,128)S(1)}, f32[2,32,8,128]{3,2,1,0:T(8,128)S(1)}, u32[]{:S(2)}, u32[]{:S(2)}) collective-permute-start(f32[2,32,8,128]{3,2,1,0:T(8,128)S(1)} %get-tuple-element.22), channel_id=1, source_target_pairs={{0,8},{8,16},{16,24},{1,9},{9,17},{17,25},{2,10},{10,18},{18,26},{... | collective-permute-start | bytes 786440 | tf_op jit(solution)/shard_map/ppermute | solution.py:552
  9.6 6.5 %collective-permute-start.3 = (f32[2,40,128]{2,1,0:T(8,128)S(1)}, f32[2,40,128]{2,1,0:T(8,128)S(1)}, u32[]{:S(2)}, u32[]{:S(2)}) collective-permute-start(f32[2,40,128]{2,1,0:T(8,128)S(1)} %get-tuple-element.23.last_ref), channel_id=1, source_target_pairs={{0,1},{1,2},{2,3},{3,4},{4,5},{5,6},{6,7},{8,9},{9,10},{10,11},{11... | collective-permute-start | bytes 122888 | tf_op jit(solution)/shard_map/ppermute | solution.py:552
  14.4 5.9 %collective-permute-start.2 = (f32[2,40,128]{2,1,0:T(8,128)S(1)}, f32[2,40,128]{2,1,0:T(8,128)S(1)}, u32[]{:S(2)}, u32[]{:S(2)}) collective-permute-start(f32[2,40,128]{2,1,0:T(8,128)S(1)} %get-tuple-element.24.first_ref), channel_id=1, source_target_pairs={{1,0},{2,1},{3,2},{4,3},{5,4},{6,5},{7,6},{9,8},{10,9},{11,10},{12... | collective-permute-start | bytes 122888 | tf_op jit(solution)/shard_map/ppermute | solution.py:552
  31.7 2.8 %collective-permute-start.4 = (f32[8,128]{1,0:T(8,128)S(1)}, f32[8,128]{1,0:T(8,128)S(1)}, u32[]{:S(2)}, u32[]{:S(2)}) collective-permute-start(f32[8,128]{1,0:T(8,128)S(1)} %get-tuple-element.25), channel_id=1, source_target_pairs={{0,8},{8,0},{16,24},{24,16},{1,9},{9,1},{17,25},{25,17},{2,10},{10... | collective-permute-start | bytes 12296 | tf_op jit(solution)/shard_map/ppermute | solution.py:558
  34.4 5.7 %collective-permute-start.5 = (f32[8,128]{1,0:T(8,128)S(1)}, f32[8,128]{1,0:T(8,128)S(1)}, u32[]{:S(2)}, u32[]{:S(2)}) collective-permute-start(f32[8,128]{1,0:T(8,128)S(1)} %add.15), channel_id=1, source_target_pairs={{0,16},{8,24},{16,0},{24,8},{1,17},{9,25},{17,1},{25,9},{2,18},{10... | collective-permute-start | bytes 12296 | tf_op jit(solution)/shard_map/ppermute | solution.py:558
  40.1 4.0 %collective-permute-start.6 = (f32[8,128]{1,0:T(8,128)S(1)}, f32[8,128]{1,0:T(8,128)S(1)}, u32[]{:S(2)}, u32[]{:S(2)}) collective-permute-start(f32[8,128]{1,0:T(8,128)S(1)} %add.16), channel_id=1, source_target_pairs={{0,1},{1,0},{2,3},{3,2},{4,5},{5,4},{6,7},{7,6},{8,9},{9,8},{10,11... | collective-permute-start | bytes 12296 | tf_op jit(solution)/shard_map/ppermute | solution.py:558
  44.2 3.6 %collective-permute-start.7 = (f32[8,128]{1,0:T(8,128)S(1)}, f32[8,128]{1,0:T(8,128)S(1)}, u32[]{:S(2)}, u32[]{:S(2)}) collective-permute-start(f32[8,128]{1,0:T(8,128)S(1)} %add.17), channel_id=1, source_target_pairs={{0,2},{1,3},{2,0},{3,1},{4,6},{5,7},{6,4},{7,5},{8,10},{9,11},{10,... | collective-permute-start | bytes 12296 | tf_op jit(solution)/shard_map/ppermute | solution.py:558
  47.8 4.5 %collective-permute-start.8 = (f32[8,128]{1,0:T(8,128)S(1)}, f32[8,128]{1,0:T(8,128)S(1)}, u32[]{:S(2)}, u32[]{:S(2)}) collective-permute-start(f32[8,128]{1,0:T(8,128)S(1)} %add.18), channel_id=1, source_target_pairs={{0,4},{1,5},{2,6},{3,7},{4,0},{5,1},{6,2},{7,3},{8,12},{9,13},{10,... | collective-permute-start | bytes 12296 | tf_op jit(solution)/shard_map/ppermute | solution.py:558
where the time goes:
time: 55.9 us; the launch traced here: 55.6 us
  starting transfers between devices  23.2 us (42%)
  Pallas kernels  15.6 us (28%)
  waiting for transfers between devices  13.7 us (25%)
  local copies, waits for them, and re-layouts  2.44 us (4%)
  between operations  0.71 us (1%)
    ppermute x5, starting transfers between devices, total_over(): lax.ppermute(value, axis, [(i, i ^ step) for i in range(lax.axis_size(axi...  12.7 us
    pallas_call x1, Pallas kernels, on_device(): pl.pallas_call(basis_kernel, out_shape=(in_vmem(*full),) * 7 + (in_vmem(D...  11.3 us
    ppermute x4, starting transfers between devices, send(): lax.ppermute(value, axis, [(i, i + step) for i in range(count) if 0 <= i...  10.5 us
    ppermute x5, waiting for transfers between devices, total_over(): lax.ppermute(value, axis, [(i, i ^ step) for i in range(lax.axis_size(axi...  7.94 us
    ppermute x4, waiting for transfers between devices, send(): lax.ppermute(value, axis, [(i, i + step) for i in range(count) if 0 <= i...  5.72 us
    pallas_call x1, Pallas kernels, on_device(): pl.pallas_call(finish_kernel, out_shape=(jax.ShapeDtypeStruct((1, *block)...  3.32 us
    unnamed x4, local copies, waits for them, and re-layouts  2.44 us
  transfers between devices with their start and end apart: 9, of which 8 were waited for; matrix products, arithmetic and copies ran while one was open for 0% of the time, Pallas kernels for 0%

commit v1 on v0

v1 whole, which is shorter than its diff:
```python
import functools

import jax
import jax.numpy as jnp
from jax import lax
from jax.experimental import pallas as pl
from jax.experimental.pallas import tpu as pltpu
from jax.sharding import PartitionSpec as P

DEPTH = 4
LANES = 128
SUB = 8
LO = 8
GROUP = 4 * DEPTH
F32 = jnp.float32
HBM_SPEC = pl.BlockSpec(memory_space=pltpu.HBM)
VMEM_SPEC = pl.BlockSpec(memory_space=pltpu.VMEM)
ANY_SPEC = pl.BlockSpec(memory_space=pl.ANY)


def in_vmem(*shape):
    return pltpu.VMEM(shape, F32)


def params(limit):
    return pltpu.CompilerParams(vmem_limit_bytes=limit * 1024 * 1024)


def lane_ids():
    return lax.broadcasted_iota(jnp.int32, (SUB, LANES), 1)


def row_ids():
    return lax.broadcasted_iota(jnp.int32, (SUB, LANES), 0)


def turn(value, shift):
    return pltpu.roll(value, shift % LANES, 1)


def reciprocal(value):
    return 1.0 / value


def even(axis):
    return lax.rem(lax.axis_index(axis), 2) == 0


def ends_kernel(log_hbm, src_hbm, near_ref, far_ref, rows_ref, sems):
    _, _, rows, cols = log_hbm.shape
    copies = []
    for index, hbm in enumerate((log_hbm, src_hbm)):
        for end, start in enumerate((0, rows - SUB)):
            for tile in range(cols // LANES):
                copies.append(
                    pltpu.make_async_copy(
                        hbm.at[0, :, pl.ds(start, SUB), pl.ds(tile * LANES, LANES)],
                        rows_ref.at[index, end, tile],
                        sems.at[index, end, tile],
                    )
                )
                copies[-1].start()
    for copy in copies:
        copy.wait()
    first = even("gx")
    for tile in range(cols // LANES):
        head = rows_ref[:, 0, tile, :, 0:DEPTH, :]
        tail = rows_ref[:, 1, tile, :, SUB - DEPTH : SUB, :]
        part = pl.ds(tile * DEPTH, DEPTH)
        near_ref[:, :, part, :] = jnp.where(first, tail, head)
        far_ref[:, :, part, :] = jnp.where(first, head, tail)


def pack(blocks_of, lane):
    lanes = lane_ids()
    total = None
    for layer, value in enumerate(blocks_of):
        moved = turn(value, layer * DEPTH - lane)
        total = moved if total is None else jnp.where(lanes // DEPTH == layer, moved, total)
    return total


def own_kernel(
    log_hbm,
    src_hbm,
    base_ref,
    inverse_ref,
    face_x_ref,
    face_y_ref,
    face_z_ref,
    last_ref,
    first_ref,
    log_ref,
    sems,
):
    _, layers, rows, cols = log_hbm.shape
    tiles, blocks = cols // LANES, rows // SUB
    slots = layers // (LANES // GROUP)
    ring = LO + rows + SUB
    last_lane = lane_ids() == LANES - 1
    copies = []
    for index, (hbm, ref) in enumerate(((log_hbm, log_ref), (src_hbm, base_ref))):
        for tile in range(tiles):
            copies.append(
                pltpu.make_async_copy(
                    hbm.at[0, :, :, pl.ds(tile * LANES, LANES)],
                    ref.at[:, tile, pl.ds(LO, rows), :],
                    sems.at[index, tile],
                )
            )
            copies[-1].start()
    for copy in copies[:tiles]:
        copy.wait()

    def at(block, step=0):
        return pl.ds(LO + block * SUB + step, SUB)

    def fill(layer, _):
        for tile in range(tiles):
            for block in range(blocks):
                value = 0.5 * jnp.exp(-log_ref[layer, tile, at(block), :])
                inverse_ref[layer, tile, at(block), :] = value
                if block == 0:
                    inverse_ref[layer, tile, pl.ds(ring, 1), :] = value[0:1]
        return 0

    lax.fori_loop(0, layers, fill, 0, unroll=slots)

    zero = jnp.zeros((SUB, LANES), F32)
    for tile in range(tiles):
        for block in range(blocks + 1):
            face_z_ref[0, tile, at(block), :] = zero
            face_z_ref[layers, tile, at(block), :] = zero

    def faces(layer, _):
        for block in range(blocks):
            values = [inverse_ref[layer, tile, at(block), :] for tile in range(tiles)]
            moved = [turn(value, -1) for value in values]
            for tile in range(tiles):
                other = moved[tile]
                if tile < tiles - 1:
                    other = jnp.where(last_lane, moved[tile + 1], other)
                face_y_ref[layer, tile, at(block), :] = reciprocal(values[tile] + other)
                face_x_ref[layer, tile, at(block), :] = reciprocal(
                    values[tile] + inverse_ref[layer, tile, at(block, 1), :]
                )
        return 0

    lax.fori_loop(0, layers, faces, 0, unroll=slots)

    def faces_z(layer, _):
        for tile in range(tiles):
            for block in range(blocks):
                face_z_ref[layer, tile, at(block), :] = reciprocal(
                    inverse_ref[layer - 1, tile, at(block), :] + inverse_ref[layer, tile, at(block), :]
                )
        return 0

    lax.fori_loop(1, layers, faces_z, 0, unroll=slots)

    for copy in copies[tiles:]:
        copy.wait()

    base_ref[:, :, pl.ds(ring, 1), :] = base_ref[:, :, pl.ds(LO, 1), :]
    for index, ref in enumerate((log_ref, base_ref)):
        for block in range(blocks):
            part = pl.ds(block * SUB, SUB)
            last_ref[index, part, :] = pack(
                [ref[layer, tiles - 1, at(block), :] for layer in range(layers)], LANES - DEPTH
            )
            first_ref[index, part, :] = pack([ref[layer, 0, at(block), :] for layer in range(layers)], 0)


def edge_kernel(near_in, far_in, last_in, first_in, last_ref, first_ref, near_ref, far_ref, halo_ref):
    del last_in, first_in
    _, layers, tiles, _, _ = halo_ref.shape
    height = last_ref.shape[1]
    one, two = even("gx"), even("gy")
    for tile in range(tiles):
        part = pl.ds(tile * DEPTH, DEPTH)
        near, far = near_in[:, :, part, :], far_in[:, :, part, :]
        halo_ref[:, :, tile, 0:DEPTH, :] = jnp.where(one, near, far)
        halo_ref[:, :, tile, DEPTH:SUB, :] = jnp.where(one, far, near)
    for index in range(2):
        part = pl.ds(height - SUB, SUB)
        last_ref[index, part, :] = pack(
            [halo_ref[index, layer, tiles - 1] for layer in range(layers)], LANES - DEPTH
        )
        first_ref[index, part, :] = pack([halo_ref[index, layer, 0] for layer in range(layers)], 0)
    near_ref[...] = jnp.where(two, last_ref[...], first_ref[...])
    far_ref[...] = jnp.where(two, first_ref[...], last_ref[...])


def basis_kernel(
    halo_ref,
    last_ref,
    first_ref,
    near_ref,
    far_ref,
    base_in,
    inverse_in,
    face_x_in,
    face_y_in,
    face_z_in,
    base_ref,
    inverse_ref,
    face_x_ref,
    face_y_ref,
    face_z_ref,
    one_ref,
    two_ref,
    three_ref,
    four_ref,
    rims_ref,
    sums_ref,
    strip_ref,
    strip_inv_ref,
    strip_x_ref,
    strip_y_ref,
    strip_z_ref,
    rim_ref,
):
    del base_in, inverse_in, face_x_in, face_y_in, face_z_in
    layers, tiles, height, _ = base_ref.shape
    rows = height - 3 * SUB
    slots = layers // (LANES // GROUP)
    groups = layers // slots
    blocks = rows // SUB
    ring = LO + rows + SUB
    lanes = lane_ids()
    place = lanes % GROUP
    subs = row_ids()
    here_x, here_y = lax.axis_index("gx"), lax.axis_index("gy")
    past_x, before_x = here_x < lax.axis_size("gx") - 1, here_x > 0
    past_y, before_y = here_y < lax.axis_size("gy") - 1, here_y > 0
    inside_rows = jnp.where(subs < DEPTH, past_x.astype(jnp.int32), before_x.astype(jnp.int32)) > 0
    inside_cols = (
        jnp.where(
            (place >= DEPTH) & (place < 2 * DEPTH),
            past_y.astype(jnp.int32),
            jnp.where((place >= 2 * DEPTH) & (place < 3 * DEPTH), before_y.astype(jnp.int32), 1),
        )
        > 0
    )
    inside_both = inside_rows & inside_cols
    first_lane, last_lane = lanes == 0, lanes == LANES - 1
    first_y = even("gy")

    def at(block, step=0):
        return pl.ds(LO + block * SUB + step, SUB)

    def close_ring(ref, index, block, value):
        if block == 0:
            ref[(*index, pl.ds(ring, 1), slice(None))] = value[0:1]
        if block == blocks:
            ref[(*index, pl.ds(LO - 1, 1), slice(None))] = value[SUB - 1 : SUB]

    def spread(index, block):
        part = pl.ds(block * SUB, SUB)
        near, far = near_ref[index, part, :], far_ref[index, part, :]
        packed = (
            last_ref[index, part, :],
            jnp.where(first_y, near, far),
            jnp.where(first_y, far, near),
            first_ref[index, part, :],
        )
        found = []
        for slot in range(slots):
            moved = [turn(value, (kind - slot) * DEPTH) for kind, value in enumerate(packed)]
            found.append(
                jnp.where(
                    place < 2 * DEPTH,
                    jnp.where(place < DEPTH, moved[0], moved[1]),
                    jnp.where(place < 3 * DEPTH, moved[2], moved[3]),
                )
            )
        return found

    def put_strip(ref, block, values):
        ref[0, at(block), :] = turn(values[-1], GROUP)
        ref[slots + 1, at(block), :] = turn(values[0], -GROUP)
        for slot, value in enumerate(values):
            ref[slot + 1, at(block), :] = value
            close_ring(ref, (slot + 1,), block, value)

    def rim_of(values, group):
        return pltpu.roll(values, LANES - 1 - DEPTH - group * GROUP, 1)

    def x_part(face_ref, index, old, old_index, block, value):
        there = old[(*old_index, at(block, 1), slice(None))]
        back = old[(*old_index, at(block, -1), slice(None))]
        return face_ref[(*index, at(block), slice(None))] * (value - there) - face_ref[
            (*index, at(block, -1), slice(None))
        ] * (back - value)

    for block in range(blocks + 1):
        put_strip(strip_ref.at[0], block, spread(1, block))
        values = [0.5 * jnp.exp(-value) for value in spread(0, block)]
        put_strip(strip_inv_ref, block, values)
        for slot, value in enumerate(values):
            rim_ref[slot, at(block), :] = value
    top, bottom = lanes >= LANES - GROUP, lanes < GROUP
    for block in range(blocks + 1):
        for slot in range(1, slots + 1):
            value = strip_inv_ref[slot, at(block), :]
            face = reciprocal(value + strip_inv_ref[slot, at(block, 1), :])
            strip_x_ref[slot - 1, at(block), :] = face
            close_ring(strip_x_ref, (slot - 1,), block, face)
            strip_y_ref[slot - 1, at(block), :] = reciprocal(value + turn(value, -1))
        for slot in range(slots + 1):
            face = reciprocal(strip_inv_ref[slot, at(block), :] + strip_inv_ref[slot + 1, at(block), :])
            if slot == 0:
                face = jnp.where(bottom, 0.0, face)
            if slot == slots:
                face = jnp.where(top, 0.0, face)
            strip_z_ref[slot, at(block), :] = face

    for power in range(1, DEPTH + 1):
        old = strip_ref.at[power - 1]
        for block in range(blocks + 1):
            levels = [old[slot, at(block), :] for slot in range(slots + 2)]
            ups = [
                strip_z_ref[slot, at(block), :] * (levels[slot] - levels[slot + 1]) for slot in range(slots + 1)
            ]
            values = []
            for slot in range(slots):
                value = levels[slot + 1]
                flux = strip_y_ref[slot, at(block), :] * (value - turn(value, -1))
                rims_ref[power - 1, slot, at(block), :] = jnp.where(
                    place == DEPTH, value, turn(flux, 2 - 2 * DEPTH)
                )
                if power < DEPTH:
                    result = (
                        (flux - turn(flux, 1))
                        + x_part(strip_x_ref, (slot,), old, (slot + 1,), block, value)
                        + (ups[slot + 1] - ups[slot])
                    )
                    values.append(jnp.where(inside_both if block == blocks else inside_cols, result, 0.0))
            if power < DEPTH:
                put_strip(strip_ref.at[power], block, values)

    def fill(layer, _):
        for tile in range(tiles):
            source = halo_ref[1, layer, tile]
            base_ref[layer, tile, at(blocks), :] = source
            close_ring(base_ref, (layer, tile), blocks, source)
            inverse_ref[layer, tile, at(blocks), :] = 0.5 * jnp.exp(-halo_ref[0, layer, tile])
        return 0

    lax.fori_loop(0, layers, fill, 0, unroll=slots)

    def faces(group, _):
        for slot in range(slots):
            layer = group * slots + slot
            for block in range(blocks + 1):
                rim = rim_of(rim_ref[slot, at(block), :], group)
                whole = block == blocks
                values = [inverse_ref[layer, tile, at(block), :] for tile in range(tiles)]
                if whole:
                    moved = [turn(value, -1) for value in values] + [rim]
                    for tile in range(tiles):
                        other = jnp.where(last_lane, moved[tile + 1], moved[tile])
                        face_y_ref[layer, tile, at(block), :] = reciprocal(values[tile] + other)
                else:
                    face_y_ref[layer, tiles - 1, at(block), :] = jnp.where(
                        last_lane, reciprocal(values[-1] + rim), face_y_ref[layer, tiles - 1, at(block), :]
                    )
                if block >= blocks - 1:
                    for tile in range(tiles):
                        face = reciprocal(values[tile] + inverse_ref[layer, tile, at(block, 1), :])
                        face_x_ref[layer, tile, at(block), :] = face
                        close_ring(face_x_ref, (layer, tile), block, face)
        return 0

    lax.fori_loop(0, groups, faces, 0)

    def faces_z(layer, _):
        for tile in range(tiles):
            face_z_ref[layer, tile, at(blocks), :] = reciprocal(
                inverse_ref[layer - 1, tile, at(blocks), :] + inverse_ref[layer, tile, at(blocks), :]
            )
        return 0

    lax.fori_loop(1, layers, faces_z, 0, unroll=slots)

    zero = jnp.zeros((SUB, LANES), F32)

    def power_step(number, old, new):
        last_power = number == DEPTH

        def chunk(group, sums):
            own_sums, next_sums = list(sums[0]), list(sums[1])
            for block in range(blocks if last_power else blocks + 1):
                levels = []
                for slot in range(-1, slots + 1):
                    layer = group * slots + slot
                    if slot < 0:
                        layer = jnp.maximum(layer, 0)
                    if slot == slots:
                        layer = jnp.minimum(layer, layers - 1)
                    levels.append([old[layer, tile, at(block), :] for tile in range(tiles)])
                ups = [
                    [
                        face_z_ref[group * slots + slot, tile, at(block), :]
                        * (levels[slot][tile] - levels[slot + 1][tile])
                        for tile in range(tiles)
                    ]
                    for slot in range(slots + 1)
                ]
                for slot in range(slots):
                    layer = group * slots + slot
                    values = levels[slot + 1]
                    rim = rim_of(rims_ref[number - 1, slot, at(block), :], group)
                    moved = [turn(value, -1) for value in values] + [rim]
                    flux = [
                        face_y_ref[layer, tile, at(block), :]
                        * (values[tile] - jnp.where(last_lane, moved[tile + 1], moved[tile]))
                        for tile in range(tiles)
                    ]
                    moved = [rim] + [turn(value, 1) for value in flux]
                    for tile in range(tiles):
                        value = values[tile]
                        result = (
                            (flux[tile] - jnp.where(first_lane, moved[tile], moved[tile + 1]))
                            + x_part(face_x_ref, (layer, tile), old, (layer, tile), block, value)
                            + (ups[slot + 1][tile] - ups[slot][tile])
                        )
                        if block == blocks:
                            result = jnp.where(inside_rows, result, 0.0)
                        else:
                            own_sums[tile] = own_sums[tile] + value * value
                            next_sums[tile] = next_sums[tile] + value * result
                        new[layer, tile, at(block), :] = result
                        if not last_power:
                            close_ring(new, (layer, tile), block, result)
            return tuple(own_sums), tuple(next_sums)

        start = (zero,) * tiles
        own_sums, next_sums = lax.fori_loop(0, groups, chunk, (start, start), unroll=1)
        found = []
        for parts in (own_sums, next_sums):
            total = functools.reduce(jnp.add, parts)
            found.append(jnp.sum(total, axis=0, keepdims=True))
        return found

    fields = (base_ref, one_ref, two_ref, three_ref, four_ref)
    found = []
    for number in range(1, DEPTH + 1):
        found += power_step(number, fields[number - 1], fields[number])
    total = jnp.concatenate(found, axis=0)
    for peer in range(sums_ref.shape[0]):
        sums_ref[peer] = total


def two_sum(first, second):
    total = first + second
    part = total - first
    return total, (first - (total - part)) + (second - part)


def quick_sum(first, second):
    total = first + second
    return total, second - (total - first)


def halves(value):
    scaled = 4097.0 * value
    high = scaled - (scaled - value)
    return high, value - high


def two_product(first, second):
    total = first * second
    first_high, first_low = halves(first)
    second_high, second_low = halves(second)
    rest = ((first_high * second_high - total) + first_high * second_low + first_low * second_high) + (
        first_low * second_low
    )
    return total, rest


def pair_add(first, second):
    total, rest = two_sum(first[0], second[0])
    return quick_sum(total, rest + (first[1] + second[1]))


def pair_sub(first, second):
    return pair_add(first, (-second[0], -second[1]))


def pair_mul(first, second):
    total, rest = two_product(first[0], second[0])
    return quick_sum(total, rest + (first[0] * second[1] + first[1] * second[0]))


def pair_div(first, second):
    guess = first[0] / second[0]
    total, rest = two_product(guess, second[0])
    left = ((first[0] - total) - rest) + (first[1] - guess * second[1])
    return quick_sum(guess, left / second[0])


def galerkin(moments):
    count = DEPTH
    matrix = {(i, j): moments[i + j + 1] for i in range(count) for j in range(i + 1)}
    right = [moments[i] for i in range(count)]
    for pivot in range(count):
        for i in range(pivot + 1, count):
            ratio = pair_div(matrix[i, pivot], matrix[pivot, pivot])
            for j in range(pivot + 1, i + 1):
                matrix[i, j] = pair_sub(matrix[i, j], pair_mul(ratio, matrix[j, pivot]))
            right[i] = pair_sub(right[i], pair_mul(ratio, right[pivot]))
    found = [None] * count
    for i in reversed(range(count)):
        value = right[i]
        for j in range(i + 1, count):
            value = pair_sub(value, pair_mul(matrix[j, i], found[j]))
        found[i] = pair_div(value, matrix[i, i])
    return [value[0] for value in found]


def finish_kernel(
    sums_ref,
    base_ref,
    one_ref,
    two_ref,
    three_ref,
    four_ref,
    face_x_ref,
    face_y_ref,
    rims_ref,
    pressure_hbm,
    residual_hbm,
    east_hbm,
    north_hbm,
    pressure_ref,
    residual_ref,
    east_ref,
    north_ref,
    field_ref,
    sems,
):
    layers, tiles, height, _ = base_ref.shape
    rows = height - 3 * SUB
    slots = layers // (LANES // GROUP)
    blocks = rows // SUB
    last_lane = lane_ids() == LANES - 1
    fields = (base_ref, one_ref, two_ref, three_ref, four_ref)

    total = functools.reduce(jnp.add, [sums_ref[peer] for peer in range(sums_ref.shape[0])])
    rest = jnp.zeros((SUB, LANES), F32)
    step = 1
    while step < LANES:
        total, lost = two_sum(total, turn(total, step))
        rest = rest + turn(rest, step) + lost
        step *= 2
    total, rest = quick_sum(total, rest)
    coefs = galerkin([(total[k : k + 1], rest[k : k + 1]) for k in range(2 * DEPTH)])
    coefs = [jnp.broadcast_to(value, (SUB, LANES)) for value in coefs]

    def at(block, step=0):
        return pl.ds(LO + block * SUB + step, SUB)

    def mix(values):
        return functools.reduce(jnp.add, [coef * value for coef, value in zip(coefs, values, strict=True)])

    outs = (
        (pressure_ref, pressure_hbm),
        (residual_ref, residual_hbm),
        (east_ref, east_hbm),
        (north_ref, north_hbm),
    )

    def copies(group):
        part = pl.ds(group * slots, slots)
        return [
            pltpu.make_async_copy(ref.at[part], hbm.at[0, part], sems.at[index, group])
            for index, (ref, hbm) in enumerate(outs)
        ]

    def chunk(group, _):
        for slot in range(slots):
            layer = group * slots + slot
            for block in range(blocks + 1):
                values = []
                for tile in range(tiles):
                    found = [ref[layer, tile, at(block), :] for ref in fields[: DEPTH + (block < blocks)]]
                    value = mix(found[:DEPTH])
                    values.append(value)
                    field_ref[tile, at(block), :] = value
                    if block < blocks:
                        spot = (layer, pl.ds(block * SUB, SUB), pl.ds(tile * LANES, LANES))
                        pressure_ref[spot] = value
                        residual_ref[spot] = found[0] - mix(found[1:])
                if block < blocks:
                    rim = mix([rims_ref[power, slot, at(block), :] for power in range(DEPTH)])
                    rim = pltpu.roll(rim, LANES - 1 - DEPTH - group * GROUP, 1)
                    moved = [turn(value, -1) for value in values] + [rim]
                    for tile in range(tiles):
                        other = jnp.where(last_lane, moved[tile + 1], moved[tile])
                        spot = (layer, pl.ds(block * SUB, SUB), pl.ds(tile * LANES, LANES))
                        north_ref[spot] = face_y_ref[layer, tile, at(block), :] * (values[tile] - other)
            for block in range(blocks):
                for tile in range(tiles):
                    spot = (layer, pl.ds(block * SUB, SUB), pl.ds(tile * LANES, LANES))
                    east_ref[spot] = face_x_ref[layer, tile, at(block), :] * (
                        field_ref[tile, at(block), :] - field_ref[tile, at(block, 1), :]
                    )
        for copy in copies(group):
            copy.start()
        return 0

    lax.fori_loop(0, layers // slots, chunk, 0)

    def drain(group, _):
        for copy in copies(group):
            copy.wait()
        return 0

    lax.fori_loop(0, layers // slots, drain, 0)


def exchange(value, axis, near):
    count = lax.axis_size(axis)
    pairs = []
    for i in range(count):
        other = i + 1 if (i % 2 == 0) == near else i - 1
        if 0 <= other < count:
            pairs.append((i, other))
    return lax.ppermute(value, axis, pairs)


def on_device(log_perm, source):
    _, layers, rows, cols = log_perm.shape
    tiles, slots = cols // LANES, layers // (LANES // GROUP)
    height = rows + 3 * SUB
    full = (layers, tiles, height, LANES)
    deep = (layers + 1, tiles, height, LANES)
    ends = (2, layers, tiles * DEPTH, LANES)
    edges = (2, rows + SUB, LANES)
    strip = (slots + 2, height, LANES)
    inner = (slots, height, LANES)
    peers = lax.axis_size("gx") * lax.axis_size("gy")
    cells = layers * rows * cols

    near, far = pl.pallas_call(
        ends_kernel,
        out_shape=(in_vmem(*ends),) * 2,
        in_specs=[HBM_SPEC] * 2,
        out_specs=[VMEM_SPEC] * 2,
        scratch_shapes=[in_vmem(2, 2, tiles, layers, SUB, LANES), pltpu.SemaphoreType.DMA((2, 2, tiles))],
        compiler_params=params(16),
        name="ends",
    )(log_perm, source)
    far = exchange(far, "gx", False)
    near = exchange(near, "gx", True)
    *fields, last, first = pl.pallas_call(
        own_kernel,
        out_shape=(in_vmem(*full),) * 4 + (in_vmem(*deep),) + (in_vmem(*edges),) * 2,
        in_specs=[HBM_SPEC] * 2,
        out_specs=[VMEM_SPEC] * 7,
        scratch_shapes=[in_vmem(*full), pltpu.SemaphoreType.DMA((2, tiles))],
        compiler_params=params(16),
        cost_estimate=pl.CostEstimate(flops=60 * cells, bytes_accessed=8 * cells, transcendentals=4 * cells),
        name="own",
    )(log_perm, source)
    last, first, near, far, halo = pl.pallas_call(
        edge_kernel,
        out_shape=(in_vmem(*edges),) * 4 + (in_vmem(2, layers, tiles, SUB, LANES),),
        in_specs=[VMEM_SPEC] * 4,
        out_specs=[VMEM_SPEC] * 5,
        input_output_aliases={2: 0, 3: 1},
        compiler_params=params(16),
        name="edges",
    )(near, far, last, first)
    far = exchange(far, "gy", False)
    near = exchange(near, "gy", True)
    results = pl.pallas_call(
        basis_kernel,
        out_shape=(in_vmem(*full),) * 4
        + (in_vmem(*deep),)
        + (in_vmem(*full),) * 4
        + (in_vmem(DEPTH, *inner), in_vmem(peers, SUB, LANES)),
        in_specs=[VMEM_SPEC] * 10,
        out_specs=[VMEM_SPEC] * 11,
        input_output_aliases={5: 0, 6: 1, 7: 2, 8: 3, 9: 4},
        scratch_shapes=[
            in_vmem(DEPTH, *strip),
            in_vmem(*strip),
            in_vmem(*inner),
            in_vmem(*inner),
            in_vmem(slots + 1, height, LANES),
            in_vmem(*inner),
        ],
        compiler_params=params(16),
        name="basis",
    )(halo, last, first, near, far, *fields)
    base, _, face_x, face_y, _, *powers, rims, sums = results
    sums = lax.all_to_all(sums, ("gx", "gy"), 0, 0)
    block = (layers, rows, cols)
    return pl.pallas_call(
        finish_kernel,
        out_shape=(jax.ShapeDtypeStruct((1, *block), F32),) * 4,
        in_specs=[VMEM_SPEC] * 9,
        out_specs=[ANY_SPEC] * 4,
        scratch_shapes=[in_vmem(*block)] * 4
        + [in_vmem(tiles, height, LANES), pltpu.SemaphoreType.DMA((4, layers // slots))],
        compiler_params=params(16),
        name="finish",
    )(sums, base, *powers, face_x, face_y, rims)


def solution(mesh):
    spec = P(None, None, "gx", "gy")
    return jax.shard_map(on_device, mesh=mesh, in_specs=(spec,) * 2, out_specs=(spec,) * 4, check_vma=False)
```

time: 55.9 us -> 46.6 us (0.83)
  blocking collectives: 0 us -> 22.1 us
  starting transfers between devices: 23.2 us -> 4.41 us
  waiting for transfers between devices: 13.7 us -> 1.33 us
    all_to_all x0 -> x1, blocking collectives: none -> 22.1 us  [on_device(): sums = lax.all_to_all(sums, ('gx', 'gy'), 0, 0)]
    ppermute x9 -> x4, starting transfers between devices: 23.2 us -> 4.41 us  [exchange(): return lax.ppermute(value, axis, pairs)]
    ppermute x9 -> x4, waiting for transfers between devices: 13.7 us -> 1.33 us  [exchange(): return lax.ppermute(value, axis, pairs)]
    pallas_call x3 -> x4, Pallas kernels: 12.3 us -> 12 us  [the longest x1 9.32 us: on_device(): pl.pallas_call(basis_kernel, out_shape=(in_vmem(*full),) * 4 + (in_vmem(*...]
  transfers between devices with their start and end apart: 9 -> 4, of which waited for: 8 -> 1; matrix products, arithmetic and copies ran while one was open for 0% -> 0% of each run, Pallas kernels for 0% -> 5%
where the time goes in v1:
time: 46.6 us; the launch traced here: 46.4 us
  blocking collectives  22.1 us (47%)
  Pallas kernels  15.4 us (33%)
  starting transfers between devices  4.41 us (9%)
  local copies, waits for them, and re-layouts  2.44 us (5%)
  waiting for transfers between devices  1.33 us (3%)
  between operations  0.7 us (2%)
    all_to_all x1, blocking collectives, on_device(): sums = lax.all_to_all(sums, ('gx', 'gy'), 0, 0)  22.1 us
    pallas_call x1, Pallas kernels, on_device(): pl.pallas_call(basis_kernel, out_shape=(in_vmem(*full),) * 4 + (in_vmem(*...  9.32 us
    ppermute x4, starting transfers between devices, exchange(): return lax.ppermute(value, axis, pairs)  4.41 us
    pallas_call x1, Pallas kernels, on_device(): pl.pallas_call(finish_kernel, out_shape=(jax.ShapeDtypeStruct((1, *block)...  3.39 us
    unnamed x4, local copies, waits for them, and re-layouts  2.44 us
    pallas_call x1, Pallas kernels, on_device(): pl.pallas_call(own_kernel, out_shape=(in_vmem(*full),) * 4 + (in_vmem(*de...  2.11 us
    ppermute x4, waiting for transfers between devices, exchange(): return lax.ppermute(value, axis, pairs)  1.33 us
  transfers between devices with their start and end apart: 4, of which 1 were waited for; matrix products, arithmetic and copies ran while one was open for 0% of the time, Pallas kernels for 5%

profile of v1, /device:TPU:0, one launch (start us, length us, event | category | flops | bytes accessed | tf_op | source)
XLA Modules:
  0.0 46.4 jit_solution(3896460075609447984)
XLA Ops:
  0.6 0.0 copy-start
  0.6 1.2 %copy-done = f32[1,32,32,256]{3,2,1,0:T(8,128)S(1)} copy-done((f32[1,32,32,256]{3,2,1,0:T(8,128)S(1)}, f32[1,32,32,256]{3,2,1,0:T(8,128)}, u32[]{:S(2)}) %copy-start) | copy-done | bytes 1048600
  1.9 0.0 copy-start.1
  1.9 1.2 %copy-done.1 = f32[1,32,32,256]{3,2,1,0:T(8,128)S(1)} copy-done((f32[1,32,32,256]{3,2,1,0:T(8,128)S(1)}, f32[1,32,32,256]{3,2,1,0:T(8,128)}, u32[]{:S(2)}) %copy-start.1) | copy-done | bytes 1048600
  3.1 0.3 ends.1
  3.4 0.5 %collective-permute-start = (f32[2,32,8,128]{3,2,1,0:T(8,128)S(1)}, f32[2,32,8,128]{3,2,1,0:T(8,128)S(1)}, u32[]{:S(2)}, u32[]{:S(2)}) collective-permute-start(f32[2,32,8,128]{3,2,1,0:T(8,128)S(1)} %get-tuple-element.27), channel_id=1, source_target_pairs={{0,8},{8,0},{16,24},{24,16},{1,9},{9,1},{17,25},{25,17},{2,10},{10... | collective-permute-start | bytes 786440 | tf_op jit(solution)/shard_map/ppermute | solution.py:630
  3.9 0.7 %collective-permute-start.1 = (f32[2,32,8,128]{3,2,1,0:T(8,128)S(1)}, f32[2,32,8,128]{3,2,1,0:T(8,128)S(1)}, u32[]{:S(2)}, u32[]{:S(2)}) collective-permute-start(f32[2,32,8,128]{3,2,1,0:T(8,128)S(1)} %get-tuple-element.28), channel_id=1, source_target_pairs={{8,16},{16,8},{9,17},{17,9},{10,18},{18,10},{11,19},{19,11},{12,20... | collective-permute-start | bytes 786440 | tf_op jit(solution)/shard_map/ppermute | solution.py:630
  4.6 2.1 %own.1 = (f32[32,2,56,128]{3,2,1,0:T(8,128)S(1)}, f32[32,2,56,128]{3,2,1,0:T(8,128)S(1)}, f32[32,2,56,128]{3,2,1,0:T(8,128)S(1)}, f32[32,2,56,128]{3,2,1,0:T(8,1...) custom-call(f32[1,32,32,256]{3,2,1,0:T(8,128)S(1)} %copy-done, ...), custom_call_target="tpu_custom_call" | custom-call | flops 15728640 | bytes 2097152 | tf_op jit(solution)/shard_map/own/pallas_call | solution.py:657
  6.7 0.0 collective-permute-done.near_in
  6.7 0.0 collective-permute-done.1.far_in
  6.8 0.2 edges.1
  7.0 2.6 %collective-permute-start.2 = (f32[2,40,128]{2,1,0:T(8,128)S(1)}, f32[2,40,128]{2,1,0:T(8,128)S(1)}, u32[]{:S(2)}, u32[]{:S(2)}) collective-permute-start(f32[2,40,128]{2,1,0:T(8,128)S(1)} %get-tuple-element.34), channel_id=1, source_target_pairs={{0,1},{1,0},{2,3},{3,2},{4,5},{5,4},{6,7},{7,6},{8,9},{9,8},{10,11... | collective-permute-start | bytes 122888 | tf_op jit(solution)/shard_map/ppermute | solution.py:630
  9.6 0.7 %collective-permute-start.3 = (f32[2,40,128]{2,1,0:T(8,128)S(1)}, f32[2,40,128]{2,1,0:T(8,128)S(1)}, u32[]{:S(2)}, u32[]{:S(2)}) collective-permute-start(f32[2,40,128]{2,1,0:T(8,128)S(1)} %get-tuple-element.35), channel_id=1, source_target_pairs={{1,2},{2,1},{3,4},{4,3},{5,6},{6,5},{9,10},{10,9},{11,12},{12,11},... | collective-permute-start | bytes 122888 | tf_op jit(solution)/shard_map/ppermute | solution.py:630
  10.2 1.3 %collective-permute-done.2.near_ref = f32[2,40,128]{2,1,0:T(8,128)S(1)} collective-permute-done((f32[2,40,128]{2,1,0:T(8,128)S(1)}, f32[2,40,128]{2,1,0:T(8,128)S(1)}, u32[]{:S(2)}, u32[]{:S(2)}) %collective-permute-start.2) | collective-permute-done | bytes 40992 | tf_op jit(solution)/shard_map/ppermute | solution.py:630
  11.6 0.0 collective-permute-done.3.far_ref
  11.6 9.3 %basis.1 = (f32[32,2,56,128]{3,2,1,0:T(8,128)S(1)}, f32[32,2,56,128]{3,2,1,0:T(8,128)S(1)}, f32[32,2,56,128]{3,2,1,0:T(8,128)S(1)}, f32[32,2,56,128]{3,2,1,0:T(8...) custom-call(f32[2,32,2,8,128]{4,3,2,1,0:T(8,128)S(1)} %get-tuple-ele, ...), custom_call_target="tpu_custom_call", output_to_operand_aliasing={{0}: (5, {}), {1}: (6, {}), {2}: (7, {}), {3}: (8, {}), {4}... | custom-call | tf_op jit(solution)/shard_map/basis/pallas_call | solution.py:678
  20.9 22.1 %all_to_all.5.sums_ref = f32[32,8,128]{2,1,0:T(8,128)S(1)} all-to-all(f32[32,8,128]{2,1,0:T(8,128)S(1)} %get-tuple-element.41), channel_id=1, replica_groups=mesh['gx'=4,'gy'=8] {'gx','gy'}, dimensions={0} | all-to-all | bytes 262144 | tf_op jit(solution)/shard_map/all_to_all | solution.py:699
  43.0 3.4 %finish.1 = (f32[1,32,32,256]{3,2,1,0:T(8,128)}, f32[1,32,32,256]{3,2,1,0:T(8,128)}, f32[1,32,32,256]{3,2,1,0:T(8,128)}, f32[1,32,32,256]{3,2,1,0:T(8,128)}) custom-call(f32[32,8,128]{2,1,0:T(8,128)S(1)} %all_to_all.5.sums_ref, f32[32,2,56,128]{3,2,1,0:T(8,128)S(1)} %get-tuple-element.42.base_ref, f32[32,2,56,128]{3,2,1,0:T(8,128)S(1)} %get-tuple-element.43.one_ref, ...), custom_call_target="tpu_custom_call" | custom-call | tf_op jit(solution)/shard_map/finish/pallas_call | solution.py:701
Async XLA Ops:
  0.6 1.2 %copy-start = (f32[1,32,32,256]{3,2,1,0:T(8,128)S(1)}, f32[1,32,32,256]{3,2,1,0:T(8,128)}, u32[]{:S(2)}) copy-start(f32[1,32,32,256]{3,2,1,0:T(8,128)} %log_hbm.3) | copy-start | bytes 3145732
  1.9 1.2 %copy-start.1 = (f32[1,32,32,256]{3,2,1,0:T(8,128)S(1)}, f32[1,32,32,256]{3,2,1,0:T(8,128)}, u32[]{:S(2)}) copy-start(f32[1,32,32,256]{3,2,1,0:T(8,128)} %src_hbm.3) | copy-start | bytes 3145732
  3.4 3.3 %collective-permute-start = (f32[2,32,8,128]{3,2,1,0:T(8,128)S(1)}, f32[2,32,8,128]{3,2,1,0:T(8,128)S(1)}, u32[]{:S(2)}, u32[]{:S(2)}) collective-permute-start(f32[2,32,8,128]{3,2,1,0:T(8,128)S(1)} %get-tuple-element.27), channel_id=1, source_target_pairs={{0,8},{8,0},{16,24},{24,16},{1,9},{9,1},{17,25},{25,17},{2,10},{10... | collective-permute-start | bytes 786440 | tf_op jit(solution)/shard_map/ppermute | solution.py:630
  3.9 2.8 %collective-permute-start.1 = (f32[2,32,8,128]{3,2,1,0:T(8,128)S(1)}, f32[2,32,8,128]{3,2,1,0:T(8,128)S(1)}, u32[]{:S(2)}, u32[]{:S(2)}) collective-permute-start(f32[2,32,8,128]{3,2,1,0:T(8,128)S(1)} %get-tuple-element.28), channel_id=1, source_target_pairs={{8,16},{16,8},{9,17},{17,9},{10,18},{18,10},{11,19},{19,11},{12,20... | collective-permute-start | bytes 786440 | tf_op jit(solution)/shard_map/ppermute | solution.py:630
  7.0 4.6 %collective-permute-start.2 = (f32[2,40,128]{2,1,0:T(8,128)S(1)}, f32[2,40,128]{2,1,0:T(8,128)S(1)}, u32[]{:S(2)}, u32[]{:S(2)}) collective-permute-start(f32[2,40,128]{2,1,0:T(8,128)S(1)} %get-tuple-element.34), channel_id=1, source_target_pairs={{0,1},{1,0},{2,3},{3,2},{4,5},{5,4},{6,7},{7,6},{8,9},{9,8},{10,11... | collective-permute-start | bytes 122888 | tf_op jit(solution)/shard_map/ppermute | solution.py:630
  9.6 2.0 %collective-permute-start.3 = (f32[2,40,128]{2,1,0:T(8,128)S(1)}, f32[2,40,128]{2,1,0:T(8,128)S(1)}, u32[]{:S(2)}, u32[]{:S(2)}) collective-permute-start(f32[2,40,128]{2,1,0:T(8,128)S(1)} %get-tuple-element.35), channel_id=1, source_target_pairs={{1,2},{2,1},{3,4},{4,3},{5,6},{6,5},{9,10},{10,9},{11,12},{12,11},... | collective-permute-start | bytes 122888 | tf_op jit(solution)/shard_map/ppermute | solution.py:630

commit v2 on v1

--- a/solution.py
+++ b/solution.py
@@ -12,6 +12,7 @@
 SUB = 8
 LO = 8
 GROUP = 4 * DEPTH
+HALO_LAYERS = 16
 F32 = jnp.float32
 HBM_SPEC = pl.BlockSpec(memory_space=pltpu.HBM)
 VMEM_SPEC = pl.BlockSpec(memory_space=pltpu.VMEM)
@@ -83,7 +84,7 @@
 def own_kernel(
     log_hbm,
     src_hbm,
-    base_ref,
+    fields_ref,
     inverse_ref,
     face_x_ref,
     face_y_ref,
@@ -98,6 +99,7 @@
     slots = layers // (LANES // GROUP)
     ring = LO + rows + SUB
     last_lane = lane_ids() == LANES - 1
+    base_ref = fields_ref.at[0]
     copies = []
     for index, (hbm, ref) in enumerate(((log_hbm, log_ref), (src_hbm, base_ref))):
         for tile in range(tiles):
@@ -140,7 +142,8 @@
                 other = moved[tile]
                 if tile < tiles - 1:
                     other = jnp.where(last_lane, moved[tile + 1], other)
-                face_y_ref[layer, tile, at(block), :] = reciprocal(values[tile] + other)
+                face = reciprocal(values[tile] + other)
+                face_y_ref[layer, tile, at(block), :] = face if tile < tiles - 1 else jnp.where(last_lane, 0.0, face)
                 face_x_ref[layer, tile, at(block), :] = reciprocal(
                     values[tile] + inverse_ref[layer, tile, at(block, 1), :]
                 )
@@ -191,49 +194,36 @@
     far_ref[...] = jnp.where(two, first_ref[...], last_ref[...])
 
 
-def basis_kernel(
-    halo_ref,
-    last_ref,
-    first_ref,
-    near_ref,
-    far_ref,
-    base_in,
-    inverse_in,
-    face_x_in,
-    face_y_in,
-    face_z_in,
-    base_ref,
-    inverse_ref,
-    face_x_ref,
-    face_y_ref,
-    face_z_ref,
-    one_ref,
-    two_ref,
-    three_ref,
-    four_ref,
-    rims_ref,
-    sums_ref,
-    strip_ref,
-    strip_inv_ref,
-    strip_x_ref,
-    strip_y_ref,
-    strip_z_ref,
-    rim_ref,
-):
-    del base_in, inverse_in, face_x_in, face_y_in, face_z_in
-    layers, tiles, height, _ = base_ref.shape
-    rows = height - 3 * SUB
-    slots = layers // (LANES // GROUP)
-    groups = layers // slots
-    blocks = rows // SUB
-    ring = LO + rows + SUB
-    lanes = lane_ids()
-    place = lanes % GROUP
-    subs = row_ids()
+def place_of(block, step=0):
+    return pl.ds(LO + block * SUB + step, SUB)
+
+
+def close_ring(ref, index, block, blocks, value):
+    ring = LO + (blocks + 1) * SUB
+    if block == 0:
+        ref[(*index, pl.ds(ring, 1), slice(None))] = value[0:1]
+    if block == blocks:
+        ref[(*index, pl.ds(LO - 1, 1), slice(None))] = value[SUB - 1 : SUB]
+
+
+def rim_of(values, group):
+    return pltpu.roll(values, LANES - 1 - DEPTH - group * GROUP, 1)
+
+
+def x_part(face_ref, index, old, old_index, block, value):
+    there = old[(*old_index, place_of(block, 1), slice(None))]
+    back = old[(*old_index, place_of(block, -1), slice(None))]
+    return face_ref[(*index, place_of(block), slice(None))] * (value - there) - face_ref[
+        (*index, place_of(block, -1), slice(None))
+    ] * (back - value)
+
+
+def inside_masks():
     here_x, here_y = lax.axis_index("gx"), lax.axis_index("gy")
     past_x, before_x = here_x < lax.axis_size("gx") - 1, here_x > 0
     past_y, before_y = here_y < lax.axis_size("gy") - 1, here_y > 0
-    inside_rows = jnp.where(subs < DEPTH, past_x.astype(jnp.int32), before_x.astype(jnp.int32)) > 0
+    place = lane_ids() % GROUP
+    inside_rows = jnp.where(row_ids() < DEPTH, past_x.astype(jnp.int32), before_x.astype(jnp.int32)) > 0
     inside_cols = (
         jnp.where(
             (place >= DEPTH) & (place < 2 * DEPTH),
@@ -242,18 +232,175 @@
         )
         > 0
     )
+    return inside_rows, inside_cols
+
+
+def apply_power(number, fields_ref, face_x_ref, face_y_ref, face_z_ref, rims_ref):
+    _, layers, tiles, height, _ = fields_ref.shape
+    blocks = (height - 3 * SUB) // SUB
+    slots = layers // (LANES // GROUP)
+    groups = layers // slots
+    old, new = fields_ref.at[number - 1], fields_ref.at[number]
+    lanes = lane_ids()
+    first_lane, last_lane = lanes == 0, lanes == LANES - 1
+    inside_rows, _ = inside_masks()
+    at = place_of
+
+    def layer_range(start, count, block):
+        levels = []
+        for step in range(-1, count + 1):
+            layer = start + step
+            if step < 0:
+                layer = jnp.maximum(layer, 0)
+            if step == count:
+                layer = jnp.minimum(layer, layers - 1)
+            levels.append([old[layer, tile, at(block), :] for tile in range(tiles)])
+        ups = [
+            [
+                face_z_ref[start + step, tile, at(block), :] * (levels[step][tile] - levels[step + 1][tile])
+                for tile in range(tiles)
+            ]
+            for step in range(count + 1)
+        ]
+        for step in range(count):
+            layer = start + step
+            values = levels[step + 1]
+            moved = [turn(value, -1) for value in values]
+            flux = []
+            for tile in range(tiles):
+                other = moved[tile]
+                if tile < tiles - 1:
+                    other = jnp.where(last_lane, moved[tile + 1], other)
+                flux.append(face_y_ref[layer, tile, at(block), :] * (values[tile] - other))
+            rim = None
+            if rims_ref is not None:
+                rim = rim_of(rims_ref[number - 1, step % slots, at(block), :], start // slots + step // slots)
+            moved = [turn(value, 1) for value in flux]
+            moved = [moved[-1] if rim is None else rim] + moved
+            if rim is not None:
+                flux[-1] = jnp.where(last_lane, rim, flux[-1])
+            for tile in range(tiles):
+                value = values[tile]
+                result = (
+                    (flux[tile] - jnp.where(first_lane, moved[tile], moved[tile + 1]))
+                    + x_part(face_x_ref, (layer, tile), old, (layer, tile), block, value)
+                    + (ups[step + 1][tile] - ups[step][tile])
+                )
+                if block == blocks:
+                    result = jnp.where(inside_rows, result, 0.0)
+                new[layer, tile, at(block), :] = result
+                if number < DEPTH:
+                    close_ring(new, (layer, tile), block, blocks, result)
+                yield tile, value, result
+
+    def chunk(group, sums):
+        own_sums, next_sums = list(sums[0]), list(sums[1])
+        for block in range(blocks):
+            for tile, value, result in layer_range(group * slots, slots, block):
+                own_sums[tile] = own_sums[tile] + value * value
+                next_sums[tile] = next_sums[tile] + value * result
+        return tuple(own_sums), tuple(next_sums)
+
+    def halo_chunk(part, _):
+        for _ in layer_range(part * HALO_LAYERS, HALO_LAYERS, blocks):
+            pass
+        return 0
+
+    start = (jnp.zeros((SUB, LANES), F32),) * tiles
+    sums = lax.fori_loop(0, groups, chunk, (start, start), unroll=2)
+    if number < DEPTH:
+        lax.fori_loop(0, layers // HALO_LAYERS, halo_chunk, 0)
+    return [functools.reduce(jnp.add, parts) for parts in sums]
+
+
+def first_kernel(
+    halo_ref,
+    fields_in,
+    inverse_in,
+    face_x_in,
+    face_y_in,
+    face_z_in,
+    fields_ref,
+    inverse_ref,
+    face_x_ref,
+    face_y_ref,
+    face_z_ref,
+    parts_ref,
+):
+    del fields_in, inverse_in, face_x_in, face_y_in, face_z_in
+    _, layers, tiles, height, _ = fields_ref.shape
+    blocks = (height - 3 * SUB) // SUB
+    slots = layers // (LANES // GROUP)
+    last_lane = lane_ids() == LANES - 1
+    at = place_of
+
+    def fill(layer, _):
+        for tile in range(tiles):
+            source = halo_ref[1, layer, tile]
+            fields_ref[0, layer, tile, at(blocks), :] = source
+            close_ring(fields_ref, (0, layer, tile), blocks, blocks, source)
+            inverse_ref[layer, tile, at(blocks), :] = 0.5 * jnp.exp(-halo_ref[0, layer, tile])
+        return 0
+
+    lax.fori_loop(0, layers, fill, 0, unroll=2 * slots)
+
+    def faces(layer, _):
+        values = [inverse_ref[layer, tile, at(blocks), :] for tile in range(tiles)]
+        moved = [turn(value, -1) for value in values]
+        for tile in range(tiles):
+            other = moved[tile]
+            if tile < tiles - 1:
+                other = jnp.where(last_lane, moved[tile + 1], other)
+            face = reciprocal(values[tile] + other)
+            face_y_ref[layer, tile, at(blocks), :] = face if tile < tiles - 1 else jnp.where(last_lane, 0.0, face)
+            for block in (blocks - 1, blocks):
+                face = reciprocal(
+                    inverse_ref[layer, tile, at(block), :] + inverse_ref[layer, tile, at(block, 1), :]
+                )
+                face_x_ref[layer, tile, at(block), :] = face
+                close_ring(face_x_ref, (layer, tile), block, blocks, face)
+            before = inverse_ref[jnp.maximum(layer - 1, 0), tile, at(blocks), :]
+            face_z_ref[layer, tile, at(blocks), :] = jnp.where(layer > 0, reciprocal(before + values[tile]), 0.0)
+        return 0
+
+    lax.fori_loop(0, layers, faces, 0, unroll=2 * slots)
+    found = apply_power(1, fields_ref, face_x_ref, face_y_ref, face_z_ref, None)
+    for which, part in enumerate(found):
+        parts_ref[which] = part
+
+
+def basis_kernel(
+    last_ref,
+    first_ref,
+    far_ref,
+    near_ref,
+    parts_ref,
+    face_x_ref,
+    face_y_ref,
+    face_z_ref,
+    fields_in,
+    fields_ref,
+    rims_ref,
+    sums_ref,
+    strip_ref,
+    strip_inv_ref,
+    strip_x_ref,
+    strip_y_ref,
+    strip_z_ref,
+):
+    del fields_in
+    _, layers, tiles, height, _ = fields_ref.shape
+    rows = height - 3 * SUB
+    slots = layers // (LANES // GROUP)
+    groups = layers // slots
+    blocks = rows // SUB
+    lanes = lane_ids()
+    place = lanes % GROUP
+    inside_rows, inside_cols = inside_masks()
     inside_both = inside_rows & inside_cols
     first_lane, last_lane = lanes == 0, lanes == LANES - 1
     first_y = even("gy")
-
-    def at(block, step=0):
-        return pl.ds(LO + block * SUB + step, SUB)
-
-    def close_ring(ref, index, block, value):
-        if block == 0:
-            ref[(*index, pl.ds(ring, 1), slice(None))] = value[0:1]
-        if block == blocks:
-            ref[(*index, pl.ds(LO - 1, 1), slice(None))] = value[SUB - 1 : SUB]
+    at = place_of
 
     def spread(index, block):
         part = pl.ds(block * SUB, SUB)
@@ -281,31 +428,19 @@
         ref[slots + 1, at(block), :] = turn(values[0], -GROUP)
         for slot, value in enumerate(values):
             ref[slot + 1, at(block), :] = value
-            close_ring(ref, (slot + 1,), block, value)
-
-    def rim_of(values, group):
-        return pltpu.roll(values, LANES - 1 - DEPTH - group * GROUP, 1)
-
-    def x_part(face_ref, index, old, old_index, block, value):
-        there = old[(*old_index, at(block, 1), slice(None))]
-        back = old[(*old_index, at(block, -1), slice(None))]
-        return face_ref[(*index, at(block), slice(None))] * (value - there) - face_ref[
-            (*index, at(block, -1), slice(None))
-        ] * (back - value)
+            close_ring(ref, (slot + 1,), block, blocks, value)
 
     for block in range(blocks + 1):
         put_strip(strip_ref.at[0], block, spread(1, block))
         values = [0.5 * jnp.exp(-value) for value in spread(0, block)]
         put_strip(strip_inv_ref, block, values)
-        for slot, value in enumerate(values):
-            rim_ref[slot, at(block), :] = value
     top, bottom = lanes >= LANES - GROUP, lanes < GROUP
     for block in range(blocks + 1):
         for slot in range(1, slots + 1):
             value = strip_inv_ref[slot, at(block), :]
             face = reciprocal(value + strip_inv_ref[slot, at(block, 1), :])
             strip_x_ref[slot - 1, at(block), :] = face
-            close_ring(strip_x_ref, (slot - 1,), block, face)
+            close_ring(strip_x_ref, (slot - 1,), block, blocks, face)
             strip_y_ref[slot - 1, at(block), :] = reciprocal(value + turn(value, -1))
         for slot in range(slots + 1):
             face = reciprocal(strip_inv_ref[slot, at(block), :] + strip_inv_ref[slot + 1, at(block), :])
@@ -326,12 +461,13 @@
             for slot in range(slots):
                 value = levels[slot + 1]
                 flux = strip_y_ref[slot, at(block), :] * (value - turn(value, -1))
+                after = turn(flux, 1)
                 rims_ref[power - 1, slot, at(block), :] = jnp.where(
-                    place == DEPTH, value, turn(flux, 2 - 2 * DEPTH)
+                    place == DEPTH, after, turn(flux, 2 - 2 * DEPTH)
                 )
                 if power < DEPTH:
                     result = (
-                        (flux - turn(flux, 1))
+                        (flux - after)
                         + x_part(strip_x_ref, (slot,), old, (slot + 1,), block, value)
                         + (ups[slot + 1] - ups[slot])
                     )
@@ -339,117 +475,34 @@
             if power < DEPTH:
                 put_strip(strip_ref.at[power], block, values)
 
-    def fill(layer, _):
-        for tile in range(tiles):
-            source = halo_ref[1, layer, tile]
-            base_ref[layer, tile, at(blocks), :] = source
-            close_ring(base_ref, (layer, tile), blocks, source)
-            inverse_ref[layer, tile, at(blocks), :] = 0.5 * jnp.exp(-halo_ref[0, layer, tile])
-        return 0
-
-    lax.fori_loop(0, layers, fill, 0, unroll=slots)
-
-    def faces(group, _):
+    zero = jnp.zeros((SUB, LANES), F32)
+
+    def complete(group, lost):
         for slot in range(slots):
             layer = group * slots + slot
             for block in range(blocks + 1):
-                rim = rim_of(rim_ref[slot, at(block), :], group)
-                whole = block == blocks
-                values = [inverse_ref[layer, tile, at(block), :] for tile in range(tiles)]
-                if whole:
-                    moved = [turn(value, -1) for value in values] + [rim]
-                    for tile in range(tiles):
-                        other = jnp.where(last_lane, moved[tile + 1], moved[tile])
-                        face_y_ref[layer, tile, at(block), :] = reciprocal(values[tile] + other)
-                else:
-                    face_y_ref[layer, tiles - 1, at(block), :] = jnp.where(
-                        last_lane, reciprocal(values[-1] + rim), face_y_ref[layer, tiles - 1, at(block), :]
-                    )
-                if block >= blocks - 1:
-                    for tile in range(tiles):
-                        face = reciprocal(values[tile] + inverse_ref[layer, tile, at(block, 1), :])
-                        face_x_ref[layer, tile, at(block), :] = face
-                        close_ring(face_x_ref, (layer, tile), block, face)
-        return 0
-
-    lax.fori_loop(0, groups, faces, 0)
-
-    def faces_z(layer, _):
-        for tile in range(tiles):
-            face_z_ref[layer, tile, at(blocks), :] = reciprocal(
-                inverse_ref[layer - 1, tile, at(blocks), :] + inverse_ref[layer, tile, at(blocks), :]
-            )
-        return 0
-
-    lax.fori_loop(1, layers, faces_z, 0, unroll=slots)
-
-    zero = jnp.zeros((SUB, LANES), F32)
-
-    def power_step(number, old, new):
-        last_power = number == DEPTH
-
-        def chunk(group, sums):
-            own_sums, next_sums = list(sums[0]), list(sums[1])
-            for block in range(blocks if last_power else blocks + 1):
-                levels = []
-                for slot in range(-1, slots + 1):
-                    layer = group * slots + slot
-                    if slot < 0:
-                        layer = jnp.maximum(layer, 0)
-                    if slot == slots:
-                        layer = jnp.minimum(layer, layers - 1)
-                    levels.append([old[layer, tile, at(block), :] for tile in range(tiles)])
-                ups = [
-                    [
-                        face_z_ref[group * slots + slot, tile, at(block), :]
-                        * (levels[slot][tile] - levels[slot + 1][tile])
-                        for tile in range(tiles)
-                    ]
-                    for slot in range(slots + 1)
-                ]
-                for slot in range(slots):
-                    layer = group * slots + slot
-                    values = levels[slot + 1]
-                    rim = rim_of(rims_ref[number - 1, slot, at(block), :], group)
-                    moved = [turn(value, -1) for value in values] + [rim]
-                    flux = [
-                        face_y_ref[layer, tile, at(block), :]
-                        * (values[tile] - jnp.where(last_lane, moved[tile + 1], moved[tile]))
-                        for tile in range(tiles)
-                    ]
-                    moved = [rim] + [turn(value, 1) for value in flux]
-                    for tile in range(tiles):
-                        value = values[tile]
-                        result = (
-                            (flux[tile] - jnp.where(first_lane, moved[tile], moved[tile + 1]))
-                            + x_part(face_x_ref, (layer, tile), old, (layer, tile), block, value)
-                            + (ups[slot + 1][tile] - ups[slot][tile])
-                        )
-                        if block == blocks:
-                            result = jnp.where(inside_rows, result, 0.0)
-                        else:
-                            own_sums[tile] = own_sums[tile] + value * value
-                            next_sums[tile] = next_sums[tile] + value * result
-                        new[layer, tile, at(block), :] = result
-                        if not last_power:
-                            close_ring(new, (layer, tile), block, result)
-            return tuple(own_sums), tuple(next_sums)
-
-        start = (zero,) * tiles
-        own_sums, next_sums = lax.fori_loop(0, groups, chunk, (start, start), unroll=1)
-        found = []
-        for parts in (own_sums, next_sums):
-            total = functools.reduce(jnp.add, parts)
-            found.append(jnp.sum(total, axis=0, keepdims=True))
-        return found
-
-    fields = (base_ref, one_ref, two_ref, three_ref, four_ref)
-    found = []
-    for number in range(1, DEPTH + 1):
-        found += power_step(number, fields[number - 1], fields[number])
-    total = jnp.concatenate(found, axis=0)
-    for peer in range(sums_ref.shape[0]):
-        sums_ref[peer] = total
+                rim = rim_of(rims_ref[0, slot, at(block), :], group)
+                for tile, part in ((0, jnp.where(first_lane, -rim, 0.0)), (tiles - 1, jnp.where(last_lane, rim, 0.0))):
+                    value = fields_ref[1, layer, tile, at(block), :] + part
+                    fields_ref[1, layer, tile, at(block), :] = value
+                    close_ring(fields_ref, (1, layer, tile), block, blocks, value)
+                    if block < blocks:
+                        lost = lost + part * fields_ref[0, layer, tile, at(block), :]
+        return lost
+
+    lost = lax.fori_loop(0, groups, complete, zero)
+
+    found = [parts_ref[0], parts_ref[1] + lost]
+    for number in range(2, DEPTH + 1):
+        found += apply_power(number, fields_ref, face_x_ref, face_y_ref, face_z_ref, rims_ref)
+    total = jnp.concatenate([jnp.sum(part, axis=0, keepdims=True) for part in found], axis=0)
+    share = LANES // SUB
+    step = LANES // 2
+    while step >= share:
+        total = total + turn(total, step)
+        step //= 2
+    total = jnp.sum(jnp.where(lanes // share == row_ids(), total, 0.0), axis=0, keepdims=True)
+    sums_ref[...] = jnp.broadcast_to(total, sums_ref.shape)
 
 
 def two_sum(first, second):
@@ -521,11 +574,7 @@
 
 def finish_kernel(
     sums_ref,
-    base_ref,
-    one_ref,
-    two_ref,
-    three_ref,
-    four_ref,
+    fields_ref,
     face_x_ref,
     face_y_ref,
     rims_ref,
@@ -540,14 +589,14 @@
     field_ref,
     sems,
 ):
-    layers, tiles, height, _ = base_ref.shape
+    _, layers, tiles, height, _ = fields_ref.shape
     rows = height - 3 * SUB
     slots = layers // (LANES // GROUP)
     blocks = rows // SUB
     last_lane = lane_ids() == LANES - 1
-    fields = (base_ref, one_ref, two_ref, three_ref, four_ref)
-
-    total = functools.reduce(jnp.add, [sums_ref[peer] for peer in range(sums_ref.shape[0])])
+
+    total = jnp.sum(sums_ref[...], axis=0, keepdims=True)
+    total = jnp.where(lane_ids() // (LANES // SUB) == row_ids(), total, 0.0)
     rest = jnp.zeros((SUB, LANES), F32)
     step = 1
     while step < LANES:
@@ -584,7 +633,9 @@
             for block in range(blocks + 1):
                 values = []
                 for tile in range(tiles):
-                    found = [ref[layer, tile, at(block), :] for ref in fields[: DEPTH + (block < blocks)]]
+                    found = [
+                        fields_ref[power, layer, tile, at(block), :] for power in range(DEPTH + (block < blocks))
+                    ]
                     value = mix(found[:DEPTH])
                     values.append(value)
                     field_ref[tile, at(block), :] = value
@@ -594,12 +645,17 @@
                         residual_ref[spot] = found[0] - mix(found[1:])
                 if block < blocks:
                     rim = mix([rims_ref[power, slot, at(block), :] for power in range(DEPTH)])
-                    rim = pltpu.roll(rim, LANES - 1 - DEPTH - group * GROUP, 1)
-                    moved = [turn(value, -1) for value in values] + [rim]
+                    rim = rim_of(rim, group)
+                    moved = [turn(value, -1) for value in values]
                     for tile in range(tiles):
-                        other = jnp.where(last_lane, moved[tile + 1], moved[tile])
+                        other = moved[tile]
+                        if tile < tiles - 1:
+                            other = jnp.where(last_lane, moved[tile + 1], other)
+                        flux = face_y_ref[layer, tile, at(block), :] * (values[tile] - other)
+                        if tile == tiles - 1:
+                            flux = jnp.where(last_lane, rim, flux)
                         spot = (layer, pl.ds(block * SUB, SUB), pl.ds(tile * LANES, LANES))
-                        north_ref[spot] = face_y_ref[layer, tile, at(block), :] * (values[tile] - other)
+                        north_ref[spot] = flux
             for block in range(blocks):
                 for tile in range(tiles):
                     spot = (layer, pl.ds(block * SUB, SUB), pl.ds(tile * LANES, LANES))
@@ -643,6 +699,8 @@
     peers = lax.axis_size("gx") * lax.axis_size("gy")
     cells = layers * rows * cols
 
+    log_perm, source = (pltpu.with_memory_space_constraint(value, pltpu.HBM) for value in (log_perm, source))
+    powers = (in_vmem(DEPTH + 1, *full),) + (in_vmem(*full),) * 3 + (in_vmem(*deep),)
     near, far = pl.pallas_call(
         ends_kernel,
         out_shape=(in_vmem(*ends),) * 2,
@@ -656,7 +714,7 @@
     near = exchange(near, "gx", True)
     *fields, last, first = pl.pallas_call(
         own_kernel,
-        out_shape=(in_vmem(*full),) * 4 + (in_vmem(*deep),) + (in_vmem(*edges),) * 2,
+        out_shape=powers + (in_vmem(*edges),) * 2,
         in_specs=[HBM_SPEC] * 2,
         out_specs=[VMEM_SPEC] * 7,
         scratch_shapes=[in_vmem(*full), pltpu.SemaphoreType.DMA((2, tiles))],
@@ -675,39 +733,44 @@
     )(near, far, last, first)
     far = exchange(far, "gy", False)
     near = exchange(near, "gy", True)
-    results = pl.pallas_call(
+    fields, _, face_x, face_y, face_z, parts = pl.pallas_call(
+        first_kernel,
+        out_shape=powers + (in_vmem(2, SUB, LANES),),
+        in_specs=[VMEM_SPEC] * 6,
+        out_specs=[VMEM_SPEC] * 6,
+        input_output_aliases={1: 0, 2: 1, 3: 2, 4: 3, 5: 4},
+        compiler_params=params(16),
+        cost_estimate=pl.CostEstimate(flops=40 * cells, bytes_accessed=8 * cells, transcendentals=cells),
+        name="first",
+    )(halo, *fields)
+    fields, rims, sums = pl.pallas_call(
         basis_kernel,
-        out_shape=(in_vmem(*full),) * 4
-        + (in_vmem(*deep),)
-        + (in_vmem(*full),) * 4
-        + (in_vmem(DEPTH, *inner), in_vmem(peers, SUB, LANES)),
-        in_specs=[VMEM_SPEC] * 10,
-        out_specs=[VMEM_SPEC] * 11,
-        input_output_aliases={5: 0, 6: 1, 7: 2, 8: 3, 9: 4},
+        out_shape=(powers[0], in_vmem(DEPTH, *inner), in_vmem(peers, LANES)),
+        in_specs=[VMEM_SPEC] * 9,
+        out_specs=[VMEM_SPEC] * 3,
+        input_output_aliases={8: 0},
         scratch_shapes=[
             in_vmem(DEPTH, *strip),
             in_vmem(*strip),
             in_vmem(*inner),
             in_vmem(*inner),
             in_vmem(slots + 1, height, LANES),
-            in_vmem(*inner),
         ],
         compiler_params=params(16),
         name="basis",
-    )(halo, last, first, near, far, *fields)
-    base, _, face_x, face_y, _, *powers, rims, sums = results
-    sums = lax.all_to_all(sums, ("gx", "gy"), 0, 0)
+    )(last, first, far, near, parts, face_x, face_y, face_z, fields)
+    sums = lax.all_to_all(sums, ("gx", "gy"), 0, 0, tiled=True)
     block = (layers, rows, cols)
     return pl.pallas_call(
         finish_kernel,
         out_shape=(jax.ShapeDtypeStruct((1, *block), F32),) * 4,
-        in_specs=[VMEM_SPEC] * 9,
+        in_specs=[VMEM_SPEC] * 5,
         out_specs=[ANY_SPEC] * 4,
         scratch_shapes=[in_vmem(*block)] * 4
         + [in_vmem(tiles, height, LANES), pltpu.SemaphoreType.DMA((4, layers // slots))],
         compiler_params=params(16),
         name="finish",
-    )(sums, base, *powers, face_x, face_y, rims)
+    )(sums, fields, face_x, face_y, rims)
 
 
 def solution(mesh):

time: 46.6 us -> 40.9 us (0.88)
  blocking collectives: 22.1 us -> 16 us
  starting transfers between devices: 4.41 us -> 7.22 us
  local copies, waits for them, and re-layouts: 2.44 us -> 0 us
  Pallas kernels: 15.4 us -> 16.8 us
  waiting for transfers between devices: 1.33 us -> 0.01 us
    all_to_all x1, blocking collectives: 22.1 us -> 16 us  [on_device(): sums = lax.all_to_all(sums, ('gx', 'gy'), 0, 0, tiled=True)]
    ppermute x4, starting transfers between devices: 4.41 us -> 7.22 us  [exchange(): return lax.ppermute(value, axis, pairs)]
    unnamed x4 -> x0, local copies, waits for them, and re-layouts: 2.44 us -> none
    ppermute x4, waiting for transfers between devices: 1.33 us -> 0.01 us  [exchange(): return lax.ppermute(value, axis, pairs)]
    pallas_call x1, Pallas kernels: 0.33 us -> 1.47 us  [on_device(): pl.pallas_call(ends_kernel, out_shape=(in_vmem(*ends),) * 2, in_specs=[HB...]
    pallas_call x2 -> x3, Pallas kernels: 11.4 us -> 11.7 us  [the longest x1 6.55 us: on_device(): pl.pallas_call(basis_kernel, out_shape=(powers[0], in_vmem(DEPTH, *inner)...]
  transfers between devices with their start and end apart: 4 -> 4, of which waited for: 1 -> 0; matrix products, arithmetic and copies ran while one was open for 0% -> 0% of each run, Pallas kernels for 5% -> 13%
where the time goes in v2:
time: 40.9 us; the launch traced here: 40.7 us
  Pallas kernels  16.8 us (41%)
  blocking collectives  16 us (39%)
  starting transfers between devices  7.22 us (18%)
  between operations  0.71 us (2%)
    all_to_all x1, blocking collectives, on_device(): sums = lax.all_to_all(sums, ('gx', 'gy'), 0, 0, tiled=True)  16 us
    ppermute x4, starting transfers between devices, exchange(): return lax.ppermute(value, axis, pairs)  7.22 us
    pallas_call x1, Pallas kernels, on_device(): pl.pallas_call(basis_kernel, out_shape=(powers[0], in_vmem(DEPTH, *inner)...  6.55 us
    pallas_call x1, Pallas kernels, on_device(): pl.pallas_call(finish_kernel, out_shape=(jax.ShapeDtypeStruct((1, *block)...  3.32 us
    pallas_call x1, Pallas kernels, on_device(): pl.pallas_call(own_kernel, out_shape=powers + (in_vmem(*edges),) * 2, in_...  3.19 us
    pallas_call x1, Pallas kernels, on_device(): pl.pallas_call(first_kernel, out_shape=powers + (in_vmem(2, SUB, LANES),)...  1.97 us
    pallas_call x1, Pallas kernels, on_device(): pl.pallas_call(ends_kernel, out_shape=(in_vmem(*ends),) * 2, in_specs=[HB...  1.47 us
  transfers between devices with their start and end apart: 4, of which 0 were waited for; matrix products, arithmetic and copies ran while one was open for 0% of the time, Pallas kernels for 13%

profile of v2, /device:TPU:0, one launch (start us, length us, event | category | flops | bytes accessed | tf_op | source)
XLA Modules:
  0.0 40.7 jit_solution(4294406642751505249)
XLA Ops:
  0.6 1.5 %ends.1 = (f32[2,32,8,128]{3,2,1,0:T(8,128)S(1)}, f32[2,32,8,128]{3,2,1,0:T(8,128)S(1)}) custom-call(f32[1,32,32,256]{3,2,1,0:T(8,128)} %log_hbm.3, f32[1,32,32,256]{3,2,1,0:T(8,128)} %src_hbm.3), custom_call_target="tpu_custom_call" | custom-call | tf_op jit(solution)/shard_map/ends/pallas_call | solution.py:704
  2.1 0.5 %collective-permute-start = (f32[2,32,8,128]{3,2,1,0:T(8,128)S(1)}, f32[2,32,8,128]{3,2,1,0:T(8,128)S(1)}, u32[]{:S(2)}, u32[]{:S(2)}) collective-permute-start(f32[2,32,8,128]{3,2,1,0:T(8,128)S(1)} %get-tuple-element.26), channel_id=1, source_target_pairs={{0,8},{8,0},{16,24},{24,16},{1,9},{9,1},{17,25},{25,17},{2,10},{10... | collective-permute-start | bytes 786440 | tf_op jit(solution)/shard_map/ppermute | solution.py:686
  2.6 0.7 %collective-permute-start.1 = (f32[2,32,8,128]{3,2,1,0:T(8,128)S(1)}, f32[2,32,8,128]{3,2,1,0:T(8,128)S(1)}, u32[]{:S(2)}, u32[]{:S(2)}) collective-permute-start(f32[2,32,8,128]{3,2,1,0:T(8,128)S(1)} %get-tuple-element.27), channel_id=1, source_target_pairs={{8,16},{16,8},{9,17},{17,9},{10,18},{18,10},{11,19},{19,11},{12,20... | collective-permute-start | bytes 786440 | tf_op jit(solution)/shard_map/ppermute | solution.py:686
  3.3 3.2 %own.1 = (f32[5,32,2,56,128]{4,3,2,1,0:T(8,128)S(1)}, f32[32,2,56,128]{3,2,1,0:T(8,128)S(1)}, f32[32,2,56,128]{3,2,1,0:T(8,128)S(1)}, f32[32,2,56,128]{3,2,1,0:T...) custom-call(f32[1,32,32,256]{3,2,1,0:T(8,128)} %log_hbm.3, ...), custom_call_target="tpu_custom_call" | custom-call | flops 15728640 | bytes 2097152 | tf_op jit(solution)/shard_map/own/pallas_call | solution.py:715
  6.5 0.0 collective-permute-done.near_in
  6.5 0.0 collective-permute-done.1.far_in
  6.5 0.2 edges.1
  6.8 0.7 %collective-permute-start.2 = (f32[2,40,128]{2,1,0:T(8,128)S(1)}, f32[2,40,128]{2,1,0:T(8,128)S(1)}, u32[]{:S(2)}, u32[]{:S(2)}) collective-permute-start(f32[2,40,128]{2,1,0:T(8,128)S(1)} %get-tuple-element.32), channel_id=1, source_target_pairs={{1,2},{2,1},{3,4},{4,3},{5,6},{6,5},{9,10},{10,9},{11,12},{12,11},... | collective-permute-start | bytes 122888 | tf_op jit(solution)/shard_map/ppermute | solution.py:686
  7.5 5.4 %collective-permute-start.3 = (f32[2,40,128]{2,1,0:T(8,128)S(1)}, f32[2,40,128]{2,1,0:T(8,128)S(1)}, u32[]{:S(2)}, u32[]{:S(2)}) collective-permute-start(f32[2,40,128]{2,1,0:T(8,128)S(1)} %get-tuple-element.33), channel_id=1, source_target_pairs={{0,1},{1,0},{2,3},{3,2},{4,5},{5,4},{6,7},{7,6},{8,9},{9,8},{10,11... | collective-permute-start | bytes 122888 | tf_op jit(solution)/shard_map/ppermute | solution.py:686
  12.8 2.0 %first.1 = (f32[5,32,2,56,128]{4,3,2,1,0:T(8,128)S(1)}, f32[32,2,56,128]{3,2,1,0:T(8,128)S(1)}, f32[32,2,56,128]{3,2,1,0:T(8,128)S(1)}, f32[32,2,56,128]{3,2,1,0...) custom-call(f32[2,32,2,8,128]{4,3,2,1,0:T(8,128)S(1)} %get-tuple-ele, ...), custom_call_target="tpu_custom_call", output_to_operand_aliasing={{0}: (1, {}), {1}: (2, {}), {2}: (3, {}), {3}: (4, {}), {4}... | custom-call | flops 10485760 | bytes 2097152 | tf_op jit(solution)/shard_map/first/pallas_call | solution.py:736
  14.8 0.0 collective-permute-done.2.far_ref
  14.8 0.0 collective-permute-done.3.near_ref
  14.8 6.5 %basis.1 = (f32[5,32,2,56,128]{4,3,2,1,0:T(8,128)S(1)}, f32[4,4,56,128]{3,2,1,0:T(8,128)S(1)}, f32[32,128]{1,0:T(8,128)S(1)}) custom-call(f32[2,40,128]{2,1,0:T(8,128)S(1)} %get-tuple-element.30.last_ref, f32[2,40,128]{2,1,0:T(8,128)S(1)} %get-tuple-element.31.first_ref, ...), custom_call_target="tpu_custom_call", output_to_operand_aliasing={{0}: (8, {})} | custom-call | tf_op jit(solution)/shard_map/basis/pallas_call | solution.py:746
  21.4 16.0 %all_to_all.11 = f32[32,1,128]{2,1,0:T(1,128)S(1)} all-to-all(f32[32,1,128]{2,1,0:T(1,128)S(1)} %bitcast.5), channel_id=1, replica_groups=mesh['gx'=4,'gy'=8] {'gx','gy'}, dimensions={0} | all-to-all | bytes 32768 | tf_op jit(solution)/shard_map/all_to_all | solution.py:762
  37.4 3.3 %finish.1 = (f32[1,32,32,256]{3,2,1,0:T(8,128)}, f32[1,32,32,256]{3,2,1,0:T(8,128)}, f32[1,32,32,256]{3,2,1,0:T(8,128)}, f32[1,32,32,256]{3,2,1,0:T(8,128)}) custom-call(f32[32,128]{1,0:T(8,128)S(1)} %bitcast.4, f32[5,32,2,56,128]{4,3,2,1,0:T(8,128)S(1)} %get-tuple-element.46.fields_ref, f32[32,2,56,128]{3,2,1,0:T(8,128)S(1)} %get-tuple-element.41.face_x_ref, ...), custom_call_target="tpu_custom_call" | custom-call | tf_op jit(solution)/shard_map/finish/pallas_call | solution.py:764
Async XLA Ops:
  2.1 4.4 %collective-permute-start = (f32[2,32,8,128]{3,2,1,0:T(8,128)S(1)}, f32[2,32,8,128]{3,2,1,0:T(8,128)S(1)}, u32[]{:S(2)}, u32[]{:S(2)}) collective-permute-start(f32[2,32,8,128]{3,2,1,0:T(8,128)S(1)} %get-tuple-element.26), channel_id=1, source_target_pairs={{0,8},{8,0},{16,24},{24,16},{1,9},{9,1},{17,25},{25,17},{2,10},{10... | collective-permute-start | bytes 786440 | tf_op jit(solution)/shard_map/ppermute | solution.py:686
  2.6 3.9 %collective-permute-start.1 = (f32[2,32,8,128]{3,2,1,0:T(8,128)S(1)}, f32[2,32,8,128]{3,2,1,0:T(8,128)S(1)}, u32[]{:S(2)}, u32[]{:S(2)}) collective-permute-start(f32[2,32,8,128]{3,2,1,0:T(8,128)S(1)} %get-tuple-element.27), channel_id=1, source_target_pairs={{8,16},{16,8},{9,17},{17,9},{10,18},{18,10},{11,19},{19,11},{12,20... | collective-permute-start | bytes 786440 | tf_op jit(solution)/shard_map/ppermute | solution.py:686
  6.8 8.0 %collective-permute-start.2 = (f32[2,40,128]{2,1,0:T(8,128)S(1)}, f32[2,40,128]{2,1,0:T(8,128)S(1)}, u32[]{:S(2)}, u32[]{:S(2)}) collective-permute-start(f32[2,40,128]{2,1,0:T(8,128)S(1)} %get-tuple-element.32), channel_id=1, source_target_pairs={{1,2},{2,1},{3,4},{4,3},{5,6},{6,5},{9,10},{10,9},{11,12},{12,11},... | collective-permute-start | bytes 122888 | tf_op jit(solution)/shard_map/ppermute | solution.py:686
  7.5 7.4 %collective-permute-start.3 = (f32[2,40,128]{2,1,0:T(8,128)S(1)}, f32[2,40,128]{2,1,0:T(8,128)S(1)}, u32[]{:S(2)}, u32[]{:S(2)}) collective-permute-start(f32[2,40,128]{2,1,0:T(8,128)S(1)} %get-tuple-element.33), channel_id=1, source_target_pairs={{0,1},{1,0},{2,3},{3,2},{4,5},{5,4},{6,7},{7,6},{8,9},{9,8},{10,11... | collective-permute-start | bytes 122888 | tf_op jit(solution)/shard_map/ppermute | solution.py:686

commit v3 on v2

--- a/solution.py
+++ b/solution.py
@@ -47,61 +47,36 @@
     return lax.rem(lax.axis_index(axis), 2) == 0
 
 
-def ends_kernel(log_hbm, src_hbm, near_ref, far_ref, rows_ref, sems):
+def far_kernel(log_hbm, src_hbm, far_ref, rows_ref, sems):
     _, _, rows, cols = log_hbm.shape
+    first = even("gx")
+    start = pl.multiple_of(jnp.where(first, 0, rows - SUB), SUB)
     copies = []
     for index, hbm in enumerate((log_hbm, src_hbm)):
-        for end, start in enumerate((0, rows - SUB)):
-            for tile in range(cols // LANES):
-                copies.append(
-                    pltpu.make_async_copy(
-                        hbm.at[0, :, pl.ds(start, SUB), pl.ds(tile * LANES, LANES)],
-                        rows_ref.at[index, end, tile],
-                        sems.at[index, end, tile],
-                    )
+        for tile in range(cols // LANES):
+            copies.append(
+                pltpu.make_async_copy(
+                    hbm.at[0, :, pl.ds(start, SUB), pl.ds(tile * LANES, LANES)],
+                    rows_ref.at[index, tile],
+                    sems.at[index, tile],
                 )
-                copies[-1].start()
+            )
+            copies[-1].start()
     for copy in copies:
         copy.wait()
+    for tile in range(cols // LANES):
+        head = rows_ref[:, tile, :, 0:DEPTH, :]
+        tail = rows_ref[:, tile, :, SUB - DEPTH : SUB, :]
+        far_ref[:, :, pl.ds(tile * DEPTH, DEPTH), :] = jnp.where(first, head, tail)
+
+
+def load_kernel(log_hbm, src_hbm, log_ref, fields_ref, near_ref, sems):
+    _, _, rows, cols = log_hbm.shape
+    tiles = cols // LANES
     first = even("gx")
-    for tile in range(cols // LANES):
-        head = rows_ref[:, 0, tile, :, 0:DEPTH, :]
-        tail = rows_ref[:, 1, tile, :, SUB - DEPTH : SUB, :]
-        part = pl.ds(tile * DEPTH, DEPTH)
-        near_ref[:, :, part, :] = jnp.where(first, tail, head)
-        far_ref[:, :, part, :] = jnp.where(first, head, tail)
-
-
-def pack(blocks_of, lane):
-    lanes = lane_ids()
-    total = None
-    for layer, value in enumerate(blocks_of):
-        moved = turn(value, layer * DEPTH - lane)
-        total = moved if total is None else jnp.where(lanes // DEPTH == layer, moved, total)
-    return total
-
-
-def own_kernel(
-    log_hbm,
-    src_hbm,
-    fields_ref,
-    inverse_ref,
-    face_x_ref,
-    face_y_ref,
-    face_z_ref,
-    last_ref,
-    first_ref,
-    log_ref,
-    sems,
-):
-    _, layers, rows, cols = log_hbm.shape
-    tiles, blocks = cols // LANES, rows // SUB
-    slots = layers // (LANES // GROUP)
-    ring = LO + rows + SUB
-    last_lane = lane_ids() == LANES - 1
-    base_ref = fields_ref.at[0]
     copies = []
-    for index, (hbm, ref) in enumerate(((log_hbm, log_ref), (src_hbm, base_ref))):
+    refs = (log_ref, fields_ref.at[0])
+    for index, (hbm, ref) in enumerate(zip((log_hbm, src_hbm), refs, strict=True)):
         for tile in range(tiles):
             copies.append(
                 pltpu.make_async_copy(
@@ -111,8 +86,43 @@
                 )
             )
             copies[-1].start()
-    for copy in copies[:tiles]:
+    for copy in copies:
         copy.wait()
+    for index, ref in enumerate(refs):
+        for tile in range(tiles):
+            head = ref[:, tile, LO : LO + DEPTH, :]
+            tail = ref[:, tile, LO + rows - DEPTH : LO + rows, :]
+            near_ref[index, :, pl.ds(tile * DEPTH, DEPTH), :] = jnp.where(first, tail, head)
+
+
+def pack(blocks_of, lane):
+    lanes = lane_ids()
+    total = None
+    for layer, value in enumerate(blocks_of):
+        moved = turn(value, layer * DEPTH - lane)
+        total = moved if total is None else jnp.where(lanes // DEPTH == layer, moved, total)
+    return total
+
+
+def own_kernel(
+    log_ref,
+    fields_in,
+    fields_ref,
+    inverse_ref,
+    face_x_ref,
+    face_y_ref,
+    face_z_ref,
+    last_ref,
+    first_ref,
+):
+    del fields_in
+    layers, tiles, height, _ = log_ref.shape
+    rows = height - 3 * SUB
+    blocks = rows // SUB
+    slots = layers // (LANES // GROUP)
+    ring = LO + rows + SUB
+    last_lane = lane_ids() == LANES - 1
+    base_ref = fields_ref.at[0]
 
     def at(block, step=0):
         return pl.ds(LO + block * SUB + step, SUB)
@@ -161,9 +171,6 @@
 
     lax.fori_loop(1, layers, faces_z, 0, unroll=slots)
 
-    for copy in copies[tiles:]:
-        copy.wait()
-
     base_ref[:, :, pl.ds(ring, 1), :] = base_ref[:, :, pl.ds(LO, 1), :]
     for index, ref in enumerate((log_ref, base_ref)):
         for block in range(blocks):
@@ -174,7 +181,7 @@
             first_ref[index, part, :] = pack([ref[layer, 0, at(block), :] for layer in range(layers)], 0)
 
 
-def edge_kernel(near_in, far_in, last_in, first_in, last_ref, first_ref, near_ref, far_ref, halo_ref):
+def edge_kernel(far_in, near_in, last_in, first_in, last_ref, first_ref, near_ref, far_ref, halo_ref):
     del last_in, first_in
     _, layers, tiles, _, _ = halo_ref.shape
     height = last_ref.shape[1]
@@ -490,7 +497,7 @@
                         lost = lost + part * fields_ref[0, layer, tile, at(block), :]
         return lost
 
-    lost = lax.fori_loop(0, groups, complete, zero)
+    lost = lax.fori_loop(0, groups, complete, zero, unroll=4)
 
     found = [parts_ref[0], parts_ref[1] + lost]
     for number in range(2, DEPTH + 1):
@@ -700,28 +707,38 @@
     cells = layers * rows * cols
 
     log_perm, source = (pltpu.with_memory_space_constraint(value, pltpu.HBM) for value in (log_perm, source))
-    powers = (in_vmem(DEPTH + 1, *full),) + (in_vmem(*full),) * 3 + (in_vmem(*deep),)
-    near, far = pl.pallas_call(
-        ends_kernel,
-        out_shape=(in_vmem(*ends),) * 2,
+    powers = (in_vmem(DEPTH + 1, *full), in_vmem(*deep)) + (in_vmem(*full),) * 2 + (in_vmem(*deep),)
+    far = pl.pallas_call(
+        far_kernel,
+        out_shape=in_vmem(*ends),
         in_specs=[HBM_SPEC] * 2,
-        out_specs=[VMEM_SPEC] * 2,
-        scratch_shapes=[in_vmem(2, 2, tiles, layers, SUB, LANES), pltpu.SemaphoreType.DMA((2, 2, tiles))],
+        out_specs=VMEM_SPEC,
+        scratch_shapes=[in_vmem(2, tiles, layers, SUB, LANES), pltpu.SemaphoreType.DMA((2, tiles))],
         compiler_params=params(16),
-        name="ends",
+        name="far",
     )(log_perm, source)
     far = exchange(far, "gx", False)
+    log_own, fields, near = pl.pallas_call(
+        load_kernel,
+        out_shape=(in_vmem(*full), powers[0], in_vmem(*ends)),
+        in_specs=[HBM_SPEC] * 2,
+        out_specs=[VMEM_SPEC] * 3,
+        scratch_shapes=[pltpu.SemaphoreType.DMA((2, tiles))],
+        compiler_params=params(16),
+        cost_estimate=pl.CostEstimate(flops=cells, bytes_accessed=8 * cells, transcendentals=0),
+        name="load",
+    )(log_perm, source)
     near = exchange(near, "gx", True)
     *fields, last, first = pl.pallas_call(
         own_kernel,
         out_shape=powers + (in_vmem(*edges),) * 2,
-        in_specs=[HBM_SPEC] * 2,
+        in_specs=[VMEM_SPEC] * 2,
         out_specs=[VMEM_SPEC] * 7,
-        scratch_shapes=[in_vmem(*full), pltpu.SemaphoreType.DMA((2, tiles))],
+        input_output_aliases={1: 0},
         compiler_params=params(16),
         cost_estimate=pl.CostEstimate(flops=60 * cells, bytes_accessed=8 * cells, transcendentals=4 * cells),
         name="own",
-    )(log_perm, source)
+    )(log_own, fields)
     last, first, near, far, halo = pl.pallas_call(
         edge_kernel,
         out_shape=(in_vmem(*edges),) * 4 + (in_vmem(2, layers, tiles, SUB, LANES),),
@@ -730,7 +747,7 @@
         input_output_aliases={2: 0, 3: 1},
         compiler_params=params(16),
         name="edges",
-    )(near, far, last, first)
+    )(far, near, last, first)
     far = exchange(far, "gy", False)
     near = exchange(near, "gy", True)
     fields, _, face_x, face_y, face_z, parts = pl.pallas_call(

time: 40.9 us -> 40.2 us (0.983)
  blocking collectives: 16 us -> 12.7 us
  starting transfers between devices: 7.22 us -> 10.1 us
    all_to_all x1, blocking collectives: 16 us -> 12.7 us  [on_device(): sums = lax.all_to_all(sums, ('gx', 'gy'), 0, 0, tiled=True)]
    ppermute x4, starting transfers between devices: 7.22 us -> 10.1 us  [exchange(): return lax.ppermute(value, axis, pairs)]
    pallas_call x1 -> x2, Pallas kernels: 1.47 us -> 2.89 us  [the longest x1 1.67 us: on_device(): pl.pallas_call(load_kernel, out_shape=(in_vmem(*full), powers[0], in_vmem...]
    pallas_call x1, Pallas kernels: 3.19 us -> 1.89 us  [on_device(): pl.pallas_call(own_kernel, out_shape=powers + (in_vmem(*edges),) * 2, in_...]
    pallas_call x1, Pallas kernels: 6.55 us -> 6.11 us  [on_device(): pl.pallas_call(basis_kernel, out_shape=(powers[0], in_vmem(DEPTH, *inner)...]
  transfers between devices with their start and end apart: 4 -> 4, of which waited for: 0 -> 0; matrix products, arithmetic and copies ran while one was open for 0% -> 0% of each run, Pallas kernels for 13% -> 14%
where the time goes in v3:
time: 40.2 us; the launch traced here: 40 us
  Pallas kernels  16.4 us (41%)
  blocking collectives  12.7 us (32%)
  starting transfers between devices  10.1 us (25%)
  between operations  0.71 us (2%)
    all_to_all x1, blocking collectives, on_device(): sums = lax.all_to_all(sums, ('gx', 'gy'), 0, 0, tiled=True)  12.7 us
    ppermute x4, starting transfers between devices, exchange(): return lax.ppermute(value, axis, pairs)  10.1 us
    pallas_call x1, Pallas kernels, on_device(): pl.pallas_call(basis_kernel, out_shape=(powers[0], in_vmem(DEPTH, *inner)...  6.11 us
    pallas_call x1, Pallas kernels, on_device(): pl.pallas_call(finish_kernel, out_shape=(jax.ShapeDtypeStruct((1, *block)...  3.32 us
    pallas_call x1, Pallas kernels, on_device(): pl.pallas_call(first_kernel, out_shape=powers + (in_vmem(2, SUB, LANES),)...  1.97 us
    pallas_call x1, Pallas kernels, on_device(): pl.pallas_call(own_kernel, out_shape=powers + (in_vmem(*edges),) * 2, in_...  1.89 us
    pallas_call x1, Pallas kernels, on_device(): pl.pallas_call(load_kernel, out_shape=(in_vmem(*full), powers[0], in_vmem...  1.67 us
    pallas_call x1, Pallas kernels, on_device(): pl.pallas_call(far_kernel, out_shape=in_vmem(*ends), in_specs=[HBM_SPEC]...  1.22 us
  transfers between devices with their start and end apart: 4, of which 0 were waited for; matrix products, arithmetic and copies ran while one was open for 0% of the time, Pallas kernels for 14%

profile of v3, /device:TPU:0, one launch (start us, length us, event | category | flops | bytes accessed | tf_op | source)
XLA Modules:
  0.0 40.0 jit_solution(4002471712705891771)
XLA Ops:
  0.6 1.2 %far.1 = f32[2,32,8,128]{3,2,1,0:T(8,128)S(1)} custom-call(f32[1,32,32,256]{3,2,1,0:T(8,128)} %log_hbm.3, f32[1,32,32,256]{3,2,1,0:T(8,128)} %src_hbm.3), custom_call_target="tpu_custom_call" | custom-call | tf_op jit(solution)/shard_map/far/pallas_call | solution.py:711
  1.9 0.7 %collective-permute-start = (f32[2,32,8,128]{3,2,1,0:T(8,128)S(1)}, f32[2,32,8,128]{3,2,1,0:T(8,128)S(1)}, u32[]{:S(2)}, u32[]{:S(2)}) collective-permute-start(f32[2,32,8,128]{3,2,1,0:T(8,128)S(1)} %far.1), channel_id=1, source_target_pairs={{8,16},{16,8},{9,17},{17,9},{10,18},{18,10},{11,19},{19,11},{12,20... | collective-permute-start | bytes 786440 | tf_op jit(solution)/shard_map/ppermute | solution.py:693
  2.5 1.7 %load.1 = (f32[32,2,56,128]{3,2,1,0:T(8,128)S(1)}, f32[5,32,2,56,128]{4,3,2,1,0:T(8,128)S(1)}, f32[2,32,8,128]{3,2,1,0:T(8,128)S(1)}) custom-call(f32[1,32,32,256]{3,2,1,0:T(8,128)} %log_hbm.3, f32[1,32,32,256]{3,2,1,0:T(8,128)} %src_hbm.3), custom_call_target="tpu_custom_call" | custom-call | flops 262144 | bytes 2097152 | tf_op jit(solution)/shard_map/load/pallas_call | solution.py:721
  4.2 4.4 %collective-permute-start.1 = (f32[2,32,8,128]{3,2,1,0:T(8,128)S(1)}, f32[2,32,8,128]{3,2,1,0:T(8,128)S(1)}, u32[]{:S(2)}, u32[]{:S(2)}) collective-permute-start(f32[2,32,8,128]{3,2,1,0:T(8,128)S(1)} %get-tuple-element.27), channel_id=1, source_target_pairs={{0,8},{8,0},{16,24},{24,16},{1,9},{9,1},{17,25},{25,17},{2,10},{10... | collective-permute-start | bytes 786440 | tf_op jit(solution)/shard_map/ppermute | solution.py:693
  8.6 1.9 %own.1 = (f32[5,32,2,56,128]{4,3,2,1,0:T(8,128)S(1)}, f32[33,2,56,128]{3,2,1,0:T(8,128)S(1)}, f32[32,2,56,128]{3,2,1,0:T(8,128)S(1)}, f32[32,2,56,128]{3,2,1,0:T...) custom-call(f32[32,2,56,128]{3,2,1,0:T(8,128)S(1)} %get-tuple-elemen, ...), custom_call_target="tpu_custom_call", output_to_operand_aliasing={{0}: (1, {})} | custom-call | flops 15728640 | bytes 2097152 | tf_op jit(solution)/shard_map/own/pallas_call | solution.py:732
  10.5 0.0 collective-permute-done.far_in
  10.5 0.0 collective-permute-done.1.near_in
  10.5 0.2 edges.1
  10.8 0.7 %collective-permute-start.2 = (f32[2,40,128]{2,1,0:T(8,128)S(1)}, f32[2,40,128]{2,1,0:T(8,128)S(1)}, u32[]{:S(2)}, u32[]{:S(2)}) collective-permute-start(f32[2,40,128]{2,1,0:T(8,128)S(1)} %get-tuple-element.34), channel_id=1, source_target_pairs={{1,2},{2,1},{3,4},{4,3},{5,6},{6,5},{9,10},{10,9},{11,12},{12,11},... | collective-permute-start | bytes 122888 | tf_op jit(solution)/shard_map/ppermute | solution.py:693
  11.4 4.4 %collective-permute-start.3 = (f32[2,40,128]{2,1,0:T(8,128)S(1)}, f32[2,40,128]{2,1,0:T(8,128)S(1)}, u32[]{:S(2)}, u32[]{:S(2)}) collective-permute-start(f32[2,40,128]{2,1,0:T(8,128)S(1)} %get-tuple-element.35), channel_id=1, source_target_pairs={{0,1},{1,0},{2,3},{3,2},{4,5},{5,4},{6,7},{7,6},{8,9},{9,8},{10,11... | collective-permute-start | bytes 122888 | tf_op jit(solution)/shard_map/ppermute | solution.py:693
  15.8 2.0 %first.1 = (f32[5,32,2,56,128]{4,3,2,1,0:T(8,128)S(1)}, f32[33,2,56,128]{3,2,1,0:T(8,128)S(1)}, f32[32,2,56,128]{3,2,1,0:T(8,128)S(1)}, f32[32,2,56,128]{3,2,1,0...) custom-call(f32[2,32,2,8,128]{4,3,2,1,0:T(8,128)S(1)} %get-tuple-ele, ...), custom_call_target="tpu_custom_call", output_to_operand_aliasing={{0}: (1, {}), {1}: (2, {}), {2}: (3, {}), {3}: (4, {}), {4}... | custom-call | flops 10485760 | bytes 2097152 | tf_op jit(solution)/shard_map/first/pallas_call | solution.py:753
  17.8 0.0 collective-permute-done.2.far_ref
  17.8 0.0 collective-permute-done.3.near_ref
  17.8 6.1 %basis.1 = (f32[5,32,2,56,128]{4,3,2,1,0:T(8,128)S(1)}, f32[4,4,56,128]{3,2,1,0:T(8,128)S(1)}, f32[32,128]{1,0:T(8,128)S(1)}) custom-call(f32[2,40,128]{2,1,0:T(8,128)S(1)} %get-tuple-element.32.last_ref, f32[2,40,128]{2,1,0:T(8,128)S(1)} %get-tuple-element.33.first_ref, ...), custom_call_target="tpu_custom_call", output_to_operand_aliasing={{0}: (8, {})} | custom-call | tf_op jit(solution)/shard_map/basis/pallas_call | solution.py:763
  23.9 12.7 %all_to_all.11 = f32[32,1,128]{2,1,0:T(1,128)S(1)} all-to-all(f32[32,1,128]{2,1,0:T(1,128)S(1)} %bitcast.5), channel_id=1, replica_groups=mesh['gx'=4,'gy'=8] {'gx','gy'}, dimensions={0} | all-to-all | bytes 32768 | tf_op jit(solution)/shard_map/all_to_all | solution.py:779
  36.6 3.3 %finish.1 = (f32[1,32,32,256]{3,2,1,0:T(8,128)}, f32[1,32,32,256]{3,2,1,0:T(8,128)}, f32[1,32,32,256]{3,2,1,0:T(8,128)}, f32[1,32,32,256]{3,2,1,0:T(8,128)}) custom-call(f32[32,128]{1,0:T(8,128)S(1)} %bitcast.4, f32[5,32,2,56,128]{4,3,2,1,0:T(8,128)S(1)} %get-tuple-element.48.fields_ref, f32[32,2,56,128]{3,2,1,0:T(8,128)S(1)} %get-tuple-element.43.face_x_ref, ...), custom_call_target="tpu_custom_call" | custom-call | tf_op jit(solution)/shard_map/finish/pallas_call | solution.py:781
Async XLA Ops:
  1.9 8.6 %collective-permute-start = (f32[2,32,8,128]{3,2,1,0:T(8,128)S(1)}, f32[2,32,8,128]{3,2,1,0:T(8,128)S(1)}, u32[]{:S(2)}, u32[]{:S(2)}) collective-permute-start(f32[2,32,8,128]{3,2,1,0:T(8,128)S(1)} %far.1), channel_id=1, source_target_pairs={{8,16},{16,8},{9,17},{17,9},{10,18},{18,10},{11,19},{19,11},{12,20... | collective-permute-start | bytes 786440 | tf_op jit(solution)/shard_map/ppermute | solution.py:693
  4.2 6.3 %collective-permute-start.1 = (f32[2,32,8,128]{3,2,1,0:T(8,128)S(1)}, f32[2,32,8,128]{3,2,1,0:T(8,128)S(1)}, u32[]{:S(2)}, u32[]{:S(2)}) collective-permute-start(f32[2,32,8,128]{3,2,1,0:T(8,128)S(1)} %get-tuple-element.27), channel_id=1, source_target_pairs={{0,8},{8,0},{16,24},{24,16},{1,9},{9,1},{17,25},{25,17},{2,10},{10... | collective-permute-start | bytes 786440 | tf_op jit(solution)/shard_map/ppermute | solution.py:693
  10.8 7.0 %collective-permute-start.2 = (f32[2,40,128]{2,1,0:T(8,128)S(1)}, f32[2,40,128]{2,1,0:T(8,128)S(1)}, u32[]{:S(2)}, u32[]{:S(2)}) collective-permute-start(f32[2,40,128]{2,1,0:T(8,128)S(1)} %get-tuple-element.34), channel_id=1, source_target_pairs={{1,2},{2,1},{3,4},{4,3},{5,6},{6,5},{9,10},{10,9},{11,12},{12,11},... | collective-permute-start | bytes 122888 | tf_op jit(solution)/shard_map/ppermute | solution.py:693
  11.4 6.4 %collective-permute-start.3 = (f32[2,40,128]{2,1,0:T(8,128)S(1)}, f32[2,40,128]{2,1,0:T(8,128)S(1)}, u32[]{:S(2)}, u32[]{:S(2)}) collective-permute-start(f32[2,40,128]{2,1,0:T(8,128)S(1)} %get-tuple-element.35), channel_id=1, source_target_pairs={{0,1},{1,0},{2,3},{3,2},{4,5},{5,4},{6,7},{7,6},{8,9},{9,8},{10,11... | collective-permute-start | bytes 122888 | tf_op jit(solution)/shard_map/ppermute | solution.py:693

commit v4 on v3

--- a/solution.py
+++ b/solution.py
@@ -36,7 +36,7 @@
 
 
 def turn(value, shift):
-    return pltpu.roll(value, shift % LANES, 1)
+    return pltpu.roll(value, shift % LANES, 1) if shift % LANES else value
 
 
 def reciprocal(value):
@@ -503,19 +503,32 @@
     for number in range(2, DEPTH + 1):
         found += apply_power(number, fields_ref, face_x_ref, face_y_ref, face_z_ref, rims_ref)
     total = jnp.concatenate([jnp.sum(part, axis=0, keepdims=True) for part in found], axis=0)
-    share = LANES // SUB
-    step = LANES // 2
-    while step >= share:
-        total = total + turn(total, step)
-        step //= 2
-    total = jnp.sum(jnp.where(lanes // share == row_ids(), total, 0.0), axis=0, keepdims=True)
-    sums_ref[...] = jnp.broadcast_to(total, sums_ref.shape)
+    total = total.T
+    total, rest = pair_total([(total[k : k + SUB], None) for k in range(0, LANES, SUB)])
+    row = jnp.concatenate([total[0:1], rest[0:1], jnp.zeros((1, LANES - 4 * DEPTH), F32)], axis=1)
+    sums_ref[...] = jnp.broadcast_to(row, sums_ref.shape)
 
 
 def two_sum(first, second):
     total = first + second
     part = total - first
     return total, (first - (total - part)) + (second - part)
+
+
+def pair_total(terms):
+    while len(terms) > 1:
+        merged = []
+        for (high, low), (other, other_low) in zip(terms[::2], terms[1::2], strict=True):
+            total, lost = two_sum(high, other)
+            merged.append((total, lost if low is None else lost + (low + other_low)))
+        terms = merged
+    total, rest = terms[0]
+    step = SUB // 2
+    while step:
+        total, lost = two_sum(total, pltpu.roll(total, step, 0))
+        rest = rest + pltpu.roll(rest, step, 0) + lost
+        step //= 2
+    return total, rest
 
 
 def quick_sum(first, second):
@@ -602,17 +615,13 @@
     blocks = rows // SUB
     last_lane = lane_ids() == LANES - 1
 
-    total = jnp.sum(sums_ref[...], axis=0, keepdims=True)
-    total = jnp.where(lane_ids() // (LANES // SUB) == row_ids(), total, 0.0)
-    rest = jnp.zeros((SUB, LANES), F32)
-    step = 1
-    while step < LANES:
-        total, lost = two_sum(total, turn(total, step))
-        rest = rest + turn(rest, step) + lost
-        step *= 2
-    total, rest = quick_sum(total, rest)
-    coefs = galerkin([(total[k : k + 1], rest[k : k + 1]) for k in range(2 * DEPTH)])
-    coefs = [jnp.broadcast_to(value, (SUB, LANES)) for value in coefs]
+    peers = sums_ref.shape[0]
+    total, rest = pair_total([(sums_ref[k : k + SUB, :], None) for k in range(0, peers, SUB)])
+    total, rest = quick_sum(total, rest + turn(total, -2 * DEPTH))
+    moments = [
+        tuple(jnp.broadcast_to(value[:, k : k + 1], (SUB, LANES)) for value in (total, rest)) for k in range(2 * DEPTH)
+    ]
+    coefs = galerkin(moments)
 
     def at(block, step=0):
         return pl.ds(LO + block * SUB + step, SUB)

time: 40.2 us -> 39.7 us (0.988)
    pallas_call x1, Pallas kernels: 3.32 us -> 2.9 us  [on_device(): pl.pallas_call(finish_kernel, out_shape=(jax.ShapeDtypeStruct((1, *block)...]
where the time goes in v4:
time: 39.7 us; the launch traced here: 39.5 us
  Pallas kernels  16 us (40%)
  blocking collectives  12.7 us (32%)
  starting transfers between devices  10.1 us (25%)
  between operations  0.71 us (2%)
    all_to_all x1, blocking collectives, on_device(): sums = lax.all_to_all(sums, ('gx', 'gy'), 0, 0, tiled=True)  12.7 us
    ppermute x4, starting transfers between devices, exchange(): return lax.ppermute(value, axis, pairs)  10.1 us
    pallas_call x1, Pallas kernels, on_device(): pl.pallas_call(basis_kernel, out_shape=(powers[0], in_vmem(DEPTH, *inner)...  6.11 us
    pallas_call x1, Pallas kernels, on_device(): pl.pallas_call(finish_kernel, out_shape=(jax.ShapeDtypeStruct((1, *block)...  2.9 us
    pallas_call x1, Pallas kernels, on_device(): pl.pallas_call(first_kernel, out_shape=powers + (in_vmem(2, SUB, LANES),)...  1.97 us
    pallas_call x1, Pallas kernels, on_device(): pl.pallas_call(own_kernel, out_shape=powers + (in_vmem(*edges),) * 2, in_...  1.89 us
    pallas_call x1, Pallas kernels, on_device(): pl.pallas_call(load_kernel, out_shape=(in_vmem(*full), powers[0], in_vmem...  1.67 us
    pallas_call x1, Pallas kernels, on_device(): pl.pallas_call(far_kernel, out_shape=in_vmem(*ends), in_specs=[HBM_SPEC]...  1.22 us
  transfers between devices with their start and end apart: 4, of which 0 were waited for; matrix products, arithmetic and copies ran while one was open for 0% of the time, Pallas kernels for 14%

profile of v4, /device:TPU:0, one launch (start us, length us, event | category | flops | bytes accessed | tf_op | source)
XLA Modules:
  0.0 39.5 jit_solution(4710608481625190489)
XLA Ops:
  0.6 1.2 %far.1 = f32[2,32,8,128]{3,2,1,0:T(8,128)S(1)} custom-call(f32[1,32,32,256]{3,2,1,0:T(8,128)} %log_hbm.3, f32[1,32,32,256]{3,2,1,0:T(8,128)} %src_hbm.3), custom_call_target="tpu_custom_call" | custom-call | tf_op jit(solution)/shard_map/far/pallas_call | solution.py:720
  1.9 0.7 %collective-permute-start = (f32[2,32,8,128]{3,2,1,0:T(8,128)S(1)}, f32[2,32,8,128]{3,2,1,0:T(8,128)S(1)}, u32[]{:S(2)}, u32[]{:S(2)}) collective-permute-start(f32[2,32,8,128]{3,2,1,0:T(8,128)S(1)} %far.1), channel_id=1, source_target_pairs={{8,16},{16,8},{9,17},{17,9},{10,18},{18,10},{11,19},{19,11},{12,20... | collective-permute-start | bytes 786440 | tf_op jit(solution)/shard_map/ppermute | solution.py:702
  2.5 1.7 %load.1 = (f32[32,2,56,128]{3,2,1,0:T(8,128)S(1)}, f32[5,32,2,56,128]{4,3,2,1,0:T(8,128)S(1)}, f32[2,32,8,128]{3,2,1,0:T(8,128)S(1)}) custom-call(f32[1,32,32,256]{3,2,1,0:T(8,128)} %log_hbm.3, f32[1,32,32,256]{3,2,1,0:T(8,128)} %src_hbm.3), custom_call_target="tpu_custom_call" | custom-call | flops 262144 | bytes 2097152 | tf_op jit(solution)/shard_map/load/pallas_call | solution.py:730
  4.2 4.4 %collective-permute-start.1 = (f32[2,32,8,128]{3,2,1,0:T(8,128)S(1)}, f32[2,32,8,128]{3,2,1,0:T(8,128)S(1)}, u32[]{:S(2)}, u32[]{:S(2)}) collective-permute-start(f32[2,32,8,128]{3,2,1,0:T(8,128)S(1)} %get-tuple-element.27), channel_id=1, source_target_pairs={{0,8},{8,0},{16,24},{24,16},{1,9},{9,1},{17,25},{25,17},{2,10},{10... | collective-permute-start | bytes 786440 | tf_op jit(solution)/shard_map/ppermute | solution.py:702
  8.6 1.9 %own.1 = (f32[5,32,2,56,128]{4,3,2,1,0:T(8,128)S(1)}, f32[33,2,56,128]{3,2,1,0:T(8,128)S(1)}, f32[32,2,56,128]{3,2,1,0:T(8,128)S(1)}, f32[32,2,56,128]{3,2,1,0:T...) custom-call(f32[32,2,56,128]{3,2,1,0:T(8,128)S(1)} %get-tuple-elemen, ...), custom_call_target="tpu_custom_call", output_to_operand_aliasing={{0}: (1, {})} | custom-call | flops 15728640 | bytes 2097152 | tf_op jit(solution)/shard_map/own/pallas_call | solution.py:741
  10.5 0.0 collective-permute-done.far_in
  10.5 0.0 collective-permute-done.1.near_in
  10.5 0.2 edges.1
  10.8 0.7 %collective-permute-start.2 = (f32[2,40,128]{2,1,0:T(8,128)S(1)}, f32[2,40,128]{2,1,0:T(8,128)S(1)}, u32[]{:S(2)}, u32[]{:S(2)}) collective-permute-start(f32[2,40,128]{2,1,0:T(8,128)S(1)} %get-tuple-element.34), channel_id=1, source_target_pairs={{1,2},{2,1},{3,4},{4,3},{5,6},{6,5},{9,10},{10,9},{11,12},{12,11},... | collective-permute-start | bytes 122888 | tf_op jit(solution)/shard_map/ppermute | solution.py:702
  11.4 4.4 %collective-permute-start.3 = (f32[2,40,128]{2,1,0:T(8,128)S(1)}, f32[2,40,128]{2,1,0:T(8,128)S(1)}, u32[]{:S(2)}, u32[]{:S(2)}) collective-permute-start(f32[2,40,128]{2,1,0:T(8,128)S(1)} %get-tuple-element.35), channel_id=1, source_target_pairs={{0,1},{1,0},{2,3},{3,2},{4,5},{5,4},{6,7},{7,6},{8,9},{9,8},{10,11... | collective-permute-start | bytes 122888 | tf_op jit(solution)/shard_map/ppermute | solution.py:702
  15.8 2.0 %first.1 = (f32[5,32,2,56,128]{4,3,2,1,0:T(8,128)S(1)}, f32[33,2,56,128]{3,2,1,0:T(8,128)S(1)}, f32[32,2,56,128]{3,2,1,0:T(8,128)S(1)}, f32[32,2,56,128]{3,2,1,0...) custom-call(f32[2,32,2,8,128]{4,3,2,1,0:T(8,128)S(1)} %get-tuple-ele, ...), custom_call_target="tpu_custom_call", output_to_operand_aliasing={{0}: (1, {}), {1}: (2, {}), {2}: (3, {}), {3}: (4, {}), {4}... | custom-call | flops 10485760 | bytes 2097152 | tf_op jit(solution)/shard_map/first/pallas_call | solution.py:762
  17.8 0.0 collective-permute-done.2.far_ref
  17.8 0.0 collective-permute-done.3.near_ref
  17.8 6.1 %basis.1 = (f32[5,32,2,56,128]{4,3,2,1,0:T(8,128)S(1)}, f32[4,4,56,128]{3,2,1,0:T(8,128)S(1)}, f32[32,128]{1,0:T(8,128)S(1)}) custom-call(f32[2,40,128]{2,1,0:T(8,128)S(1)} %get-tuple-element.32.last_ref, f32[2,40,128]{2,1,0:T(8,128)S(1)} %get-tuple-element.33.first_ref, ...), custom_call_target="tpu_custom_call", output_to_operand_aliasing={{0}: (8, {})} | custom-call | tf_op jit(solution)/shard_map/basis/pallas_call | solution.py:772
  23.9 12.7 %all_to_all.11 = f32[32,1,128]{2,1,0:T(1,128)S(1)} all-to-all(f32[32,1,128]{2,1,0:T(1,128)S(1)} %bitcast.5), channel_id=1, replica_groups=mesh['gx'=4,'gy'=8] {'gx','gy'}, dimensions={0} | all-to-all | bytes 32768 | tf_op jit(solution)/shard_map/all_to_all | solution.py:788
  36.6 2.9 %finish.1 = (f32[1,32,32,256]{3,2,1,0:T(8,128)}, f32[1,32,32,256]{3,2,1,0:T(8,128)}, f32[1,32,32,256]{3,2,1,0:T(8,128)}, f32[1,32,32,256]{3,2,1,0:T(8,128)}) custom-call(f32[32,128]{1,0:T(8,128)S(1)} %bitcast.4, f32[5,32,2,56,128]{4,3,2,1,0:T(8,128)S(1)} %get-tuple-element.48.fields_ref, f32[32,2,56,128]{3,2,1,0:T(8,128)S(1)} %get-tuple-element.43.face_x_ref, ...), custom_call_target="tpu_custom_call" | custom-call | tf_op jit(solution)/shard_map/finish/pallas_call | solution.py:790
Async XLA Ops:
  1.9 8.6 %collective-permute-start = (f32[2,32,8,128]{3,2,1,0:T(8,128)S(1)}, f32[2,32,8,128]{3,2,1,0:T(8,128)S(1)}, u32[]{:S(2)}, u32[]{:S(2)}) collective-permute-start(f32[2,32,8,128]{3,2,1,0:T(8,128)S(1)} %far.1), channel_id=1, source_target_pairs={{8,16},{16,8},{9,17},{17,9},{10,18},{18,10},{11,19},{19,11},{12,20... | collective-permute-start | bytes 786440 | tf_op jit(solution)/shard_map/ppermute | solution.py:702
  4.2 6.3 %collective-permute-start.1 = (f32[2,32,8,128]{3,2,1,0:T(8,128)S(1)}, f32[2,32,8,128]{3,2,1,0:T(8,128)S(1)}, u32[]{:S(2)}, u32[]{:S(2)}) collective-permute-start(f32[2,32,8,128]{3,2,1,0:T(8,128)S(1)} %get-tuple-element.27), channel_id=1, source_target_pairs={{0,8},{8,0},{16,24},{24,16},{1,9},{9,1},{17,25},{25,17},{2,10},{10... | collective-permute-start | bytes 786440 | tf_op jit(solution)/shard_map/ppermute | solution.py:702
  10.8 7.0 %collective-permute-start.2 = (f32[2,40,128]{2,1,0:T(8,128)S(1)}, f32[2,40,128]{2,1,0:T(8,128)S(1)}, u32[]{:S(2)}, u32[]{:S(2)}) collective-permute-start(f32[2,40,128]{2,1,0:T(8,128)S(1)} %get-tuple-element.34), channel_id=1, source_target_pairs={{1,2},{2,1},{3,4},{4,3},{5,6},{6,5},{9,10},{10,9},{11,12},{12,11},... | collective-permute-start | bytes 122888 | tf_op jit(solution)/shard_map/ppermute | solution.py:702
  11.4 6.4 %collective-permute-start.3 = (f32[2,40,128]{2,1,0:T(8,128)S(1)}, f32[2,40,128]{2,1,0:T(8,128)S(1)}, u32[]{:S(2)}, u32[]{:S(2)}) collective-permute-start(f32[2,40,128]{2,1,0:T(8,128)S(1)} %get-tuple-element.35), channel_id=1, source_target_pairs={{0,1},{1,0},{2,3},{3,2},{4,5},{5,4},{6,7},{7,6},{8,9},{9,8},{10,11... | collective-permute-start | bytes 122888 | tf_op jit(solution)/shard_map/ppermute | solution.py:702

commit v5 on v4

--- a/solution.py
+++ b/solution.py
@@ -13,6 +13,7 @@
 LO = 8
 GROUP = 4 * DEPTH
 HALO_LAYERS = 16
+SPARE = 3
 F32 = jnp.float32
 HBM_SPEC = pl.BlockSpec(memory_space=pltpu.HBM)
 VMEM_SPEC = pl.BlockSpec(memory_space=pltpu.VMEM)
@@ -104,6 +105,20 @@
     return total
 
 
+def put_column_faces(face_y_ref, face_w_ref, layer, place, values):
+    lanes = lane_ids()
+    first_lane, last_lane = lanes == 0, lanes == LANES - 1
+    tiles = len(values)
+    moved = [turn(value, -1) for value in values]
+    others = [jnp.where(last_lane, moved[tile + 1], moved[tile]) for tile in range(tiles - 1)] + [moved[-1]]
+    faces = [reciprocal(value + other) for value, other in zip(values, others, strict=True)]
+    faces[-1] = jnp.where(last_lane, 0.0, faces[-1])
+    moved = [jnp.zeros((SUB, LANES), F32)] + [turn(face, 1) for face in faces]
+    for tile in range(tiles):
+        face_y_ref[layer, tile, place, :] = faces[tile]
+        face_w_ref[layer, tile, place, :] = jnp.where(first_lane, moved[tile], moved[tile + 1])
+
+
 def own_kernel(
     log_ref,
     fields_in,
@@ -112,6 +127,7 @@
     face_x_ref,
     face_y_ref,
     face_z_ref,
+    face_w_ref,
     last_ref,
     first_ref,
 ):
@@ -121,7 +137,6 @@
     blocks = rows // SUB
     slots = layers // (LANES // GROUP)
     ring = LO + rows + SUB
-    last_lane = lane_ids() == LANES - 1
     base_ref = fields_ref.at[0]
 
     def at(block, step=0):
@@ -147,13 +162,8 @@
     def faces(layer, _):
         for block in range(blocks):
             values = [inverse_ref[layer, tile, at(block), :] for tile in range(tiles)]
-            moved = [turn(value, -1) for value in values]
+            put_column_faces(face_y_ref, face_w_ref, layer, at(block), values)
             for tile in range(tiles):
-                other = moved[tile]
-                if tile < tiles - 1:
-                    other = jnp.where(last_lane, moved[tile + 1], other)
-                face = reciprocal(values[tile] + other)
-                face_y_ref[layer, tile, at(block), :] = face if tile < tiles - 1 else jnp.where(last_lane, 0.0, face)
                 face_x_ref[layer, tile, at(block), :] = reciprocal(
                     values[tile] + inverse_ref[layer, tile, at(block, 1), :]
                 )
@@ -242,7 +252,7 @@
     return inside_rows, inside_cols
 
 
-def apply_power(number, fields_ref, face_x_ref, face_y_ref, face_z_ref, rims_ref):
+def apply_power(number, fields_ref, face_x_ref, face_y_ref, face_z_ref, face_w_ref, rims_ref):
     _, layers, tiles, height, _ = fields_ref.shape
     blocks = (height - 3 * SUB) // SUB
     slots = layers // (LANES // GROUP)
@@ -272,24 +282,24 @@
         for step in range(count):
             layer = start + step
             values = levels[step + 1]
-            moved = [turn(value, -1) for value in values]
-            flux = []
-            for tile in range(tiles):
-                other = moved[tile]
-                if tile < tiles - 1:
-                    other = jnp.where(last_lane, moved[tile + 1], other)
-                flux.append(face_y_ref[layer, tile, at(block), :] * (values[tile] - other))
+            ahead = [turn(value, -1) for value in values]
+            behind = [turn(value, 1) for value in values]
             rim = None
             if rims_ref is not None:
                 rim = rim_of(rims_ref[number - 1, step % slots, at(block), :], start // slots + step // slots)
-            moved = [turn(value, 1) for value in flux]
-            moved = [moved[-1] if rim is None else rim] + moved
+            out, back = [], []
+            for tile in range(tiles):
+                other = ahead[tile] if tile == tiles - 1 else jnp.where(last_lane, ahead[tile + 1], ahead[tile])
+                out.append(face_y_ref[layer, tile, at(block), :] * (values[tile] - other))
+                other = behind[tile] if tile == 0 else jnp.where(first_lane, behind[tile - 1], behind[tile])
+                back.append(face_w_ref[layer, tile, at(block), :] * (other - values[tile]))
             if rim is not None:
-                flux[-1] = jnp.where(last_lane, rim, flux[-1])
+                out[-1] = jnp.where(last_lane, rim, out[-1])
+                back[0] = jnp.where(first_lane, rim, back[0])
             for tile in range(tiles):
                 value = values[tile]
                 result = (
-                    (flux[tile] - jnp.where(first_lane, moved[tile], moved[tile + 1]))
+                    (out[tile] - back[tile])
                     + x_part(face_x_ref, (layer, tile), old, (layer, tile), block, value)
                     + (ups[step + 1][tile] - ups[step][tile])
                 )
@@ -327,18 +337,19 @@
     face_x_in,
     face_y_in,
     face_z_in,
+    face_w_in,
     fields_ref,
     inverse_ref,
     face_x_ref,
     face_y_ref,
     face_z_ref,
+    face_w_ref,
     parts_ref,
 ):
-    del fields_in, inverse_in, face_x_in, face_y_in, face_z_in
+    del fields_in, inverse_in, face_x_in, face_y_in, face_z_in, face_w_in
     _, layers, tiles, height, _ = fields_ref.shape
     blocks = (height - 3 * SUB) // SUB
     slots = layers // (LANES // GROUP)
-    last_lane = lane_ids() == LANES - 1
     at = place_of
 
     def fill(layer, _):
@@ -353,13 +364,8 @@
 
     def faces(layer, _):
         values = [inverse_ref[layer, tile, at(blocks), :] for tile in range(tiles)]
-        moved = [turn(value, -1) for value in values]
+        put_column_faces(face_y_ref, face_w_ref, layer, at(blocks), values)
         for tile in range(tiles):
-            other = moved[tile]
-            if tile < tiles - 1:
-                other = jnp.where(last_lane, moved[tile + 1], other)
-            face = reciprocal(values[tile] + other)
-            face_y_ref[layer, tile, at(blocks), :] = face if tile < tiles - 1 else jnp.where(last_lane, 0.0, face)
             for block in (blocks - 1, blocks):
                 face = reciprocal(
                     inverse_ref[layer, tile, at(block), :] + inverse_ref[layer, tile, at(block, 1), :]
@@ -371,7 +377,7 @@
         return 0
 
     lax.fori_loop(0, layers, faces, 0, unroll=2 * slots)
-    found = apply_power(1, fields_ref, face_x_ref, face_y_ref, face_z_ref, None)
+    found = apply_power(1, fields_ref, face_x_ref, face_y_ref, face_z_ref, face_w_ref, None)
     for which, part in enumerate(found):
         parts_ref[which] = part
 
@@ -385,6 +391,7 @@
     face_x_ref,
     face_y_ref,
     face_z_ref,
+    face_w_ref,
     fields_in,
     fields_ref,
     rims_ref,
@@ -501,7 +508,7 @@
 
     found = [parts_ref[0], parts_ref[1] + lost]
     for number in range(2, DEPTH + 1):
-        found += apply_power(number, fields_ref, face_x_ref, face_y_ref, face_z_ref, rims_ref)
+        found += apply_power(number, fields_ref, face_x_ref, face_y_ref, face_z_ref, face_w_ref, rims_ref)
     total = jnp.concatenate([jnp.sum(part, axis=0, keepdims=True) for part in found], axis=0)
     total = total.T
     total, rest = pair_total([(total[k : k + SUB], None) for k in range(0, LANES, SUB)])
@@ -708,6 +715,7 @@
     height = rows + 3 * SUB
     full = (layers, tiles, height, LANES)
     deep = (layers + 1, tiles, height, LANES)
+    spare = (layers + SPARE, tiles, height, LANES)
     ends = (2, layers, tiles * DEPTH, LANES)
     edges = (2, rows + SUB, LANES)
     strip = (slots + 2, height, LANES)
@@ -716,7 +724,7 @@
     cells = layers * rows * cols
 
     log_perm, source = (pltpu.with_memory_space_constraint(value, pltpu.HBM) for value in (log_perm, source))
-    powers = (in_vmem(DEPTH + 1, *full), in_vmem(*deep)) + (in_vmem(*full),) * 2 + (in_vmem(*deep),)
+    powers = (in_vmem(DEPTH + 1, *full), in_vmem(*spare)) + (in_vmem(*full),) * 2 + (in_vmem(*deep), in_vmem(*full))
     far = pl.pallas_call(
         far_kernel,
         out_shape=in_vmem(*ends),
@@ -742,7 +750,7 @@
         own_kernel,
         out_shape=powers + (in_vmem(*edges),) * 2,
         in_specs=[VMEM_SPEC] * 2,
-        out_specs=[VMEM_SPEC] * 7,
+        out_specs=[VMEM_SPEC] * 8,
         input_output_aliases={1: 0},
         compiler_params=params(16),
         cost_estimate=pl.CostEstimate(flops=60 * cells, bytes_accessed=8 * cells, transcendentals=4 * cells),
@@ -759,12 +767,12 @@
     )(far, near, last, first)
     far = exchange(far, "gy", False)
     near = exchange(near, "gy", True)
-    fields, _, face_x, face_y, face_z, parts = pl.pallas_call(
+    fields, _, face_x, face_y, face_z, face_w, parts = pl.pallas_call(
         first_kernel,
         out_shape=powers + (in_vmem(2, SUB, LANES),),
-        in_specs=[VMEM_SPEC] * 6,
-        out_specs=[VMEM_SPEC] * 6,
-        input_output_aliases={1: 0, 2: 1, 3: 2, 4: 3, 5: 4},
+        in_specs=[VMEM_SPEC] * 7,
+        out_specs=[VMEM_SPEC] * 7,
+        input_output_aliases={1: 0, 2: 1, 3: 2, 4: 3, 5: 4, 6: 5},
         compiler_params=params(16),
         cost_estimate=pl.CostEstimate(flops=40 * cells, bytes_accessed=8 * cells, transcendentals=cells),
         name="first",
@@ -772,9 +780,9 @@
     fields, rims, sums = pl.pallas_call(
         basis_kernel,
         out_shape=(powers[0], in_vmem(DEPTH, *inner), in_vmem(peers, LANES)),
-        in_specs=[VMEM_SPEC] * 9,
+        in_specs=[VMEM_SPEC] * 10,
         out_specs=[VMEM_SPEC] * 3,
-        input_output_aliases={8: 0},
+        input_output_aliases={9: 0},
         scratch_shapes=[
             in_vmem(DEPTH, *strip),
             in_vmem(*strip),
@@ -784,7 +792,7 @@
         ],
         compiler_params=params(16),
         name="basis",
-    )(last, first, far, near, parts, face_x, face_y, face_z, fields)
+    )(last, first, far, near, parts, face_x, face_y, face_z, face_w, fields)
     sums = lax.all_to_all(sums, ("gx", "gy"), 0, 0, tiled=True)
     block = (layers, rows, cols)
     return pl.pallas_call(

time: 39.7 us -> 38.9 us (0.980)
  blocking collectives: 12.7 us -> 12.2 us
    pallas_call x1, Pallas kernels: 6.11 us -> 5.27 us  [on_device(): pl.pallas_call(basis_kernel, out_shape=(powers[0], in_vmem(DEPTH, *inner)...]
    pallas_call x1, Pallas kernels: 1.89 us -> 2.46 us  [on_device(): pl.pallas_call(own_kernel, out_shape=powers + (in_vmem(*edges),) * 2, in_...]
    all_to_all x1, blocking collectives: 12.7 us -> 12.2 us  [on_device(): sums = lax.all_to_all(sums, ('gx', 'gy'), 0, 0, tiled=True)]
  transfers between devices with their start and end apart: 4 -> 4, of which waited for: 0 -> 0; matrix products, arithmetic and copies ran while one was open for 0% -> 0% of each run, Pallas kernels for 14% -> 16%
where the time goes in v5:
time: 38.9 us; the launch traced here: 38.7 us
  Pallas kernels  15.8 us (41%)
  blocking collectives  12.2 us (31%)
  starting transfers between devices  10.1 us (26%)
  between operations  0.71 us (2%)
    all_to_all x1, blocking collectives, on_device(): sums = lax.all_to_all(sums, ('gx', 'gy'), 0, 0, tiled=True)  12.2 us
    ppermute x4, starting transfers between devices, exchange(): return lax.ppermute(value, axis, pairs)  10.1 us
    pallas_call x1, Pallas kernels, on_device(): pl.pallas_call(basis_kernel, out_shape=(powers[0], in_vmem(DEPTH, *inner)...  5.27 us
    pallas_call x1, Pallas kernels, on_device(): pl.pallas_call(finish_kernel, out_shape=(jax.ShapeDtypeStruct((1, *block)...  2.92 us
    pallas_call x1, Pallas kernels, on_device(): pl.pallas_call(own_kernel, out_shape=powers + (in_vmem(*edges),) * 2, in_...  2.46 us
    pallas_call x1, Pallas kernels, on_device(): pl.pallas_call(first_kernel, out_shape=powers + (in_vmem(2, SUB, LANES),)...  1.97 us
    pallas_call x1, Pallas kernels, on_device(): pl.pallas_call(load_kernel, out_shape=(in_vmem(*full), powers[0], in_vmem...  1.67 us
    pallas_call x1, Pallas kernels, on_device(): pl.pallas_call(far_kernel, out_shape=in_vmem(*ends), in_specs=[HBM_SPEC]...  1.22 us
  transfers between devices with their start and end apart: 4, of which 0 were waited for; matrix products, arithmetic and copies ran while one was open for 0% of the time, Pallas kernels for 16%

profile of v5, /device:TPU:0, one launch (start us, length us, event | category | flops | bytes accessed | tf_op | source)
XLA Modules:
  0.0 38.7 jit_solution(746327837972860033)
XLA Ops:
  0.6 1.2 %far.1 = f32[2,32,8,128]{3,2,1,0:T(8,128)S(1)} custom-call(f32[1,32,32,256]{3,2,1,0:T(8,128)} %log_hbm.3, f32[1,32,32,256]{3,2,1,0:T(8,128)} %src_hbm.3), custom_call_target="tpu_custom_call" | custom-call | tf_op jit(solution)/shard_map/far/pallas_call | solution.py:728
  1.9 0.7 %collective-permute-start = (f32[2,32,8,128]{3,2,1,0:T(8,128)S(1)}, f32[2,32,8,128]{3,2,1,0:T(8,128)S(1)}, u32[]{:S(2)}, u32[]{:S(2)}) collective-permute-start(f32[2,32,8,128]{3,2,1,0:T(8,128)S(1)} %far.1), channel_id=1, source_target_pairs={{8,16},{16,8},{9,17},{17,9},{10,18},{18,10},{11,19},{19,11},{12,20... | collective-permute-start | bytes 786440 | tf_op jit(solution)/shard_map/ppermute | solution.py:709
  2.5 1.7 %load.1 = (f32[32,2,56,128]{3,2,1,0:T(8,128)S(1)}, f32[5,32,2,56,128]{4,3,2,1,0:T(8,128)S(1)}, f32[2,32,8,128]{3,2,1,0:T(8,128)S(1)}) custom-call(f32[1,32,32,256]{3,2,1,0:T(8,128)} %log_hbm.3, f32[1,32,32,256]{3,2,1,0:T(8,128)} %src_hbm.3), custom_call_target="tpu_custom_call" | custom-call | flops 262144 | bytes 2097152 | tf_op jit(solution)/shard_map/load/pallas_call | solution.py:738
  4.2 4.4 %collective-permute-start.1 = (f32[2,32,8,128]{3,2,1,0:T(8,128)S(1)}, f32[2,32,8,128]{3,2,1,0:T(8,128)S(1)}, u32[]{:S(2)}, u32[]{:S(2)}) collective-permute-start(f32[2,32,8,128]{3,2,1,0:T(8,128)S(1)} %get-tuple-element.29), channel_id=1, source_target_pairs={{0,8},{8,0},{16,24},{24,16},{1,9},{9,1},{17,25},{25,17},{2,10},{10... | collective-permute-start | bytes 786440 | tf_op jit(solution)/shard_map/ppermute | solution.py:709
  8.6 2.5 %own.1 = (f32[5,32,2,56,128]{4,3,2,1,0:T(8,128)S(1)}, f32[35,2,56,128]{3,2,1,0:T(8,128)S(1)}, f32[32,2,56,128]{3,2,1,0:T(8,128)S(1)}, f32[32,2,56,128]{3,2,1,0:T...) custom-call(f32[32,2,56,128]{3,2,1,0:T(8,128)S(1)} %get-tuple-elemen, ...), custom_call_target="tpu_custom_call", output_to_operand_aliasing={{0}: (1, {})} | custom-call | flops 15728640 | bytes 2097152 | tf_op jit(solution)/shard_map/own/pallas_call | solution.py:749
  11.1 0.0 collective-permute-done.far_in
  11.1 0.0 collective-permute-done.1.near_in
  11.1 0.2 edges.1
  11.3 0.7 %collective-permute-start.2 = (f32[2,40,128]{2,1,0:T(8,128)S(1)}, f32[2,40,128]{2,1,0:T(8,128)S(1)}, u32[]{:S(2)}, u32[]{:S(2)}) collective-permute-start(f32[2,40,128]{2,1,0:T(8,128)S(1)} %get-tuple-element.36), channel_id=1, source_target_pairs={{1,2},{2,1},{3,4},{4,3},{5,6},{6,5},{9,10},{10,9},{11,12},{12,11},... | collective-permute-start | bytes 122888 | tf_op jit(solution)/shard_map/ppermute | solution.py:709
  12.0 4.3 %collective-permute-start.3 = (f32[2,40,128]{2,1,0:T(8,128)S(1)}, f32[2,40,128]{2,1,0:T(8,128)S(1)}, u32[]{:S(2)}, u32[]{:S(2)}) collective-permute-start(f32[2,40,128]{2,1,0:T(8,128)S(1)} %get-tuple-element.37), channel_id=1, source_target_pairs={{0,1},{1,0},{2,3},{3,2},{4,5},{5,4},{6,7},{7,6},{8,9},{9,8},{10,11... | collective-permute-start | bytes 122888 | tf_op jit(solution)/shard_map/ppermute | solution.py:709
  16.4 2.0 %first.1 = (f32[5,32,2,56,128]{4,3,2,1,0:T(8,128)S(1)}, f32[35,2,56,128]{3,2,1,0:T(8,128)S(1)}, f32[32,2,56,128]{3,2,1,0:T(8,128)S(1)}, f32[32,2,56,128]{3,2,1,0...) custom-call(f32[2,32,2,8,128]{4,3,2,1,0:T(8,128)S(1)} %get-tuple-ele, ...), custom_call_target="tpu_custom_call", output_to_operand_aliasing={{0}: (1, {}), {1}: (2, {}), {2}: (3, {}), {3}: (4, {}), {4}... | custom-call | flops 10485760 | bytes 2097152 | tf_op jit(solution)/shard_map/first/pallas_call | solution.py:770
  18.3 0.0 collective-permute-done.2.far_ref
  18.3 0.0 collective-permute-done.3.near_ref
  18.4 5.3 %basis.1 = (f32[5,32,2,56,128]{4,3,2,1,0:T(8,128)S(1)}, f32[4,4,56,128]{3,2,1,0:T(8,128)S(1)}, f32[32,128]{1,0:T(8,128)S(1)}) custom-call(f32[2,40,128]{2,1,0:T(8,128)S(1)} %get-tuple-element.34.last_ref, f32[2,40,128]{2,1,0:T(8,128)S(1)} %get-tuple-element.35.first_ref, ...), custom_call_target="tpu_custom_call", output_to_operand_aliasing={{0}: (9, {})} | custom-call | tf_op jit(solution)/shard_map/basis/pallas_call | solution.py:780
  23.6 12.2 %all_to_all.11 = f32[32,1,128]{2,1,0:T(1,128)S(1)} all-to-all(f32[32,1,128]{2,1,0:T(1,128)S(1)} %bitcast.5), channel_id=1, replica_groups=mesh['gx'=4,'gy'=8] {'gx','gy'}, dimensions={0} | all-to-all | bytes 32768 | tf_op jit(solution)/shard_map/all_to_all | solution.py:796
  35.8 2.9 %finish.1 = (f32[1,32,32,256]{3,2,1,0:T(8,128)}, f32[1,32,32,256]{3,2,1,0:T(8,128)}, f32[1,32,32,256]{3,2,1,0:T(8,128)}, f32[1,32,32,256]{3,2,1,0:T(8,128)}) custom-call(f32[32,128]{1,0:T(8,128)S(1)} %bitcast.4, f32[5,32,2,56,128]{4,3,2,1,0:T(8,128)S(1)} %get-tuple-element.52.fields_ref, f32[32,2,56,128]{3,2,1,0:T(8,128)S(1)} %get-tuple-element.46.face_x_ref, ...), custom_call_target="tpu_custom_call" | custom-call | tf_op jit(solution)/shard_map/finish/pallas_call | solution.py:798
Async XLA Ops:
  1.9 9.2 %collective-permute-start = (f32[2,32,8,128]{3,2,1,0:T(8,128)S(1)}, f32[2,32,8,128]{3,2,1,0:T(8,128)S(1)}, u32[]{:S(2)}, u32[]{:S(2)}) collective-permute-start(f32[2,32,8,128]{3,2,1,0:T(8,128)S(1)} %far.1), channel_id=1, source_target_pairs={{8,16},{16,8},{9,17},{17,9},{10,18},{18,10},{11,19},{19,11},{12,20... | collective-permute-start | bytes 786440 | tf_op jit(solution)/shard_map/ppermute | solution.py:709
  4.2 6.9 %collective-permute-start.1 = (f32[2,32,8,128]{3,2,1,0:T(8,128)S(1)}, f32[2,32,8,128]{3,2,1,0:T(8,128)S(1)}, u32[]{:S(2)}, u32[]{:S(2)}) collective-permute-start(f32[2,32,8,128]{3,2,1,0:T(8,128)S(1)} %get-tuple-element.29), channel_id=1, source_target_pairs={{0,8},{8,0},{16,24},{24,16},{1,9},{9,1},{17,25},{25,17},{2,10},{10... | collective-permute-start | bytes 786440 | tf_op jit(solution)/shard_map/ppermute | solution.py:709
  11.3 7.0 %collective-permute-start.2 = (f32[2,40,128]{2,1,0:T(8,128)S(1)}, f32[2,40,128]{2,1,0:T(8,128)S(1)}, u32[]{:S(2)}, u32[]{:S(2)}) collective-permute-start(f32[2,40,128]{2,1,0:T(8,128)S(1)} %get-tuple-element.36), channel_id=1, source_target_pairs={{1,2},{2,1},{3,4},{4,3},{5,6},{6,5},{9,10},{10,9},{11,12},{12,11},... | collective-permute-start | bytes 122888 | tf_op jit(solution)/shard_map/ppermute | solution.py:709
  12.0 6.3 %collective-permute-start.3 = (f32[2,40,128]{2,1,0:T(8,128)S(1)}, f32[2,40,128]{2,1,0:T(8,128)S(1)}, u32[]{:S(2)}, u32[]{:S(2)}) collective-permute-start(f32[2,40,128]{2,1,0:T(8,128)S(1)} %get-tuple-element.37), channel_id=1, source_target_pairs={{0,1},{1,0},{2,3},{3,2},{4,5},{5,4},{6,7},{7,6},{8,9},{9,8},{10,11... | collective-permute-start | bytes 122888 | tf_op jit(solution)/shard_map/ppermute | solution.py:709

commit v6 on v5

--- a/solution.py
+++ b/solution.py
@@ -12,7 +12,7 @@
 SUB = 8
 LO = 8
 GROUP = 4 * DEPTH
-HALO_LAYERS = 16
+CHUNK = 8
 SPARE = 3
 F32 = jnp.float32
 HBM_SPEC = pl.BlockSpec(memory_space=pltpu.HBM)
@@ -256,7 +256,6 @@
     _, layers, tiles, height, _ = fields_ref.shape
     blocks = (height - 3 * SUB) // SUB
     slots = layers // (LANES // GROUP)
-    groups = layers // slots
     old, new = fields_ref.at[number - 1], fields_ref.at[number]
     lanes = lane_ids()
     first_lane, last_lane = lanes == 0, lanes == LANES - 1
@@ -313,20 +312,16 @@
     def chunk(group, sums):
         own_sums, next_sums = list(sums[0]), list(sums[1])
         for block in range(blocks):
-            for tile, value, result in layer_range(group * slots, slots, block):
+            for tile, value, result in layer_range(group * CHUNK, CHUNK, block):
                 own_sums[tile] = own_sums[tile] + value * value
                 next_sums[tile] = next_sums[tile] + value * result
         return tuple(own_sums), tuple(next_sums)
 
-    def halo_chunk(part, _):
-        for _ in layer_range(part * HALO_LAYERS, HALO_LAYERS, blocks):
+    start = (jnp.zeros((SUB, LANES), F32),) * tiles
+    sums = lax.fori_loop(0, layers // CHUNK, chunk, (start, start))
+    if number < DEPTH:
+        for _ in layer_range(0, layers, blocks):
             pass
-        return 0
-
-    start = (jnp.zeros((SUB, LANES), F32),) * tiles
-    sums = lax.fori_loop(0, groups, chunk, (start, start), unroll=2)
-    if number < DEPTH:
-        lax.fori_loop(0, layers // HALO_LAYERS, halo_chunk, 0)
     return [functools.reduce(jnp.add, parts) for parts in sums]
 
 

time: 38.9 us -> 38.7 us (level)
  Pallas kernels: 15.8 us -> 15.4 us
  transfers between devices with their start and end apart: 4 -> 4, of which waited for: 0 -> 1; matrix products, arithmetic and copies ran while one was open for 0% -> 0% of each run, Pallas kernels for 16% -> 16%
where the time goes in v6:
time: 38.7 us; the launch traced here: 38.5 us
  Pallas kernels  15.4 us (40%)
  blocking collectives  12.2 us (32%)
  starting transfers between devices  10.1 us (26%)
  between operations  0.7 us (2%)
    all_to_all x1, blocking collectives, on_device(): sums = lax.all_to_all(sums, ('gx', 'gy'), 0, 0, tiled=True)  12.2 us
    ppermute x4, starting transfers between devices, exchange(): return lax.ppermute(value, axis, pairs)  10.1 us
    pallas_call x1, Pallas kernels, on_device(): pl.pallas_call(basis_kernel, out_shape=(powers[0], in_vmem(DEPTH, *inner)...  5.04 us
    pallas_call x1, Pallas kernels, on_device(): pl.pallas_call(finish_kernel, out_shape=(jax.ShapeDtypeStruct((1, *block)...  2.92 us
    pallas_call x1, Pallas kernels, on_device(): pl.pallas_call(own_kernel, out_shape=powers + (in_vmem(*edges),) * 2, in_...  2.46 us
    pallas_call x1, Pallas kernels, on_device(): pl.pallas_call(first_kernel, out_shape=powers + (in_vmem(2, SUB, LANES),)...  1.88 us
    pallas_call x1, Pallas kernels, on_device(): pl.pallas_call(load_kernel, out_shape=(in_vmem(*full), powers[0], in_vmem...  1.67 us
    pallas_call x1, Pallas kernels, on_device(): pl.pallas_call(far_kernel, out_shape=in_vmem(*ends), in_specs=[HBM_SPEC]...  1.22 us
  transfers between devices with their start and end apart: 4, of which 1 were waited for; matrix products, arithmetic and copies ran while one was open for 0% of the time, Pallas kernels for 16%

profile of v6, /device:TPU:0, one launch (start us, length us, event | category | flops | bytes accessed | tf_op | source)
XLA Modules:
  0.0 38.5 jit_solution(14192143326956165380)
XLA Ops:
  0.6 1.2 %far.1 = f32[2,32,8,128]{3,2,1,0:T(8,128)S(1)} custom-call(f32[1,32,32,256]{3,2,1,0:T(8,128)} %log_hbm.3, f32[1,32,32,256]{3,2,1,0:T(8,128)} %src_hbm.3), custom_call_target="tpu_custom_call" | custom-call | tf_op jit(solution)/shard_map/far/pallas_call | solution.py:723
  1.9 0.7 %collective-permute-start = (f32[2,32,8,128]{3,2,1,0:T(8,128)S(1)}, f32[2,32,8,128]{3,2,1,0:T(8,128)S(1)}, u32[]{:S(2)}, u32[]{:S(2)}) collective-permute-start(f32[2,32,8,128]{3,2,1,0:T(8,128)S(1)} %far.1), channel_id=1, source_target_pairs={{8,16},{16,8},{9,17},{17,9},{10,18},{18,10},{11,19},{19,11},{12,20... | collective-permute-start | bytes 786440 | tf_op jit(solution)/shard_map/ppermute | solution.py:704
  2.5 1.7 %load.1 = (f32[32,2,56,128]{3,2,1,0:T(8,128)S(1)}, f32[5,32,2,56,128]{4,3,2,1,0:T(8,128)S(1)}, f32[2,32,8,128]{3,2,1,0:T(8,128)S(1)}) custom-call(f32[1,32,32,256]{3,2,1,0:T(8,128)} %log_hbm.3, f32[1,32,32,256]{3,2,1,0:T(8,128)} %src_hbm.3), custom_call_target="tpu_custom_call" | custom-call | flops 262144 | bytes 2097152 | tf_op jit(solution)/shard_map/load/pallas_call | solution.py:733
  4.2 4.4 %collective-permute-start.1 = (f32[2,32,8,128]{3,2,1,0:T(8,128)S(1)}, f32[2,32,8,128]{3,2,1,0:T(8,128)S(1)}, u32[]{:S(2)}, u32[]{:S(2)}) collective-permute-start(f32[2,32,8,128]{3,2,1,0:T(8,128)S(1)} %get-tuple-element.29), channel_id=1, source_target_pairs={{0,8},{8,0},{16,24},{24,16},{1,9},{9,1},{17,25},{25,17},{2,10},{10... | collective-permute-start | bytes 786440 | tf_op jit(solution)/shard_map/ppermute | solution.py:704
  8.6 2.5 %own.1 = (f32[5,32,2,56,128]{4,3,2,1,0:T(8,128)S(1)}, f32[35,2,56,128]{3,2,1,0:T(8,128)S(1)}, f32[32,2,56,128]{3,2,1,0:T(8,128)S(1)}, f32[32,2,56,128]{3,2,1,0:T...) custom-call(f32[32,2,56,128]{3,2,1,0:T(8,128)S(1)} %get-tuple-elemen, ...), custom_call_target="tpu_custom_call", output_to_operand_aliasing={{0}: (1, {})} | custom-call | flops 15728640 | bytes 2097152 | tf_op jit(solution)/shard_map/own/pallas_call | solution.py:744
  11.1 0.0 collective-permute-done.far_in
  11.1 0.0 collective-permute-done.1.near_in
  11.1 0.2 edges.1
  11.3 0.7 %collective-permute-start.2 = (f32[2,40,128]{2,1,0:T(8,128)S(1)}, f32[2,40,128]{2,1,0:T(8,128)S(1)}, u32[]{:S(2)}, u32[]{:S(2)}) collective-permute-start(f32[2,40,128]{2,1,0:T(8,128)S(1)} %get-tuple-element.36), channel_id=1, source_target_pairs={{1,2},{2,1},{3,4},{4,3},{5,6},{6,5},{9,10},{10,9},{11,12},{12,11},... | collective-permute-start | bytes 122888 | tf_op jit(solution)/shard_map/ppermute | solution.py:704
  12.0 4.3 %collective-permute-start.3 = (f32[2,40,128]{2,1,0:T(8,128)S(1)}, f32[2,40,128]{2,1,0:T(8,128)S(1)}, u32[]{:S(2)}, u32[]{:S(2)}) collective-permute-start(f32[2,40,128]{2,1,0:T(8,128)S(1)} %get-tuple-element.37), channel_id=1, source_target_pairs={{0,1},{1,0},{2,3},{3,2},{4,5},{5,4},{6,7},{7,6},{8,9},{9,8},{10,11... | collective-permute-start | bytes 122888 | tf_op jit(solution)/shard_map/ppermute | solution.py:704
  16.4 1.9 %first.1 = (f32[5,32,2,56,128]{4,3,2,1,0:T(8,128)S(1)}, f32[35,2,56,128]{3,2,1,0:T(8,128)S(1)}, f32[32,2,56,128]{3,2,1,0:T(8,128)S(1)}, f32[32,2,56,128]{3,2,1,0...) custom-call(f32[2,32,2,8,128]{4,3,2,1,0:T(8,128)S(1)} %get-tuple-ele, ...), custom_call_target="tpu_custom_call", output_to_operand_aliasing={{0}: (1, {}), {1}: (2, {}), {2}: (3, {}), {3}: (4, {}), {4}... | custom-call | flops 10485760 | bytes 2097152 | tf_op jit(solution)/shard_map/first/pallas_call | solution.py:765
  18.2 0.0 collective-permute-done.2.far_ref
  18.3 0.1 collective-permute-done.3.near_ref
  18.3 5.0 %basis.1 = (f32[5,32,2,56,128]{4,3,2,1,0:T(8,128)S(1)}, f32[4,4,56,128]{3,2,1,0:T(8,128)S(1)}, f32[32,128]{1,0:T(8,128)S(1)}) custom-call(f32[2,40,128]{2,1,0:T(8,128)S(1)} %get-tuple-element.34.last_ref, f32[2,40,128]{2,1,0:T(8,128)S(1)} %get-tuple-element.35.first_ref, ...), custom_call_target="tpu_custom_call", output_to_operand_aliasing={{0}: (9, {})} | custom-call | tf_op jit(solution)/shard_map/basis/pallas_call | solution.py:775
  23.4 12.2 %all_to_all.11 = f32[32,1,128]{2,1,0:T(1,128)S(1)} all-to-all(f32[32,1,128]{2,1,0:T(1,128)S(1)} %bitcast.5), channel_id=1, replica_groups=mesh['gx'=4,'gy'=8] {'gx','gy'}, dimensions={0} | all-to-all | bytes 32768 | tf_op jit(solution)/shard_map/all_to_all | solution.py:791
  35.6 2.9 %finish.1 = (f32[1,32,32,256]{3,2,1,0:T(8,128)}, f32[1,32,32,256]{3,2,1,0:T(8,128)}, f32[1,32,32,256]{3,2,1,0:T(8,128)}, f32[1,32,32,256]{3,2,1,0:T(8,128)}) custom-call(f32[32,128]{1,0:T(8,128)S(1)} %bitcast.4, f32[5,32,2,56,128]{4,3,2,1,0:T(8,128)S(1)} %get-tuple-element.52.fields_ref, f32[32,2,56,128]{3,2,1,0:T(8,128)S(1)} %get-tuple-element.46.face_x_ref, ...), custom_call_target="tpu_custom_call" | custom-call | tf_op jit(solution)/shard_map/finish/pallas_call | solution.py:793
Async XLA Ops:
  1.9 9.2 %collective-permute-start = (f32[2,32,8,128]{3,2,1,0:T(8,128)S(1)}, f32[2,32,8,128]{3,2,1,0:T(8,128)S(1)}, u32[]{:S(2)}, u32[]{:S(2)}) collective-permute-start(f32[2,32,8,128]{3,2,1,0:T(8,128)S(1)} %far.1), channel_id=1, source_target_pairs={{8,16},{16,8},{9,17},{17,9},{10,18},{18,10},{11,19},{19,11},{12,20... | collective-permute-start | bytes 786440 | tf_op jit(solution)/shard_map/ppermute | solution.py:704
  4.2 6.9 %collective-permute-start.1 = (f32[2,32,8,128]{3,2,1,0:T(8,128)S(1)}, f32[2,32,8,128]{3,2,1,0:T(8,128)S(1)}, u32[]{:S(2)}, u32[]{:S(2)}) collective-permute-start(f32[2,32,8,128]{3,2,1,0:T(8,128)S(1)} %get-tuple-element.29), channel_id=1, source_target_pairs={{0,8},{8,0},{16,24},{24,16},{1,9},{9,1},{17,25},{25,17},{2,10},{10... | collective-permute-start | bytes 786440 | tf_op jit(solution)/shard_map/ppermute | solution.py:704
  11.3 6.9 %collective-permute-start.2 = (f32[2,40,128]{2,1,0:T(8,128)S(1)}, f32[2,40,128]{2,1,0:T(8,128)S(1)}, u32[]{:S(2)}, u32[]{:S(2)}) collective-permute-start(f32[2,40,128]{2,1,0:T(8,128)S(1)} %get-tuple-element.36), channel_id=1, source_target_pairs={{1,2},{2,1},{3,4},{4,3},{5,6},{6,5},{9,10},{10,9},{11,12},{12,11},... | collective-permute-start | bytes 122888 | tf_op jit(solution)/shard_map/ppermute | solution.py:704
  12.0 6.3 %collective-permute-start.3 = (f32[2,40,128]{2,1,0:T(8,128)S(1)}, f32[2,40,128]{2,1,0:T(8,128)S(1)}, u32[]{:S(2)}, u32[]{:S(2)}) collective-permute-start(f32[2,40,128]{2,1,0:T(8,128)S(1)} %get-tuple-element.37), channel_id=1, source_target_pairs={{0,1},{1,0},{2,3},{3,2},{4,5},{5,4},{6,7},{7,6},{8,9},{9,8},{10,11... | collective-permute-start | bytes 122888 | tf_op jit(solution)/shard_map/ppermute | solution.py:704

commit v7 on v6

--- a/solution.py
+++ b/solution.py
@@ -355,7 +355,7 @@
             inverse_ref[layer, tile, at(blocks), :] = 0.5 * jnp.exp(-halo_ref[0, layer, tile])
         return 0
 
-    lax.fori_loop(0, layers, fill, 0, unroll=2 * slots)
+    lax.fori_loop(0, layers, fill, 0, unroll=layers)
 
     def faces(layer, _):
         values = [inverse_ref[layer, tile, at(blocks), :] for tile in range(tiles)]
@@ -371,7 +371,7 @@
             face_z_ref[layer, tile, at(blocks), :] = jnp.where(layer > 0, reciprocal(before + values[tile]), 0.0)
         return 0
 
-    lax.fori_loop(0, layers, faces, 0, unroll=2 * slots)
+    lax.fori_loop(0, layers, faces, 0, unroll=4 * slots)
     found = apply_power(1, fields_ref, face_x_ref, face_y_ref, face_z_ref, face_w_ref, None)
     for which, part in enumerate(found):
         parts_ref[which] = part

time: 38.7 us -> 38.7 us (level)
  transfers between devices with their start and end apart: 4 -> 4, of which waited for: 1 -> 1; matrix products, arithmetic and copies ran while one was open for 0% -> 0% of each run, Pallas kernels for 16% -> 15%
where the time goes in v7:
time: 38.7 us; the launch traced here: 38.5 us
  Pallas kernels  15.1 us (39%)
  blocking collectives  12.2 us (32%)
  starting transfers between devices  10.1 us (26%)
  between operations  0.7 us (2%)
  waiting for transfers between devices  0.43 us (1%)
    all_to_all x1, blocking collectives, on_device(): sums = lax.all_to_all(sums, ('gx', 'gy'), 0, 0, tiled=True)  12.2 us
    ppermute x4, starting transfers between devices, exchange(): return lax.ppermute(value, axis, pairs)  10.1 us
    pallas_call x1, Pallas kernels, on_device(): pl.pallas_call(basis_kernel, out_shape=(powers[0], in_vmem(DEPTH, *inner)...  5.04 us
    pallas_call x1, Pallas kernels, on_device(): pl.pallas_call(finish_kernel, out_shape=(jax.ShapeDtypeStruct((1, *block)...  2.92 us
    pallas_call x1, Pallas kernels, on_device(): pl.pallas_call(own_kernel, out_shape=powers + (in_vmem(*edges),) * 2, in_...  2.46 us
    pallas_call x1, Pallas kernels, on_device(): pl.pallas_call(load_kernel, out_shape=(in_vmem(*full), powers[0], in_vmem...  1.67 us
    pallas_call x1, Pallas kernels, on_device(): pl.pallas_call(first_kernel, out_shape=powers + (in_vmem(2, SUB, LANES),)...  1.54 us
    pallas_call x1, Pallas kernels, on_device(): pl.pallas_call(far_kernel, out_shape=in_vmem(*ends), in_specs=[HBM_SPEC]...  1.22 us
  transfers between devices with their start and end apart: 4, of which 1 were waited for; matrix products, arithmetic and copies ran while one was open for 0% of the time, Pallas kernels for 15%

profile of v7, /device:TPU:0, one launch (start us, length us, event | category | flops | bytes accessed | tf_op | source)
XLA Modules:
  0.0 38.5 jit_solution(15601235179032805049)
XLA Ops:
  0.6 1.2 %far.1 = f32[2,32,8,128]{3,2,1,0:T(8,128)S(1)} custom-call(f32[1,32,32,256]{3,2,1,0:T(8,128)} %log_hbm.3, f32[1,32,32,256]{3,2,1,0:T(8,128)} %src_hbm.3), custom_call_target="tpu_custom_call" | custom-call | tf_op jit(solution)/shard_map/far/pallas_call | solution.py:723
  1.9 0.7 %collective-permute-start = (f32[2,32,8,128]{3,2,1,0:T(8,128)S(1)}, f32[2,32,8,128]{3,2,1,0:T(8,128)S(1)}, u32[]{:S(2)}, u32[]{:S(2)}) collective-permute-start(f32[2,32,8,128]{3,2,1,0:T(8,128)S(1)} %far.1), channel_id=1, source_target_pairs={{8,16},{16,8},{9,17},{17,9},{10,18},{18,10},{11,19},{19,11},{12,20... | collective-permute-start | bytes 786440 | tf_op jit(solution)/shard_map/ppermute | solution.py:704
  2.5 1.7 %load.1 = (f32[32,2,56,128]{3,2,1,0:T(8,128)S(1)}, f32[5,32,2,56,128]{4,3,2,1,0:T(8,128)S(1)}, f32[2,32,8,128]{3,2,1,0:T(8,128)S(1)}) custom-call(f32[1,32,32,256]{3,2,1,0:T(8,128)} %log_hbm.3, f32[1,32,32,256]{3,2,1,0:T(8,128)} %src_hbm.3), custom_call_target="tpu_custom_call" | custom-call | flops 262144 | bytes 2097152 | tf_op jit(solution)/shard_map/load/pallas_call | solution.py:733
  4.2 4.4 %collective-permute-start.1 = (f32[2,32,8,128]{3,2,1,0:T(8,128)S(1)}, f32[2,32,8,128]{3,2,1,0:T(8,128)S(1)}, u32[]{:S(2)}, u32[]{:S(2)}) collective-permute-start(f32[2,32,8,128]{3,2,1,0:T(8,128)S(1)} %get-tuple-element.29), channel_id=1, source_target_pairs={{0,8},{8,0},{16,24},{24,16},{1,9},{9,1},{17,25},{25,17},{2,10},{10... | collective-permute-start | bytes 786440 | tf_op jit(solution)/shard_map/ppermute | solution.py:704
  8.6 2.5 %own.1 = (f32[5,32,2,56,128]{4,3,2,1,0:T(8,128)S(1)}, f32[35,2,56,128]{3,2,1,0:T(8,128)S(1)}, f32[32,2,56,128]{3,2,1,0:T(8,128)S(1)}, f32[32,2,56,128]{3,2,1,0:T...) custom-call(f32[32,2,56,128]{3,2,1,0:T(8,128)S(1)} %get-tuple-elemen, ...), custom_call_target="tpu_custom_call", output_to_operand_aliasing={{0}: (1, {})} | custom-call | flops 15728640 | bytes 2097152 | tf_op jit(solution)/shard_map/own/pallas_call | solution.py:744
  11.1 0.0 collective-permute-done.far_in
  11.1 0.0 collective-permute-done.1.near_in
  11.1 0.2 edges.1
  11.3 0.7 %collective-permute-start.2 = (f32[2,40,128]{2,1,0:T(8,128)S(1)}, f32[2,40,128]{2,1,0:T(8,128)S(1)}, u32[]{:S(2)}, u32[]{:S(2)}) collective-permute-start(f32[2,40,128]{2,1,0:T(8,128)S(1)} %get-tuple-element.36), channel_id=1, source_target_pairs={{1,2},{2,1},{3,4},{4,3},{5,6},{6,5},{9,10},{10,9},{11,12},{12,11},... | collective-permute-start | bytes 122888 | tf_op jit(solution)/shard_map/ppermute | solution.py:704
  12.0 4.3 %collective-permute-start.3 = (f32[2,40,128]{2,1,0:T(8,128)S(1)}, f32[2,40,128]{2,1,0:T(8,128)S(1)}, u32[]{:S(2)}, u32[]{:S(2)}) collective-permute-start(f32[2,40,128]{2,1,0:T(8,128)S(1)} %get-tuple-element.37), channel_id=1, source_target_pairs={{0,1},{1,0},{2,3},{3,2},{4,5},{5,4},{6,7},{7,6},{8,9},{9,8},{10,11... | collective-permute-start | bytes 122888 | tf_op jit(solution)/shard_map/ppermute | solution.py:704
  16.4 1.5 %first.1 = (f32[5,32,2,56,128]{4,3,2,1,0:T(8,128)S(1)}, f32[35,2,56,128]{3,2,1,0:T(8,128)S(1)}, f32[32,2,56,128]{3,2,1,0:T(8,128)S(1)}, f32[32,2,56,128]{3,2,1,0...) custom-call(f32[2,32,2,8,128]{4,3,2,1,0:T(8,128)S(1)} %get-tuple-ele, ...), custom_call_target="tpu_custom_call", output_to_operand_aliasing={{0}: (1, {}), {1}: (2, {}), {2}: (3, {}), {3}: (4, {}), {4}... | custom-call | flops 10485760 | bytes 2097152 | tf_op jit(solution)/shard_map/first/pallas_call | solution.py:765
  17.9 0.0 collective-permute-done.2.far_ref
  17.9 0.4 %collective-permute-done.3.near_ref = f32[2,40,128]{2,1,0:T(8,128)S(1)} collective-permute-done((f32[2,40,128]{2,1,0:T(8,128)S(1)}, f32[2,40,128]{2,1,0:T(8,128)S(1)}, u32[]{:S(2)}, u32[]{:S(2)}) %collective-permute-start.3) | collective-permute-done | bytes 40992 | tf_op jit(solution)/shard_map/ppermute | solution.py:704
  18.3 5.0 %basis.1 = (f32[5,32,2,56,128]{4,3,2,1,0:T(8,128)S(1)}, f32[4,4,56,128]{3,2,1,0:T(8,128)S(1)}, f32[32,128]{1,0:T(8,128)S(1)}) custom-call(f32[2,40,128]{2,1,0:T(8,128)S(1)} %get-tuple-element.34.last_ref, f32[2,40,128]{2,1,0:T(8,128)S(1)} %get-tuple-element.35.first_ref, ...), custom_call_target="tpu_custom_call", output_to_operand_aliasing={{0}: (9, {})} | custom-call | tf_op jit(solution)/shard_map/basis/pallas_call | solution.py:775
  23.4 12.2 %all_to_all.11 = f32[32,1,128]{2,1,0:T(1,128)S(1)} all-to-all(f32[32,1,128]{2,1,0:T(1,128)S(1)} %bitcast.5), channel_id=1, replica_groups=mesh['gx'=4,'gy'=8] {'gx','gy'}, dimensions={0} | all-to-all | bytes 32768 | tf_op jit(solution)/shard_map/all_to_all | solution.py:791
  35.6 2.9 %finish.1 = (f32[1,32,32,256]{3,2,1,0:T(8,128)}, f32[1,32,32,256]{3,2,1,0:T(8,128)}, f32[1,32,32,256]{3,2,1,0:T(8,128)}, f32[1,32,32,256]{3,2,1,0:T(8,128)}) custom-call(f32[32,128]{1,0:T(8,128)S(1)} %bitcast.4, f32[5,32,2,56,128]{4,3,2,1,0:T(8,128)S(1)} %get-tuple-element.52.fields_ref, f32[32,2,56,128]{3,2,1,0:T(8,128)S(1)} %get-tuple-element.46.face_x_ref, ...), custom_call_target="tpu_custom_call" | custom-call | tf_op jit(solution)/shard_map/finish/pallas_call | solution.py:793
Async XLA Ops:
  1.9 9.2 %collective-permute-start = (f32[2,32,8,128]{3,2,1,0:T(8,128)S(1)}, f32[2,32,8,128]{3,2,1,0:T(8,128)S(1)}, u32[]{:S(2)}, u32[]{:S(2)}) collective-permute-start(f32[2,32,8,128]{3,2,1,0:T(8,128)S(1)} %far.1), channel_id=1, source_target_pairs={{8,16},{16,8},{9,17},{17,9},{10,18},{18,10},{11,19},{19,11},{12,20... | collective-permute-start | bytes 786440 | tf_op jit(solution)/shard_map/ppermute | solution.py:704
  4.2 6.9 %collective-permute-start.1 = (f32[2,32,8,128]{3,2,1,0:T(8,128)S(1)}, f32[2,32,8,128]{3,2,1,0:T(8,128)S(1)}, u32[]{:S(2)}, u32[]{:S(2)}) collective-permute-start(f32[2,32,8,128]{3,2,1,0:T(8,128)S(1)} %get-tuple-element.29), channel_id=1, source_target_pairs={{0,8},{8,0},{16,24},{24,16},{1,9},{9,1},{17,25},{25,17},{2,10},{10... | collective-permute-start | bytes 786440 | tf_op jit(solution)/shard_map/ppermute | solution.py:704
  11.3 6.6 %collective-permute-start.2 = (f32[2,40,128]{2,1,0:T(8,128)S(1)}, f32[2,40,128]{2,1,0:T(8,128)S(1)}, u32[]{:S(2)}, u32[]{:S(2)}) collective-permute-start(f32[2,40,128]{2,1,0:T(8,128)S(1)} %get-tuple-element.36), channel_id=1, source_target_pairs={{1,2},{2,1},{3,4},{4,3},{5,6},{6,5},{9,10},{10,9},{11,12},{12,11},... | collective-permute-start | bytes 122888 | tf_op jit(solution)/shard_map/ppermute | solution.py:704
  12.0 6.3 %collective-permute-start.3 = (f32[2,40,128]{2,1,0:T(8,128)S(1)}, f32[2,40,128]{2,1,0:T(8,128)S(1)}, u32[]{:S(2)}, u32[]{:S(2)}) collective-permute-start(f32[2,40,128]{2,1,0:T(8,128)S(1)} %get-tuple-element.37), channel_id=1, source_target_pairs={{0,1},{1,0},{2,3},{3,2},{4,5},{5,4},{6,7},{7,6},{8,9},{9,8},{10,11... | collective-permute-start | bytes 122888 | tf_op jit(solution)/shard_map/ppermute | solution.py:704

commit v8 on v7

--- a/solution.py
+++ b/solution.py
@@ -151,7 +151,7 @@
                     inverse_ref[layer, tile, pl.ds(ring, 1), :] = value[0:1]
         return 0
 
-    lax.fori_loop(0, layers, fill, 0, unroll=slots)
+    lax.fori_loop(0, layers, fill, 0, unroll=2 * slots)
 
     zero = jnp.zeros((SUB, LANES), F32)
     for tile in range(tiles):
@@ -169,7 +169,7 @@
                 )
         return 0
 
-    lax.fori_loop(0, layers, faces, 0, unroll=slots)
+    lax.fori_loop(0, layers, faces, 0, unroll=2 * slots)
 
     def faces_z(layer, _):
         for tile in range(tiles):
@@ -179,7 +179,7 @@
                 )
         return 0
 
-    lax.fori_loop(1, layers, faces_z, 0, unroll=slots)
+    lax.fori_loop(1, layers, faces_z, 0, unroll=2 * slots)
 
     base_ref[:, :, pl.ds(ring, 1), :] = base_ref[:, :, pl.ds(LO, 1), :]
     for index, ref in enumerate((log_ref, base_ref)):

time: 38.7 us -> 38.7 us (level)
  Pallas kernels: 15.1 us -> 14.7 us
  blocking collectives: 12.2 us -> 12.6 us
    all_to_all x1, blocking collectives: 12.2 us -> 12.6 us  [on_device(): sums = lax.all_to_all(sums, ('gx', 'gy'), 0, 0, tiled=True)]
    pallas_call x1, Pallas kernels: 2.46 us -> 2.06 us  [on_device(): pl.pallas_call(own_kernel, out_shape=powers + (in_vmem(*edges),) * 2, in_...]
  transfers between devices with their start and end apart: 4 -> 4, of which waited for: 1 -> 1; matrix products, arithmetic and copies ran while one was open for 0% -> 0% of each run, Pallas kernels for 15% -> 14%
where the time goes in v8:
time: 38.7 us; the launch traced here: 38.5 us
  Pallas kernels  14.7 us (38%)
  blocking collectives  12.6 us (33%)
  starting transfers between devices  10.1 us (26%)
  between operations  0.7 us (2%)
  waiting for transfers between devices  0.43 us (1%)
    all_to_all x1, blocking collectives, on_device(): sums = lax.all_to_all(sums, ('gx', 'gy'), 0, 0, tiled=True)  12.6 us
    ppermute x4, starting transfers between devices, exchange(): return lax.ppermute(value, axis, pairs)  10.1 us
    pallas_call x1, Pallas kernels, on_device(): pl.pallas_call(basis_kernel, out_shape=(powers[0], in_vmem(DEPTH, *inner)...  5.04 us
    pallas_call x1, Pallas kernels, on_device(): pl.pallas_call(finish_kernel, out_shape=(jax.ShapeDtypeStruct((1, *block)...  2.92 us
    pallas_call x1, Pallas kernels, on_device(): pl.pallas_call(own_kernel, out_shape=powers + (in_vmem(*edges),) * 2, in_...  2.06 us
    pallas_call x1, Pallas kernels, on_device(): pl.pallas_call(load_kernel, out_shape=(in_vmem(*full), powers[0], in_vmem...  1.67 us
    pallas_call x1, Pallas kernels, on_device(): pl.pallas_call(first_kernel, out_shape=powers + (in_vmem(2, SUB, LANES),)...  1.54 us
    pallas_call x1, Pallas kernels, on_device(): pl.pallas_call(far_kernel, out_shape=in_vmem(*ends), in_specs=[HBM_SPEC]...  1.22 us
  transfers between devices with their start and end apart: 4, of which 1 were waited for; matrix products, arithmetic and copies ran while one was open for 0% of the time, Pallas kernels for 14%

profile of v8, /device:TPU:0, one launch (start us, length us, event | category | flops | bytes accessed | tf_op | source)
XLA Modules:
  0.0 38.5 jit_solution(4614831730779589005)
XLA Ops:
  0.6 1.2 %far.1 = f32[2,32,8,128]{3,2,1,0:T(8,128)S(1)} custom-call(f32[1,32,32,256]{3,2,1,0:T(8,128)} %log_hbm.3, f32[1,32,32,256]{3,2,1,0:T(8,128)} %src_hbm.3), custom_call_target="tpu_custom_call" | custom-call | tf_op jit(solution)/shard_map/far/pallas_call | solution.py:723
  1.9 0.7 %collective-permute-start = (f32[2,32,8,128]{3,2,1,0:T(8,128)S(1)}, f32[2,32,8,128]{3,2,1,0:T(8,128)S(1)}, u32[]{:S(2)}, u32[]{:S(2)}) collective-permute-start(f32[2,32,8,128]{3,2,1,0:T(8,128)S(1)} %far.1), channel_id=1, source_target_pairs={{8,16},{16,8},{9,17},{17,9},{10,18},{18,10},{11,19},{19,11},{12,20... | collective-permute-start | bytes 786440 | tf_op jit(solution)/shard_map/ppermute | solution.py:704
  2.5 1.7 %load.1 = (f32[32,2,56,128]{3,2,1,0:T(8,128)S(1)}, f32[5,32,2,56,128]{4,3,2,1,0:T(8,128)S(1)}, f32[2,32,8,128]{3,2,1,0:T(8,128)S(1)}) custom-call(f32[1,32,32,256]{3,2,1,0:T(8,128)} %log_hbm.3, f32[1,32,32,256]{3,2,1,0:T(8,128)} %src_hbm.3), custom_call_target="tpu_custom_call" | custom-call | flops 262144 | bytes 2097152 | tf_op jit(solution)/shard_map/load/pallas_call | solution.py:733
  4.2 4.4 %collective-permute-start.1 = (f32[2,32,8,128]{3,2,1,0:T(8,128)S(1)}, f32[2,32,8,128]{3,2,1,0:T(8,128)S(1)}, u32[]{:S(2)}, u32[]{:S(2)}) collective-permute-start(f32[2,32,8,128]{3,2,1,0:T(8,128)S(1)} %get-tuple-element.29), channel_id=1, source_target_pairs={{0,8},{8,0},{16,24},{24,16},{1,9},{9,1},{17,25},{25,17},{2,10},{10... | collective-permute-start | bytes 786440 | tf_op jit(solution)/shard_map/ppermute | solution.py:704
  8.6 2.1 %own.1 = (f32[5,32,2,56,128]{4,3,2,1,0:T(8,128)S(1)}, f32[35,2,56,128]{3,2,1,0:T(8,128)S(1)}, f32[32,2,56,128]{3,2,1,0:T(8,128)S(1)}, f32[32,2,56,128]{3,2,1,0:T...) custom-call(f32[32,2,56,128]{3,2,1,0:T(8,128)S(1)} %get-tuple-elemen, ...), custom_call_target="tpu_custom_call", output_to_operand_aliasing={{0}: (1, {})} | custom-call | flops 15728640 | bytes 2097152 | tf_op jit(solution)/shard_map/own/pallas_call | solution.py:744
  10.7 0.0 collective-permute-done.far_in
  10.7 0.0 collective-permute-done.1.near_in
  10.7 0.2 edges.1
  10.9 0.7 %collective-permute-start.2 = (f32[2,40,128]{2,1,0:T(8,128)S(1)}, f32[2,40,128]{2,1,0:T(8,128)S(1)}, u32[]{:S(2)}, u32[]{:S(2)}) collective-permute-start(f32[2,40,128]{2,1,0:T(8,128)S(1)} %get-tuple-element.36), channel_id=1, source_target_pairs={{1,2},{2,1},{3,4},{4,3},{5,6},{6,5},{9,10},{10,9},{11,12},{12,11},... | collective-permute-start | bytes 122888 | tf_op jit(solution)/shard_map/ppermute | solution.py:704
  11.6 4.3 %collective-permute-start.3 = (f32[2,40,128]{2,1,0:T(8,128)S(1)}, f32[2,40,128]{2,1,0:T(8,128)S(1)}, u32[]{:S(2)}, u32[]{:S(2)}) collective-permute-start(f32[2,40,128]{2,1,0:T(8,128)S(1)} %get-tuple-element.37), channel_id=1, source_target_pairs={{0,1},{1,0},{2,3},{3,2},{4,5},{5,4},{6,7},{7,6},{8,9},{9,8},{10,11... | collective-permute-start | bytes 122888 | tf_op jit(solution)/shard_map/ppermute | solution.py:704
  16.0 1.5 %first.1 = (f32[5,32,2,56,128]{4,3,2,1,0:T(8,128)S(1)}, f32[35,2,56,128]{3,2,1,0:T(8,128)S(1)}, f32[32,2,56,128]{3,2,1,0:T(8,128)S(1)}, f32[32,2,56,128]{3,2,1,0...) custom-call(f32[2,32,2,8,128]{4,3,2,1,0:T(8,128)S(1)} %get-tuple-ele, ...), custom_call_target="tpu_custom_call", output_to_operand_aliasing={{0}: (1, {}), {1}: (2, {}), {2}: (3, {}), {3}: (4, {}), {4}... | custom-call | flops 10485760 | bytes 2097152 | tf_op jit(solution)/shard_map/first/pallas_call | solution.py:765
  17.5 0.0 collective-permute-done.2.far_ref
  17.5 0.4 %collective-permute-done.3.near_ref = f32[2,40,128]{2,1,0:T(8,128)S(1)} collective-permute-done((f32[2,40,128]{2,1,0:T(8,128)S(1)}, f32[2,40,128]{2,1,0:T(8,128)S(1)}, u32[]{:S(2)}, u32[]{:S(2)}) %collective-permute-start.3) | collective-permute-done | bytes 40992 | tf_op jit(solution)/shard_map/ppermute | solution.py:704
  17.9 5.0 %basis.1 = (f32[5,32,2,56,128]{4,3,2,1,0:T(8,128)S(1)}, f32[4,4,56,128]{3,2,1,0:T(8,128)S(1)}, f32[32,128]{1,0:T(8,128)S(1)}) custom-call(f32[2,40,128]{2,1,0:T(8,128)S(1)} %get-tuple-element.34.last_ref, f32[2,40,128]{2,1,0:T(8,128)S(1)} %get-tuple-element.35.first_ref, ...), custom_call_target="tpu_custom_call", output_to_operand_aliasing={{0}: (9, {})} | custom-call | tf_op jit(solution)/shard_map/basis/pallas_call | solution.py:775
  23.0 12.6 %all_to_all.11 = f32[32,1,128]{2,1,0:T(1,128)S(1)} all-to-all(f32[32,1,128]{2,1,0:T(1,128)S(1)} %bitcast.5), channel_id=1, replica_groups=mesh['gx'=4,'gy'=8] {'gx','gy'}, dimensions={0} | all-to-all | bytes 32768 | tf_op jit(solution)/shard_map/all_to_all | solution.py:791
  35.6 2.9 %finish.1 = (f32[1,32,32,256]{3,2,1,0:T(8,128)}, f32[1,32,32,256]{3,2,1,0:T(8,128)}, f32[1,32,32,256]{3,2,1,0:T(8,128)}, f32[1,32,32,256]{3,2,1,0:T(8,128)}) custom-call(f32[32,128]{1,0:T(8,128)S(1)} %bitcast.4, f32[5,32,2,56,128]{4,3,2,1,0:T(8,128)S(1)} %get-tuple-element.52.fields_ref, f32[32,2,56,128]{3,2,1,0:T(8,128)S(1)} %get-tuple-element.46.face_x_ref, ...), custom_call_target="tpu_custom_call" | custom-call | tf_op jit(solution)/shard_map/finish/pallas_call | solution.py:793
Async XLA Ops:
  1.9 8.8 %collective-permute-start = (f32[2,32,8,128]{3,2,1,0:T(8,128)S(1)}, f32[2,32,8,128]{3,2,1,0:T(8,128)S(1)}, u32[]{:S(2)}, u32[]{:S(2)}) collective-permute-start(f32[2,32,8,128]{3,2,1,0:T(8,128)S(1)} %far.1), channel_id=1, source_target_pairs={{8,16},{16,8},{9,17},{17,9},{10,18},{18,10},{11,19},{19,11},{12,20... | collective-permute-start | bytes 786440 | tf_op jit(solution)/shard_map/ppermute | solution.py:704
  4.2 6.5 %collective-permute-start.1 = (f32[2,32,8,128]{3,2,1,0:T(8,128)S(1)}, f32[2,32,8,128]{3,2,1,0:T(8,128)S(1)}, u32[]{:S(2)}, u32[]{:S(2)}) collective-permute-start(f32[2,32,8,128]{3,2,1,0:T(8,128)S(1)} %get-tuple-element.29), channel_id=1, source_target_pairs={{0,8},{8,0},{16,24},{24,16},{1,9},{9,1},{17,25},{25,17},{2,10},{10... | collective-permute-start | bytes 786440 | tf_op jit(solution)/shard_map/ppermute | solution.py:704
  10.9 6.6 %collective-permute-start.2 = (f32[2,40,128]{2,1,0:T(8,128)S(1)}, f32[2,40,128]{2,1,0:T(8,128)S(1)}, u32[]{:S(2)}, u32[]{:S(2)}) collective-permute-start(f32[2,40,128]{2,1,0:T(8,128)S(1)} %get-tuple-element.36), channel_id=1, source_target_pairs={{1,2},{2,1},{3,4},{4,3},{5,6},{6,5},{9,10},{10,9},{11,12},{12,11},... | collective-permute-start | bytes 122888 | tf_op jit(solution)/shard_map/ppermute | solution.py:704
  11.6 6.3 %collective-permute-start.3 = (f32[2,40,128]{2,1,0:T(8,128)S(1)}, f32[2,40,128]{2,1,0:T(8,128)S(1)}, u32[]{:S(2)}, u32[]{:S(2)}) collective-permute-start(f32[2,40,128]{2,1,0:T(8,128)S(1)} %get-tuple-element.37), channel_id=1, source_target_pairs={{0,1},{1,0},{2,3},{3,2},{4,5},{5,4},{6,7},{7,6},{8,9},{9,8},{10,11... | collective-permute-start | bytes 122888 | tf_op jit(solution)/shard_map/ppermute | solution.py:704
